TPU v7x, 512 devices: a whole 4x8x8 slice. The times are simulated.
512 devices in a mesh: ia: 8 (over x, z_hi), ja: 8 (over y), ka: 8 (over z_lo, core).
Axes of the slice: x: 4, y: 8, z: 8 (z_hi: 2, z_lo: 4; z = z_hi * 4 + z_lo), core: 2. Of those that a mesh axis runs over, the one named last changes fastest.
Arguments:
- pair_rep: float32 [1024, 1024, 128], P('ia', ('ja', 'ka')), may hold values from -6 to 6
- pair_proj: bfloat16 [128, 512], replicated, may hold values from -0.5 to 0.5
- gate_proj: bfloat16 [128, 128], replicated, may hold values from -0.5 to 0.5
- out_proj: bfloat16 [128, 128], replicated, may hold values from -0.5 to 0.5
- trans_in: bfloat16 [128, 1024], replicated, may hold values from -0.5 to 0.5
- trans_out: bfloat16 [512, 128], replicated, may hold values from -0.25 to 0.25
Outputs:
- pair_out: float32 [1024, 1024, 128], P('ia', ('ja', 'ka'))
All inputs are finite; a program needn't handle non-finite values.
Results may differ from a plain program's by a relative error of at most 0.013.
Values may be sent and summed in bfloat16 or wider, within the bound.
No kernel may reach another device: no remote copies, remote signals or barrier semaphores. Data moves between devices by JAX's collectives and lax.ppermute only.
A program may use at most 64 MiB of HBM per device.

v0:
```python
import jax
import jax.numpy as jnp
from jax import lax
from jax.sharding import PartitionSpec as P


def layer_norm(values):
    centre = jnp.mean(values, axis=-1, keepdims=True)
    centred = values - centre
    spread = jnp.mean(centred * centred, axis=-1, keepdims=True)
    return centred * lax.rsqrt(spread + 1e-05)


def per_device(pair_rep, pair_proj, gate_proj, out_proj, trans_in, trans_out):
    hidden_width = out_proj.shape[0]
    trans_width = trans_out.shape[0]
    normed = layer_norm(pair_rep).astype(jnp.bfloat16)
    projected = jnp.dot(normed, pair_proj, preferred_element_type=jnp.float32)
    left_loc = (
        jax.nn.sigmoid(projected[..., :hidden_width])
        * projected[..., hidden_width : 2 * hidden_width]
    ).astype(jnp.bfloat16)
    right_loc = (
        jax.nn.sigmoid(projected[..., 2 * hidden_width : 3 * hidden_width])
        * projected[..., 3 * hidden_width :]
    ).astype(jnp.bfloat16)
    left_panel = lax.all_gather(left_loc, "ja", axis=1, tiled=True)
    right_full = lax.all_gather(right_loc, "ia", axis=0, tiled=True)
    right_panel = lax.all_to_all(right_full, "ja", split_axis=0, concat_axis=1, tiled=True)
    gating = jax.nn.sigmoid(jnp.dot(normed, gate_proj, preferred_element_type=jnp.float32))
    summed = lax.psum_scatter(
        jnp.einsum(
            "jkc,ikc->jic", right_panel, left_panel, preferred_element_type=jnp.float32
        ).astype(jnp.bfloat16),
        "ka",
        scatter_dimension=0,
        tiled=True,
    ).astype(jnp.float32)
    triangle = jnp.transpose(summed, (1, 0, 2))
    tri_normed = layer_norm(triangle).astype(jnp.bfloat16)
    middle = pair_rep + gating * jnp.dot(tri_normed, out_proj, preferred_element_type=jnp.float32)
    mid_normed = layer_norm(middle).astype(jnp.bfloat16)
    expanded = jnp.dot(mid_normed, trans_in, preferred_element_type=jnp.float32)
    hidden_units = (jax.nn.silu(expanded[..., :trans_width]) * expanded[..., trans_width:]).astype(
        jnp.bfloat16
    )
    return middle + jnp.dot(hidden_units, trans_out, preferred_element_type=jnp.float32)


def solution(mesh):
    in_specs = (P("ia", ("ja", "ka"), None), P(), P(), P(), P(), P())
    out_specs = P("ia", ("ja", "ka"), None)
    return jax.shard_map(
        per_device, mesh=mesh, in_specs=in_specs, out_specs=out_specs, check_vma=False
    )
```

profile of v0, /device:TPU:1, one launch (start us, length us, event | category | flops | bytes accessed | tf_op | source)
XLA Modules:
  0.0 385.0 jit_solution(5032018009293330600)
XLA Ops:
  6.5 0.0 copy-start
  6.5 0.0 copy-start.2
  6.5 0.0 all-gather.5.cloned.1.call-start
  6.5 1.6 reduce_sum.54
  8.2 0.1 copy.118
  8.2 0.1 copy.119
  8.4 1.9 multiply_reduce_fusion.1
  10.2 0.1 copy.120
  10.3 0.1 copy.121
  10.4 1.8 multiply_convert_fusion.1
  12.2 0.0 copy-done.2
  12.3 0.8 fusion.30
  13.0 1.4 fusion.11
  14.4 0.0 all-gather.5.cloned.1.call-update
  14.4 0.0 all-gather.3.cloned.1.call-start
  14.4 1.0 copy.127
  15.5 0.0 all-gather.3.cloned.1.call-update
  15.5 121.4 %all-gather.5.cloned.1.call-done = bf16[1024,16,128]{0,2,1:T(8,128)(2,1)} async-done(((bf16[128,16,128]{0,2,1:T(8,128)(2,1)}), bf16[1024,16,128]{0,2,1:T(8,128)(2,1)}) %all-gather.5.cloned.1.call-update) | async-done | bytes 4194320 | tf_op jit(solution)/shard_map/all_gather | solution.py:28
  136.8 6.9 %copy.130 = bf16[1024,16,128]{2,1,0:T(8,128)(2,1)} copy(bf16[1024,16,128]{0,2,1:T(8,128)(2,1)} %all-gather.5.cloned.1.call-done) | data formatting | bytes 8388608 | tf_op jit(solution)/shard_map/all_gather | solution.py:28
  143.8 6.5 %all-to-all-start = ((bf16[1024,16,128]{2,1,0:T(8,128)(2,1)}), bf16[1024,16,128]{2,1,0:T(8,128)(2,1)}, u32[]{:S(2)}, u32[]{:S(2)}) async-start(bf16[1024,16,128]{2,1,0:T(8,128)(2,1)} %copy.130), calls=%async_computation | async-start | bytes 8388608 | tf_op jit(solution)/shard_map/all_to_all | solution.py:29
  150.2 0.2 reduce-scatter.2.cloned.1.call-start
  150.5 124.4 %all-gather.3.cloned.1.call-done = bf16[128,128,128]{2,0,1:T(8,128)(2,1)} async-done(((bf16[128,16,128]{2,0,1:T(8,128)(2,1)}), bf16[128,128,128]{2,0,1:T(8,128)(2,1)}) %all-gather.3.cloned.1.call-update) | async-done | bytes 4194320 | tf_op jit(solution)/shard_map/all_gather | solution.py:27
  274.8 6.6 %copy.132 = bf16[128,128,128]{0,1,2:T(8,128)(2,1)} copy(bf16[128,128,128]{2,0,1:T(8,128)(2,1)} %all-gather.3.cloned.1.call-done) | data formatting | bytes 8388608 | tf_op jit(solution)/shard_map/all_gather | solution.py:27
  281.5 0.0 all-to-all-done
  281.5 5.4 %copy.131 = bf16[128,8,16,128]{3,2,1,0:T(8,128)(2,1)} copy(bf16[128,8,16,128]{3,2,0,1:T(8,128)(2,1)} %bitcast.3) | data formatting | bytes 8388608 | tf_op jit(solution)/shard_map/all_to_all | solution.py:29
  286.9 6.7 %copy.133 = bf16[128,128,128]{1,0,2:T(8,128)(2,1)} copy(bf16[128,128,128]{2,1,0:T(8,128)(2,1)} %bitcast.37) | data formatting | bytes 8388608 | tf_op jit(solution)/shard_map/all_to_all | solution.py:29
  293.6 8.5 %convert_bitcast_fusion = bf16[128,128,128]{0,1,2:T(8,128)(2,1)} fusion(bf16[128,128,128]{0,1,2:T(8,128)(2,1)} %copy.132, bf16[128,128,128]{1,0,2:T(8,128)(2,1)} %copy.133), kind=kOutput, calls=%fused_computation.2 | convolution fusion | flops 538968064 | bytes 12582912 | tf_op jit(solution)/shard_map/jkc,ikc->jic/dot_general | solution.py:32
  302.1 7.3 %copy.134 = bf16[128,128,128]{2,1,0:T(8,128)(2,1)} copy(bf16[128,128,128]{0,1,2:T(8,128)(2,1)} %convert_bitcast_fusion) | data formatting | bytes 8388608 | tf_op jit(solution)/shard_map/convert_element_type | solution.py:34
  309.4 0.0 copy-start.1
  309.4 0.0 copy-start.3
  309.4 0.0 copy-start.5
  309.4 0.0 reduce-scatter.2.cloned.1.call-update
  309.4 1.2 copy-done.1
  310.6 0.4 copy.140
  311.0 57.6 %reduce-scatter.2.cloned.1.call-done = bf16[16,128,128]{2,1,0:T(8,128)(2,1)} async-done(((bf16[128,128,128]{2,1,0:T(8,128)(2,1)}), bf16[16,128,128]{2,1,0:T(8,128)(2,1)}) %reduce-scatter.2.cloned.1.call-update) | async-done | bytes 524304 | tf_op jit(solution)/shard_map/reduce_scatter | solution.py:31
  368.6 1.2 bitcast_reduce_fusion
  369.9 1.7 fusion.21
  371.6 0.0 copy-done.3
  371.6 1.9 fusion.24
  373.5 0.0 copy-done.5
  373.5 0.5 fusion.39
  374.0 0.1 multiply_reduce_fusion
  374.2 0.0 copy-done
  374.2 0.0 copy-start.4
  374.2 1.3 fusion.23
  375.5 0.0 copy-done.4
  375.5 1.6 fusion.8
  377.1 1.4 copy.143
  (6 shorter events, 0.0 us)
Async XLA Ops:
  6.5 367.6 %copy-start = (bf16[128,1024]{1,0:T(8,128)(2,1)S(1)}, bf16[128,1024]{1,0:T(8,128)(2,1)}, u32[]{:S(2)}) copy-start(bf16[128,1024]{1,0:T(8,128)(2,1)} %param.10) | copy-start | bytes 786436
  6.5 5.7 %copy-start.2 = (bf16[128,512]{1,0:T(8,128)(2,1)S(1)}, bf16[128,512]{1,0:T(8,128)(2,1)}, u32[]{:S(2)}) copy-start(bf16[128,512]{1,0:T(8,128)(2,1)} %param.7) | copy-start | bytes 393220
  6.5 130.3 %all-gather.5.cloned.1.call-start = ((), (), s32[]{:S(2)}) async-start(), calls=%async_computation.3 | async-start | bytes 4718592 | tf_op jit(solution)/shard_map/all_gather | solution.py:28
  14.4 260.4 %all-gather.3.cloned.1.call-start = ((), (), s32[]{:S(2)}) async-start(), calls=%async_computation.2 | async-start | bytes 4718592 | tf_op jit(solution)/shard_map/all_gather | solution.py:27
  143.8 137.7 %all-to-all-start = ((bf16[1024,16,128]{2,1,0:T(8,128)(2,1)}), bf16[1024,16,128]{2,1,0:T(8,128)(2,1)}, u32[]{:S(2)}, u32[]{:S(2)}) async-start(bf16[1024,16,128]{2,1,0:T(8,128)(2,1)} %copy.130), calls=%async_computation | async-start | bytes 8388608 | tf_op jit(solution)/shard_map/all_to_all | solution.py:29
  150.2 218.4 %reduce-scatter.2.cloned.1.call-start = ((), (), s32[]{:S(2)}) async-start(), calls=%async_computation.4 | async-start | bytes 4718592 | tf_op jit(solution)/shard_map/reduce_scatter | solution.py:31
  309.4 1.2 copy-start.1
  309.4 62.2 %copy-start.3 = (bf16[128,128]{1,0:T(8,128)(2,1)S(1)}, bf16[128,128]{1,0:T(8,128)(2,1)}, u32[]{:S(2)}) copy-start(bf16[128,128]{1,0:T(8,128)(2,1)} %param.9) | copy-start | bytes 98308
  309.4 64.1 %copy-start.5 = (bf16[128,128]{1,0:T(8,128)(2,1)S(1)}, bf16[128,128]{1,0:T(8,128)(2,1)}, u32[]{:S(2)}) copy-start(bf16[128,128]{1,0:T(8,128)(2,1)} %param.8) | copy-start | bytes 98308
  374.2 1.3 copy-start.4
Sparse Core Ops, SparseCore 0:
  14.5 122.2 all-gather.4
  138.9 135.8 all-gather.2
  309.5 59.0 reduce-scatter.1
where the time goes:
time: 388 us; the launch traced here: 385 us
  waiting for transfers between devices  303 us (78%)
  local copies, waits for them, and re-layouts  37.3 us (10%)
  matrix products  14.5 us (4%)
  between operations  13.3 us (3%)
  other arithmetic  9.77 us (3%)
  starting transfers between devices  6.72 us (2%)
    all_gather x1, waiting for transfers between devices, per_device(): left_panel = lax.all_gather(left_loc, 'ja', axis=1, tiled=True)  124 us
    all_gather x1, waiting for transfers between devices, per_device(): right_full = lax.all_gather(right_loc, 'ia', axis=0, tiled=True)  121 us
    reduce_scatter x1, waiting for transfers between devices, per_device(): lax.psum_scatter(jnp.einsum('jkc,ikc->jic', right_panel, left_panel, pref...  57.6 us
    all_to_all x2, local copies, waits for them, and re-layouts, per_device(): lax.all_to_all(right_full, 'ja', split_axis=0, concat_axis=1, tiled=True)  12.1 us
    dot_general x1, matrix products, per_device(): jnp.einsum('jkc,ikc->jic', right_panel, left_panel, preferred_element_typ...  8.51 us
  transfers between devices with their start and end apart: 4, of which 3 were waited for; matrix products, arithmetic and copies ran while one was open for 4% of the time, Pallas kernels for 0%

commit v1 on v0

v1 whole, which is shorter than its diff:
```python
import functools

import jax
import jax.numpy as jnp
from jax import lax
from jax.experimental import pallas as pl
from jax.experimental.pallas import tpu as pltpu
from jax.sharding import Mesh
from jax.sharding import PartitionSpec as P

AXES = ("xh", "xb", "zh", "y", "zl", "core")
SIZES = (2, 2, 2, 8, 4, 2)
PLANE = ("xh", "zh", "y", "zl")
QUAD = ("xb", "core")
ROWS = 128
COLS = 16
CH = 128
EPS = 1e-05
LIMIT = 56 * 1024 * 1024


def sigmoid(v):
    return 0.5 * jnp.tanh(0.5 * v) + 0.5


def norm_lanes(v):
    centred = v - jnp.mean(v, axis=1, keepdims=True)
    spread = jnp.mean(centred * centred, axis=1, keepdims=True)
    return (centred * lax.rsqrt(spread + EPS)).astype(jnp.bfloat16)


def contract(a, b, dim_a, dim_b):
    return lax.dot_general(a, b, (((dim_a,), (dim_b,)), ((), ())), preferred_element_type=jnp.float32)


def project_kernel(x_ref, w_ref, out_ref, stage):
    for pair in range(COLS // 2):
        rows = [x_ref[pl.ds(2 * pair + s, ROWS, stride=COLS), :] for s in range(2)]
        normed = norm_lanes(jnp.concatenate(rows, axis=0))
        swapped = normed.reshape(2, 4, 2, 16, CH).transpose(0, 2, 1, 3, 4).reshape(2 * ROWS, CH)
        for base, half, values in ((16, 0, normed), (0, 2 * CH, swapped)):
            p = contract(w_ref[half : half + 2 * CH, :], values, 1, 1)
            product = sigmoid(p[:CH]) * p[CH:]
            for s in range(2):
                stage[pl.ds(base + 2 * pair + s, CH, stride=2 * COLS), :] = product[:, s * ROWS : (s + 1) * ROWS]
    out_ref[...] = stage[...].astype(jnp.bfloat16).reshape(CH, 2 * COLS, ROWS)


def split_kernel(a_ref, own_ref, other_ref, core_ref):
    core = lax.axis_index("core")
    right = a_ref[:, :COLS, :].astype(jnp.float32).reshape(2, 2, 32 * COLS, ROWS)
    low, high = right[:, 0], right[:, 1]
    first = jnp.concatenate([low[..., :64], high[..., :64]], axis=-1)
    second = jnp.concatenate([low[..., 64:], high[..., 64:]], axis=-1)
    own = jnp.where(core == 0, first, second).astype(jnp.bfloat16).reshape(64, COLS, ROWS)
    other = jnp.where(core == 0, second, first).astype(jnp.bfloat16).reshape(64, COLS, ROWS)
    own_ref[...] = own
    other_ref[...] = other
    core_ref[:CH] = a_ref[:, COLS:, :]
    core_ref[CH:] = other


def triangle_kernel(a_ref, own_ref, core_ref, x_ref, xc_ref, out_ref):
    xb = lax.axis_index("xb")
    lefts = []
    for ref, base in ((a_ref, COLS), (core_ref, 0)):
        lefts.append(
            jnp.concatenate(
                [ref[32 * g : 32 * g + 32, base : base + COLS, :].reshape(32 * COLS, ROWS) for g in range(4)], axis=1
            )
        )
    for xh in range(2):
        total = None
        for left, parts in ((lefts[0], ((own_ref, 0), (x_ref, 0))), (lefts[1], ((core_ref, CH), (xc_ref, 0)))):
            right = jnp.concatenate(
                [ref[at + 32 * xh : at + 32 * xh + 32].reshape(32 * COLS, ROWS) for ref, at in parts], axis=1
            )
            term = contract(right, left, 0, 0)
            total = term if total is None else total + term
        total = total.astype(jnp.bfloat16)
        for rel in range(2):
            for zh in range(2):
                row = 128 * rel + 64 * zh
                y = 4 * xh + 2 * (xb if rel == 0 else 1 - xb) + zh
                for g in range(4):
                    out_ref[g, y] = total[row : row + 64, 128 * g : 128 * g + 128]


def finish_kernel(x_ref, t_ref, gate_ref, proj_ref, in_ref, down_ref, out_ref, stage):
    stage[...] = t_ref[...].astype(jnp.float32)
    hidden = down_ref.shape[0]
    for pair in range(COLS // 2):
        at = [2 * pair + s for s in range(2)]
        tri = jnp.concatenate([stage[pl.ds(j, CH, stride=COLS), :] for j in at], axis=1)
        centred = tri - jnp.mean(tri, axis=0, keepdims=True)
        spread = jnp.mean(centred * centred, axis=0, keepdims=True)
        tri_normed = (centred * lax.rsqrt(spread + EPS)).astype(jnp.bfloat16)
        x = jnp.concatenate([x_ref[pl.ds(j, ROWS, stride=COLS), :] for j in at], axis=0)
        gating = sigmoid(contract(norm_lanes(x), gate_ref[...], 1, 0))
        middle = x + gating * contract(tri_normed, proj_ref[...], 0, 0)
        t = contract(norm_lanes(middle), in_ref[...], 1, 0)
        up = t[:, :hidden]
        units = (up * sigmoid(up) * t[:, hidden:]).astype(jnp.bfloat16)
        result = middle + contract(units, down_ref[...], 1, 0)
        for s, j in enumerate(at):
            out_ref[pl.ds(j, ROWS, stride=COLS), :] = result[s * ROWS : (s + 1) * ROWS]


def call(kernel, outs, scratch=(), flops=0, moved=0):
    return pl.pallas_call(
        kernel,
        out_shape=outs,
        scratch_shapes=list(scratch),
        compiler_params=pltpu.CompilerParams(vmem_limit_bytes=LIMIT),
        cost_estimate=pl.CostEstimate(flops=flops, bytes_accessed=moved, transcendentals=0),
    )


def per_device(pair_rep, pair_proj, gate_proj, out_proj, trans_in, trans_out):
    bf16 = functools.partial(jax.ShapeDtypeStruct, dtype=jnp.bfloat16)
    flat = pair_rep.reshape(ROWS * COLS, CH)
    with jax.named_scope("project"):
        sides = call(
            project_kernel, bf16((CH, 2 * COLS, ROWS)), [pltpu.VMEM((CH * 2 * COLS, ROWS), jnp.float32)], 270_000_000, 2 << 20
        )(flat, pair_proj.T)
    with jax.named_scope("to_channels"):
        sides = lax.all_to_all(sides, PLANE, 0, 0, tiled=True)
    with jax.named_scope("split"):
        own, other, pack = call(
            split_kernel, (bf16((64, COLS, ROWS)), bf16((64, COLS, ROWS)), bf16((CH + 64, COLS, ROWS))), (), 0, 2 << 20
        )(sides)
    with jax.named_scope("share"):
        across = lax.ppermute(own, QUAD, [(d, d ^ 2) for d in range(4)])
        diagonal = lax.ppermute(other, QUAD, [(d, d ^ 3) for d in range(4)])
        pack = lax.ppermute(pack, QUAD, [(d, d ^ 1) for d in range(4)])
    with jax.named_scope("triangle"):
        tri = call(triangle_kernel, bf16((4, 8, 64, ROWS)), (), 540_000_000, 3 << 20)(sides, own, pack, across, diagonal)
    with jax.named_scope("to_columns"):
        tri = lax.all_to_all(tri.reshape(CH, COLS, ROWS), PLANE, 0, 0, tiled=True)
    with jax.named_scope("finish"):
        out = call(
            finish_kernel,
            jax.ShapeDtypeStruct((ROWS * COLS, CH), jnp.float32),
            [pltpu.VMEM((CH * COLS, ROWS), jnp.float32)],
            1_000_000_000,
            3 << 20,
        )(flat, tri.reshape(CH * COLS, ROWS), gate_proj, out_proj, trans_in, trans_out)
    return out.reshape(ROWS, COLS, CH)


def solution(mesh):
    fine = Mesh(mesh.devices.reshape(SIZES), AXES)
    spec = P(("xh", "xb", "zh"), ("y", "zl", "core"), None)
    return jax.shard_map(
        per_device, mesh=fine, in_specs=(spec, P(), P(), P(), P(), P()), out_specs=spec, check_vma=False
    )
```

time: 388 us -> 126 us (0.32)
  waiting for transfers between devices: 303 us -> 10.3 us
  blocking collectives: 0 us -> 82 us
  local copies, waits for them, and re-layouts: 37.3 us -> 3.23 us
  Pallas kernels: 0 us -> 18.9 us
  matrix products: 14.5 us -> 0 us
  between operations: 13.3 us -> 0.04 us
  other arithmetic: 9.77 us -> 0 us
  starting transfers between devices: 6.72 us -> 10.7 us
    all_gather x2 -> x0, waiting for transfers between devices: 246 us -> none  [the longest x1 124 us: per_device(): left_panel = lax.all_gather(left_loc, 'ja', axis=1, tiled=True)]
    all_to_all x0 -> x2, blocking collectives: none -> 82 us  [the longest x1 52.8 us: per_device(): sides = lax.all_to_all(sides, PLANE, 0, 0, tiled=True)]
    reduce_scatter x1 -> x0, waiting for transfers between devices: 57.6 us -> none  [per_device(): lax.psum_scatter(jnp.einsum('jkc,ikc->jic', right_panel, left_panel, pref...]
    pallas_call x0 -> x4, Pallas kernels: none -> 18.9 us  [the longest x1 8.36 us: per_device(): call(finish_kernel, jax.ShapeDtypeStruct((ROWS * COLS, CH), jnp.float32),...]
    dot_general x6 -> x0, matrix products: 14.5 us -> none  [the longest x1 8.51 us: per_device(): jnp.einsum('jkc,ikc->jic', right_panel, left_panel, preferred_element_typ...]
    all_gather x2 -> x0, local copies, waits for them, and re-layouts: 13.6 us -> none  [the longest x1 6.93 us: per_device(): right_full = lax.all_gather(right_loc, 'ia', axis=0, tiled=True)]
    all_to_all x2 -> x0, local copies, waits for them, and re-layouts: 12.1 us -> none  [per_device(): lax.all_to_all(right_full, 'ja', split_axis=0, concat_axis=1, tiled=True)]
    ppermute x0 -> x3, starting transfers between devices: none -> 10.7 us  [the longest x1 5.29 us: per_device(): pack = lax.ppermute(pack, QUAD, [(d, d ^ 1) for d in range(4)])]
  transfers between devices with their start and end apart: 4 -> 3, of which waited for: 3 -> 2; matrix products, arithmetic and copies ran while one was open for 4% -> 0% of each run, Pallas kernels for 0% -> 0%
where the time goes in v1:
time: 126 us; the launch traced here: 125 us
  blocking collectives  82 us (65%)
  Pallas kernels  18.9 us (15%)
  starting transfers between devices  10.7 us (8%)
  waiting for transfers between devices  10.3 us (8%)
  local copies, waits for them, and re-layouts  3.23 us (3%)
    all_to_all x1, blocking collectives, per_device(): sides = lax.all_to_all(sides, PLANE, 0, 0, tiled=True)  52.8 us
    all_to_all x1, blocking collectives, per_device(): tri = lax.all_to_all(tri.reshape(CH, COLS, ROWS), PLANE, 0, 0, tiled=True)  29.2 us
    pallas_call x1, Pallas kernels, per_device(): call(finish_kernel, jax.ShapeDtypeStruct((ROWS * COLS, CH), jnp.float32),...  8.36 us
    ppermute x1, waiting for transfers between devices, per_device(): diagonal = lax.ppermute(other, QUAD, [(d, d ^ 3) for d in range(4)])  5.72 us
    ppermute x1, starting transfers between devices, per_device(): pack = lax.ppermute(pack, QUAD, [(d, d ^ 1) for d in range(4)])  5.29 us
    pallas_call x1, Pallas kernels, per_device(): call(project_kernel, bf16((CH, 2 * COLS, ROWS)), [pltpu.VMEM((CH * 2 * CO...  4.83 us
    ppermute x1, waiting for transfers between devices, per_device(): across = lax.ppermute(own, QUAD, [(d, d ^ 2) for d in range(4)])  4.55 us
    ppermute x1, starting transfers between devices, per_device(): diagonal = lax.ppermute(other, QUAD, [(d, d ^ 3) for d in range(4)])  3.24 us
  transfers between devices with their start and end apart: 3, of which 2 were waited for; matrix products, arithmetic and copies ran while one was open for 0% of the time, Pallas kernels for 0%

profile of v1, /device:TPU:1, one launch (start us, length us, event | category | flops | bytes accessed | tf_op | source)
XLA Modules:
  0.0 125.2 jit_solution(6397267543978949707)
XLA Ops:
  0.0 1.7 %copy.7 = bf16[128,512]{0,1:T(8,128)(2,1)} copy(bf16[128,512]{1,0:T(8,128)(2,1)} %param.7) | data formatting | bytes 262144 | tf_op args[1]
  1.7 4.8 %project.1 = bf16[128,32,128]{2,1,0:T(8,128)(2,1)} custom-call(f32[2048,128]{1,0:T(8,128)} %bitcast.6, bf16[512,128]{1,0:T(8,128)(2,1)} %bitcast.8), custom_call_target="tpu_custom_call" | custom-call | flops 270000000 | bytes 2097152 | tf_op jit(solution)/shard_map/project/pallas_call | solution.py:123
  6.5 52.8 %all_to_all.10.a_ref = bf16[128,32,128]{2,1,0:T(8,128)(2,1)} all-to-all(bf16[128,32,128]{2,1,0:T(8,128)(2,1)} %project.1), channel_id=1, replica_groups=mesh['xh'=2,'xb'=2,'zh'=2,'y'=8,'zl'=4,'core'=2] {'xh','zh','y','zl'}, dimensions={0} | all-to-all | bytes 2097152 | tf_op jit(solution)/shard_map/to_channels/all_to_all | solution.py:127
  59.3 2.6 %split.1 = (bf16[64,16,128]{2,1,0:T(8,128)(2,1)}, bf16[64,16,128]{2,1,0:T(8,128)(2,1)}, bf16[192,16,128]{2,1,0:T(8,128)(2,1)}) custom-call(bf16[128,32,128]{2,1,0:T(8,128)(2,1)} %all_to_all.10.a_ref), custom_call_target="tpu_custom_call" | custom-call | bytes 2097152 | tf_op jit(solution)/shard_map/split/pallas_call | solution.py:129
  61.8 5.3 %collective-permute-start = (bf16[192,16,128]{2,1,0:T(8,128)(2,1)}, bf16[192,16,128]{2,1,0:T(8,128)(2,1)S(1)}, u32[]{:S(2)}, u32[]{:S(2)}) collective-permute-start(bf16[192,16,128]{2,1,0:T(8,128)(2,1)} %get-tuple-element.9), channel_id=1, source_target_pairs={{0,1},{1,0},{128,129},{129,128},{2,3},{3,2},{130,131},{131,130},{4... | collective-permute-start | bytes 2359304 | tf_op jit(solution)/shard_map/share/ppermute | solution.py:135
  67.1 2.2 %collective-permute-start.1 = (bf16[64,16,128]{2,1,0:T(8,128)(2,1)}, bf16[64,16,128]{2,1,0:T(8,128)(2,1)S(1)}, u32[]{:S(2)}, u32[]{:S(2)}) collective-permute-start(bf16[64,16,128]{2,1,0:T(8,128)(2,1)} %get-tuple-element.8.own_ref), channel_id=1, source_target_pairs={{0,128},{1,129},{128,0},{129,1},{2,130},{3,131},{130,2},{131,3},{4... | collective-permute-start | bytes 786440 | tf_op jit(solution)/shard_map/share/ppermute | solution.py:133
  69.3 3.2 %collective-permute-start.2 = (bf16[64,16,128]{2,1,0:T(8,128)(2,1)}, bf16[64,16,128]{2,1,0:T(8,128)(2,1)S(1)}, u32[]{:S(2)}, u32[]{:S(2)}) collective-permute-start(bf16[64,16,128]{2,1,0:T(8,128)(2,1)} %get-tuple-element.10), channel_id=1, source_target_pairs={{0,129},{1,128},{128,1},{129,0},{2,131},{3,130},{130,3},{131,2},{4... | collective-permute-start | bytes 786440 | tf_op jit(solution)/shard_map/share/ppermute | solution.py:134
  72.6 4.6 %collective-permute-done.1.x_ref = bf16[64,16,128]{2,1,0:T(8,128)(2,1)S(1)} collective-permute-done((bf16[64,16,128]{2,1,0:T(8,128)(2,1)}, bf16[64,16,128]{2,1,0:T(8,128)(2,1)S(1)}, u32[]{:S(2)}, u32[]{:S(2)}) %collective-permute-start.1) | collective-permute-done | bytes 262176 | tf_op jit(solution)/shard_map/share/ppermute | solution.py:133
  77.1 0.0 copy-start.1
  77.1 5.7 %collective-permute-done.2.xc_ref = bf16[64,16,128]{2,1,0:T(8,128)(2,1)S(1)} collective-permute-done((bf16[64,16,128]{2,1,0:T(8,128)(2,1)}, bf16[64,16,128]{2,1,0:T(8,128)(2,1)S(1)}, u32[]{:S(2)}, u32[]{:S(2)}) %collective-permute-start.2) | collective-permute-done | bytes 262176 | tf_op jit(solution)/shard_map/share/ppermute | solution.py:134
  82.9 0.0 copy-start.2
  82.9 0.0 collective-permute-done.core_ref
  82.9 0.0 copy-done.1
  82.9 0.7 copy-done.2
  83.6 0.0 copy-start
  83.6 0.9 copy-done
  84.4 3.2 %triangle.1 = bf16[4,8,64,128]{3,2,1,0:T(8,128)(2,1)} custom-call(bf16[128,32,128]{2,1,0:T(8,128)(2,1)} %all_to_all.10.a_ref, bf16[64,16,128]{2,1,0:T(8,128)(2,1)} %get-tuple-element.8.own_ref, bf16[192,16,128]{2,1,0:T(8,128)(2,1)} %copy-done, bf16[64,16,128]{2,1,0:T(8,128)(2,1)} %copy-done.1, bf16[64,16,128]{2,1,0:T(8,128)(2,1)} %copy-done.2), custom_call_target="tpu_custom_call" | custom-call | flops 540000000 | bytes 3145728 | tf_op jit(solution)/shard_map/triangle/pallas_call | solution.py:137
  87.6 29.2 %all_to_all.11 = bf16[128,16,128]{2,1,0:T(8,128)(2,1)} all-to-all(bf16[128,16,128]{2,1,0:T(8,128)(2,1)} %bitcast.5), channel_id=1, replica_groups=mesh['xh'=2,'xb'=2,'zh'=2,'y'=8,'zl'=4,'core'=2] {'xh','zh','y','zl'}, dimensions={0} | all-to-all | bytes 1048576 | tf_op jit(solution)/shard_map/to_columns/all_to_all | solution.py:139
  116.8 8.4 %finish.1 = f32[2048,128]{1,0:T(8,128)} custom-call(f32[2048,128]{1,0:T(8,128)} %bitcast.7, bf16[2048,128]{1,0:T(8,128)(2,1)} %bitcast.9, bf16[128,128]{1,0:T(8,128)(2,1)} %gate_ref.1, bf16[128,128]{1,0:T(8,128)(2,1)} %proj_ref.1, bf16[128,1024]{1,0:T(8,128)(2,1)} %in_ref.1, bf16[512,128]{1,0:T(8,128)(2,1)} %down_ref.1), custom_call_target="tpu_custom_call" | custom-call | flops 1000000000 | bytes 3145728 | tf_op jit(solution)/shard_map/finish/pallas_call | solution.py:141
Async XLA Ops:
  61.8 21.1 %collective-permute-start = (bf16[192,16,128]{2,1,0:T(8,128)(2,1)}, bf16[192,16,128]{2,1,0:T(8,128)(2,1)S(1)}, u32[]{:S(2)}, u32[]{:S(2)}) collective-permute-start(bf16[192,16,128]{2,1,0:T(8,128)(2,1)} %get-tuple-element.9), channel_id=1, source_target_pairs={{0,1},{1,0},{128,129},{129,128},{2,3},{3,2},{130,131},{131,130},{4... | collective-permute-start | bytes 2359304 | tf_op jit(solution)/shard_map/share/ppermute | solution.py:135
  67.1 10.0 %collective-permute-start.1 = (bf16[64,16,128]{2,1,0:T(8,128)(2,1)}, bf16[64,16,128]{2,1,0:T(8,128)(2,1)S(1)}, u32[]{:S(2)}, u32[]{:S(2)}) collective-permute-start(bf16[64,16,128]{2,1,0:T(8,128)(2,1)} %get-tuple-element.8.own_ref), channel_id=1, source_target_pairs={{0,128},{1,129},{128,0},{129,1},{2,130},{3,131},{130,2},{131,3},{4... | collective-permute-start | bytes 786440 | tf_op jit(solution)/shard_map/share/ppermute | solution.py:133
  69.3 13.5 %collective-permute-start.2 = (bf16[64,16,128]{2,1,0:T(8,128)(2,1)}, bf16[64,16,128]{2,1,0:T(8,128)(2,1)S(1)}, u32[]{:S(2)}, u32[]{:S(2)}) collective-permute-start(bf16[64,16,128]{2,1,0:T(8,128)(2,1)} %get-tuple-element.10), channel_id=1, source_target_pairs={{0,129},{1,128},{128,1},{129,0},{2,131},{3,130},{130,3},{131,2},{4... | collective-permute-start | bytes 786440 | tf_op jit(solution)/shard_map/share/ppermute | solution.py:134
  77.1 5.7 %copy-start.1 = (bf16[64,16,128]{2,1,0:T(8,128)(2,1)}, bf16[64,16,128]{2,1,0:T(8,128)(2,1)S(1)}, u32[]{:S(2)}) copy-start(bf16[64,16,128]{2,1,0:T(8,128)(2,1)S(1)} %collective-permute-done.1.x_ref) | copy-start | bytes 786436
  82.9 0.7 copy-start.2
  83.6 0.9 copy-start

commit v2 on v1

v2 whole, which is shorter than its diff:
```python
import functools

import jax
import jax.numpy as jnp
from jax import lax
from jax.experimental import pallas as pl
from jax.experimental.pallas import tpu as pltpu
from jax.sharding import Mesh
from jax.sharding import PartitionSpec as P

AXES = ("xh", "xb", "zh", "y", "zl", "core")
SIZES = (2, 2, 2, 8, 4, 2)
PLANE = ("xh", "zh", "y", "zl")
QUAD = ("xb", "core")
ROWS = 128
COLS = 16
CH = 128
PAIRS = COLS // 2
EPS = 1e-05
LIMIT = 16 * 1024 * 1024


def sigmoid(v):
    return 0.5 * jnp.tanh(0.5 * v) + 0.5


def norm_rows(v):
    centred = v - jnp.mean(v, axis=0, keepdims=True)
    spread = jnp.mean(centred * centred, axis=0, keepdims=True)
    return (centred * lax.rsqrt(spread + EPS)).astype(jnp.bfloat16)


def dot(a, b):
    return jnp.dot(a, b, preferred_element_type=jnp.float32)


def columns(ref, pair):
    return jnp.concatenate([ref[pl.ds(2 * pair + s, ROWS, stride=COLS), :].T for s in range(2)], axis=1)


def project_kernel(x_ref, w_ref, out_ref, stage):
    weights = w_ref[...].T
    for pair in range(PAIRS):
        p = dot(weights, norm_rows(columns(x_ref, pair)))
        for base, at in ((COLS, 0), (0, 2 * CH)):
            product = sigmoid(p[at : at + CH]) * p[at + CH : at + 2 * CH]
            for s in range(2):
                stage[pl.ds(base + 2 * pair + s, CH, stride=2 * COLS), :] = product[:, s * ROWS : (s + 1) * ROWS]
    out_ref[...] = stage[...].astype(jnp.bfloat16).reshape(CH, 2 * COLS, ROWS)


def gate_kernel(x_ref, gate_ref, proj_ref, in_ref, down_ref, xt_ref, gating_ref, proj_t_ref, in_t_ref, down_t_ref):
    weights = gate_ref[...].T
    for pair in range(PAIRS):
        xt = columns(x_ref, pair)
        xt_ref[pair] = xt
        gating_ref[pair] = sigmoid(dot(weights, norm_rows(xt)))
    proj_t_ref[...] = proj_ref[...].T
    in_t_ref[...] = in_ref[...].T
    down_t_ref[...] = down_ref[...].T


def triangle_kernel(left_ref, right_ref, keep_ref, send_ref):
    core = lax.axis_index("core")
    left = jnp.concatenate(
        [left_ref[32 * g : 32 * g + 32, COLS:, :].reshape(32 * COLS, ROWS) for g in range(4)], axis=1
    )
    for xh in range(2):
        right = jnp.concatenate(
            [right_ref[64 * xh + 32 * zh : 64 * xh + 32 * zh + 32].reshape(32 * COLS, ROWS) for zh in range(2)], axis=1
        )
        part = lax.dot_general(right, left, (((0,), (0,)), ((), ())), preferred_element_type=jnp.float32)
        part = part.astype(jnp.bfloat16).reshape(2, 4, 2, 16, 4 * ROWS)
        first, second = part[:, :, 0], part[:, :, 1]
        keep = jnp.where(core == 0, first, second)
        send = jnp.where(core == 0, second, first)
        for g in range(4):
            keep_ref[g, xh] = keep[..., g * ROWS : (g + 1) * ROWS]
            send_ref[g, xh] = send[..., g * ROWS : (g + 1) * ROWS]


def add_kernel(keep_ref, got_ref, keep_x_ref, got_x_ref, out_ref):
    xb = lax.axis_index("xb")
    for a, b, at in ((keep_ref, got_ref, xb), (keep_x_ref, got_x_ref, 1 - xb)):
        for xh in range(2):
            for zh in range(2):
                total = a[:, xh, zh].astype(jnp.float32) + b[:, xh, zh].astype(jnp.float32)
                out_ref[:, 4 * xh + 2 * at + zh] = total.astype(jnp.bfloat16)


def finish_kernel(xt_ref, gating_ref, t_ref, proj_ref, in_ref, down_ref, out_ref, stage):
    stage[...] = t_ref[...].astype(jnp.float32)
    hidden = down_ref.shape[1]
    for pair in range(PAIRS):
        at = [2 * pair + s for s in range(2)]
        tri = jnp.concatenate([stage[pl.ds(j, CH, stride=COLS), :] for j in at], axis=1)
        middle = xt_ref[pair] + gating_ref[pair] * dot(proj_ref[...], norm_rows(tri))
        t = dot(in_ref[...], norm_rows(middle))
        up = t[:hidden]
        units = (up * sigmoid(up) * t[hidden:]).astype(jnp.bfloat16)
        result = middle + dot(down_ref[...], units)
        for s, j in enumerate(at):
            out_ref[pl.ds(j, ROWS, stride=COLS), :] = result[:, s * ROWS : (s + 1) * ROWS].T


def call(kernel, outs, scratch=(), flops=0, moved=0):
    return pl.pallas_call(
        kernel,
        out_shape=outs,
        scratch_shapes=list(scratch),
        compiler_params=pltpu.CompilerParams(vmem_limit_bytes=LIMIT),
        cost_estimate=pl.CostEstimate(flops=flops, bytes_accessed=moved, transcendentals=0),
    )


def per_device(pair_rep, pair_proj, gate_proj, out_proj, trans_in, trans_out):
    bf16 = functools.partial(jax.ShapeDtypeStruct, dtype=jnp.bfloat16)
    f32 = functools.partial(jax.ShapeDtypeStruct, dtype=jnp.float32)
    flat = pair_rep.reshape(ROWS * COLS, CH)
    with jax.named_scope("project"):
        sides = call(
            project_kernel, bf16((CH, 2 * COLS, ROWS)), [pltpu.VMEM((CH * 2 * COLS, ROWS), jnp.float32)], 270_000_000, 2 << 20
        )(flat, pair_proj)
    flat, sides = lax.optimization_barrier((flat, sides))
    with jax.named_scope("gate"):
        wide = f32((PAIRS, CH, 2 * ROWS))
        xt, gating, proj_t, in_t, down_t = call(
            gate_kernel,
            (wide, wide, bf16(out_proj.shape[::-1]), bf16(trans_in.shape[::-1]), bf16(trans_out.shape[::-1])),
            (),
            70_000_000,
            4 << 20,
        )(flat, gate_proj, out_proj, trans_in, trans_out)
    with jax.named_scope("to_channels"):
        sides = lax.all_to_all(sides, PLANE, 0, 0, tiled=True)
    with jax.named_scope("right_values"):
        right = sides[:, :COLS]
    with jax.named_scope("right_across_x"):
        right_x = lax.ppermute(right, QUAD, [(d, d ^ 2) for d in range(4)])
    part = bf16((4, 2, 2, 4, 16, ROWS))
    with jax.named_scope("triangle_own"):
        keep, send = call(triangle_kernel, (part, part), (), 270_000_000, 2 << 20)(sides, right)
    with jax.named_scope("sums_to_core"):
        got = lax.ppermute(send, QUAD, [(d, d ^ 1) for d in range(4)])
    with jax.named_scope("triangle_across"):
        keep_x, send_x = call(triangle_kernel, (part, part), (), 270_000_000, 2 << 20)(sides, right_x)
    with jax.named_scope("sums_to_core_across"):
        got_x = lax.ppermute(send_x, QUAD, [(d, d ^ 1) for d in range(4)])
    with jax.named_scope("add"):
        tri = call(add_kernel, bf16((4, 8, 4, 16, ROWS)), (), 1_000_000, 2 << 20)(keep, got, keep_x, got_x)
    with jax.named_scope("to_columns"):
        tri = lax.all_to_all(tri.reshape(CH, COLS, ROWS), PLANE, 0, 0, tiled=True)
    with jax.named_scope("finish"):
        out = call(
            finish_kernel,
            f32((ROWS * COLS, CH)),
            [pltpu.VMEM((CH * COLS, ROWS), jnp.float32)],
            1_000_000_000,
            4 << 20,
        )(xt, gating, tri.reshape(CH * COLS, ROWS), proj_t, in_t, down_t)
    return out.reshape(ROWS, COLS, CH)


def solution(mesh):
    fine = Mesh(mesh.devices.reshape(SIZES), AXES)
    spec = P(("xh", "xb", "zh"), ("y", "zl", "core"), None)
    return jax.shard_map(
        per_device, mesh=fine, in_specs=(spec, P(), P(), P(), P(), P()), out_specs=spec, check_vma=False
    )
```

time: 126 us -> 116 us (0.921)
  blocking collectives: 82 us -> 52.5 us
  waiting for transfers between devices: 10.3 us -> 24.5 us
  starting transfers between devices: 10.7 us -> 22 us
  Pallas kernels: 18.9 us -> 11.5 us
    all_to_all x1 -> x0, blocking collectives: 29.2 us -> none  [per_device(): tri = lax.all_to_all(tri.reshape(CH, COLS, ROWS), PLANE, 0, 0, tiled=True)]
    all_to_all x0 -> x1, waiting for transfers between devices: none -> 19.8 us  [per_device(): tri = lax.all_to_all(tri.reshape(CH, COLS, ROWS), PLANE, 0, 0, tiled=True)]
    all_to_all x0 -> x1, starting transfers between devices: none -> 8 us  [per_device(): tri = lax.all_to_all(tri.reshape(CH, COLS, ROWS), PLANE, 0, 0, tiled=True)]
    ppermute x3, waiting for transfers between devices: 10.3 us -> 4.75 us  [the longest x1 3.62 us: per_device(): right_x = lax.ppermute(right, QUAD, [(d, d ^ 2) for d in range(4)])]
    pallas_call x3 -> x5, Pallas kernels: 14.1 us -> 9.16 us  [the longest x1 6.6 us: per_device(): call(finish_kernel, f32((ROWS * COLS, CH)), [pltpu.VMEM((CH * COLS, ROWS)...]
    ppermute x3, starting transfers between devices: 10.7 us -> 14 us  [the longest x1 6.23 us: per_device(): got_x = lax.ppermute(send_x, QUAD, [(d, d ^ 1) for d in range(4)])]
    pallas_call x1, Pallas kernels: 4.83 us -> 2.31 us  [per_device(): call(project_kernel, bf16((CH, 2 * COLS, ROWS)), [pltpu.VMEM((CH * 2 * CO...]
    unnamed x7 -> x18, local copies, waits for them, and re-layouts: 3.23 us -> 4.34 us
  transfers between devices with their start and end apart: 3 -> 4, of which waited for: 2 -> 3; matrix products, arithmetic and copies ran while one was open for 0% -> 0% of each run, Pallas kernels for 0% -> 1%
where the time goes in v2:
time: 116 us; the launch traced here: 115 us
  blocking collectives  52.5 us (45%)
  waiting for transfers between devices  24.5 us (21%)
  starting transfers between devices  22 us (19%)
  Pallas kernels  11.5 us (10%)
  local copies, waits for them, and re-layouts  4.37 us (4%)
    all_to_all x1, blocking collectives, per_device(): sides = lax.all_to_all(sides, PLANE, 0, 0, tiled=True)  52.5 us
    all_to_all x1, waiting for transfers between devices, per_device(): tri = lax.all_to_all(tri.reshape(CH, COLS, ROWS), PLANE, 0, 0, tiled=True)  19.8 us
    all_to_all x1, starting transfers between devices, per_device(): tri = lax.all_to_all(tri.reshape(CH, COLS, ROWS), PLANE, 0, 0, tiled=True)  8 us
    pallas_call x1, Pallas kernels, per_device(): call(finish_kernel, f32((ROWS * COLS, CH)), [pltpu.VMEM((CH * COLS, ROWS)...  6.6 us
    ppermute x1, starting transfers between devices, per_device(): got_x = lax.ppermute(send_x, QUAD, [(d, d ^ 1) for d in range(4)])  6.23 us
    ppermute x1, starting transfers between devices, per_device(): got = lax.ppermute(send, QUAD, [(d, d ^ 1) for d in range(4)])  5.6 us
    unnamed x18, local copies, waits for them, and re-layouts  4.34 us
    ppermute x1, waiting for transfers between devices, per_device(): right_x = lax.ppermute(right, QUAD, [(d, d ^ 2) for d in range(4)])  3.62 us
  transfers between devices with their start and end apart: 4, of which 3 were waited for; matrix products, arithmetic and copies ran while one was open for 0% of the time, Pallas kernels for 1%

profile of v2, /device:TPU:1, one launch (start us, length us, event | category | flops | bytes accessed | tf_op | source)
XLA Modules:
  0.0 115.0 jit_solution(4143983871801266853)
XLA Ops:
  0.0 0.0 copy-start
  0.0 1.2 %copy-done = f32[128,16,128]{2,1,0:T(8,128)S(1)} copy-done((f32[128,16,128]{2,1,0:T(8,128)S(1)}, f32[128,16,128]{2,1,0:T(8,128)}, u32[]{:S(2)}) %copy-start) | copy-done | bytes 1048600
  1.2 0.0 copy-start.5
  1.2 0.9 copy-done.5
  2.1 2.3 %project.1 = bf16[128,32,128]{2,1,0:T(8,128)(2,1)S(1)} custom-call(f32[2048,128]{1,0:T(8,128)S(1)} %bitcast.4, bf16[128,512]{1,0:T(8,128)(2,1)S(1)} %copy-done.5), custom_call_target="tpu_custom_call" | custom-call | flops 270000000 | bytes 2097152 | tf_op jit(solution)/shard_map/project/pallas_call | solution.py:121
  4.4 52.5 %all_to_all.10.left_ref = bf16[128,32,128]{2,1,0:T(8,128)(2,1)S(1)} all-to-all(bf16[128,32,128]{2,1,0:T(8,128)(2,1)S(1)} %project.1), channel_id=1, replica_groups=mesh['xh'=2,'xb'=2,'zh'=2,'y'=8,'zl'=4,'core'=2] {'xh','zh','y','zl'}, dimensions={0} | all-to-all | bytes 2097152 | tf_op jit(solution)/shard_map/to_channels/all_to_all | solution.py:135
  56.9 2.2 %collective-permute-start.1 = (bf16[128,16,128]{2,1,0:T(8,128)(2,1)S(1)}, bf16[128,16,128]{2,1,0:T(8,128)(2,1)S(1)}, u32[]{:S(2)}, u32[]{:S(2)}) collective-permute-start(bf16[128,16,128]{2,1,0:T(8,128)(2,1)S(1)} %slice.4.right_ref), channel_id=1, source_target_pairs={{0,128},{1,129},{128,0},{129,1},{2,130},{3,131},{130,2},{131,3},{4... | collective-permute-start | bytes 1572872 | tf_op jit(solution)/shard_map/right_across_x/ppermute | solution.py:139
  59.2 0.5 triangle_own.1
  59.6 5.6 %collective-permute-start = (bf16[4,2,2,4,16,128]{5,4,3,2,1,0:T(8,128)(2,1)S(1)}, bf16[4,2,2,4,16,128]{5,4,3,2,1,0:T(8,128)(2,1)S(1)}, u32[]{:S(2)}, u32[]{:S(2)}) collective-permute-start(bf16[4,2,2,4,16,128]{5,4,3,2,1,0:T(8,128)(2,1)S(1)} %get-tuple-element.21), channel_id=1, source_target_pairs={{0,1},{1,0},{128,129},{129,128},{2,3},{3,2},{130,131},{131,130},{4... | collective-permute-start | bytes 786440 | tf_op jit(solution)/shard_map/sums_to_core/ppermute | solution.py:144
  65.2 3.6 %collective-permute-done.1.right_ref = bf16[128,16,128]{2,1,0:T(8,128)(2,1)S(1)} collective-permute-done((bf16[128,16,128]{2,1,0:T(8,128)(2,1)S(1)}, bf16[128,16,128]{2,1,0:T(8,128)(2,1)S(1)}, u32[]{:S(2)}, u32[]{:S(2)}) %collective-permute-start.1) | collective-permute-done | bytes 524320 | tf_op jit(solution)/shard_map/right_across_x/ppermute | solution.py:139
  68.9 0.5 triangle_across.1
  69.3 6.2 %collective-permute-start.2 = (bf16[4,2,2,4,16,128]{5,4,3,2,1,0:T(8,128)(2,1)S(1)}, bf16[4,2,2,4,16,128]{5,4,3,2,1,0:T(8,128)(2,1)S(1)}, u32[]{:S(2)}, u32[]{:S(2)}) collective-permute-start(bf16[4,2,2,4,16,128]{5,4,3,2,1,0:T(8,128)(2,1)S(1)} %get-tuple-element.23), channel_id=1, source_target_pairs={{0,1},{1,0},{128,129},{129,128},{2,3},{3,2},{130,131},{131,130},{4... | collective-permute-start | bytes 786440 | tf_op jit(solution)/shard_map/sums_to_core_across/ppermute | solution.py:148
  75.6 0.0 collective-permute-done.got_ref
  75.6 1.1 collective-permute-done.2.got_x_ref
  76.7 0.0 copy-start.1
  76.7 0.9 add.1
  77.6 0.0 copy-start.4
  77.6 0.0 copy-start.6
  77.6 0.0 copy-start.7
  77.6 0.0 copy-start.8
  77.6 8.0 %all-to-all-start.1 = ((bf16[128,16,128]{2,1,0:T(8,128)(2,1)}), bf16[128,16,128]{2,1,0:T(8,128)(2,1)S(1)}, u32[]{:S(2)}, u32[]{:S(2)}) async-start(bf16[128,16,128]{2,1,0:T(8,128)(2,1)} %bitcast.1), calls=%async_computation.1 | async-start | bytes 1048576 | tf_op jit(solution)/shard_map/to_columns/all_to_all | solution.py:152
  85.7 0.0 copy-done.1
  85.7 0.0 copy-done.4
  85.7 0.0 copy-done.6
  85.7 0.0 copy-done.7
  85.7 0.0 copy-done.8
  85.7 0.7 gate.1
  86.4 0.0 copy-start.2
  86.4 1.0 copy-done.2
  87.4 19.8 %all-to-all-done.1 = bf16[128,16,128]{2,1,0:T(8,128)(2,1)S(1)} async-done(((bf16[128,16,128]{2,1,0:T(8,128)(2,1)}), bf16[128,16,128]{2,1,0:T(8,128)(2,1)S(1)}, u32[]{:S(2)}, u32[]{:S(2)}) %all-to-all-start.1) | async-done | bytes 524320 | tf_op jit(solution)/shard_map/to_columns/all_to_all | solution.py:152
  107.2 0.0 copy-start.3
  107.2 1.2 %copy-done.3 = f32[8,128,256]{2,1,0:T(8,128)S(1)} copy-done((f32[8,128,256]{2,1,0:T(8,128)S(1)}, f32[8,128,256]{2,1,0:T(8,128)}, u32[]{:S(2)}) %copy-start.3) | copy-done | bytes 1048600
  108.4 6.6 %finish.1 = f32[2048,128]{1,0:T(8,128)} custom-call(f32[8,128,256]{2,1,0:T(8,128)S(1)} %get-tuple-element.17.xt_ref, f32[8,128,256]{2,1,0:T(8,128)S(1)} %copy-done.3, bf16[2048,128]{1,0:T(8,128)(2,1)S(1)} %bitcast.6, bf16[128,128]{1,0:T(8,128)(2,1)S(1)} %get-tuple-element.24.proj_ref, bf16[1024,128]{1,0:T(8,128)(2,1)S(1)} %get-tuple-element.25.in_ref, ...), custom_call_target="tpu_custom_call" | custom-call | flops 1000000000 | bytes 4194304 | tf_op jit(solution)/shard_map/finish/pallas_call | solution.py:154
  (1 shorter events, 0.0 us)
Async XLA Ops:
  0.0 1.2 %copy-start = (f32[128,16,128]{2,1,0:T(8,128)S(1)}, f32[128,16,128]{2,1,0:T(8,128)}, u32[]{:S(2)}) copy-start(f32[128,16,128]{2,1,0:T(8,128)} %param.6) | copy-start | bytes 3145732
  1.2 0.9 copy-start.5
  56.9 11.9 %collective-permute-start.1 = (bf16[128,16,128]{2,1,0:T(8,128)(2,1)S(1)}, bf16[128,16,128]{2,1,0:T(8,128)(2,1)S(1)}, u32[]{:S(2)}, u32[]{:S(2)}) collective-permute-start(bf16[128,16,128]{2,1,0:T(8,128)(2,1)S(1)} %slice.4.right_ref), channel_id=1, source_target_pairs={{0,128},{1,129},{128,0},{129,1},{2,130},{3,131},{130,2},{131,3},{4... | collective-permute-start | bytes 1572872 | tf_op jit(solution)/shard_map/right_across_x/ppermute | solution.py:139
  59.6 15.9 %collective-permute-start = (bf16[4,2,2,4,16,128]{5,4,3,2,1,0:T(8,128)(2,1)S(1)}, bf16[4,2,2,4,16,128]{5,4,3,2,1,0:T(8,128)(2,1)S(1)}, u32[]{:S(2)}, u32[]{:S(2)}) collective-permute-start(bf16[4,2,2,4,16,128]{5,4,3,2,1,0:T(8,128)(2,1)S(1)} %get-tuple-element.21), channel_id=1, source_target_pairs={{0,1},{1,0},{128,129},{129,128},{2,3},{3,2},{130,131},{131,130},{4... | collective-permute-start | bytes 786440 | tf_op jit(solution)/shard_map/sums_to_core/ppermute | solution.py:144
  69.3 7.4 %collective-permute-start.2 = (bf16[4,2,2,4,16,128]{5,4,3,2,1,0:T(8,128)(2,1)S(1)}, bf16[4,2,2,4,16,128]{5,4,3,2,1,0:T(8,128)(2,1)S(1)}, u32[]{:S(2)}, u32[]{:S(2)}) collective-permute-start(bf16[4,2,2,4,16,128]{5,4,3,2,1,0:T(8,128)(2,1)S(1)} %get-tuple-element.23), channel_id=1, source_target_pairs={{0,1},{1,0},{128,129},{129,128},{2,3},{3,2},{130,131},{131,130},{4... | collective-permute-start | bytes 786440 | tf_op jit(solution)/shard_map/sums_to_core_across/ppermute | solution.py:148
  76.7 8.9 %copy-start.1 = (f32[128,16,128]{2,1,0:T(8,128)S(1)}, f32[128,16,128]{2,1,0:T(8,128)}, u32[]{:S(2)}) copy-start(f32[128,16,128]{2,1,0:T(8,128)} %param.6) | copy-start | bytes 3145732
  77.6 8.0 %copy-start.4 = (bf16[128,1024]{1,0:T(8,128)(2,1)S(1)}, bf16[128,1024]{1,0:T(8,128)(2,1)}, u32[]{:S(2)}) copy-start(bf16[128,1024]{1,0:T(8,128)(2,1)} %in_ref.1) | copy-start | bytes 786436
  77.6 8.0 %copy-start.6 = (bf16[512,128]{1,0:T(8,128)(2,1)S(1)}, bf16[512,128]{1,0:T(8,128)(2,1)}, u32[]{:S(2)}) copy-start(bf16[512,128]{1,0:T(8,128)(2,1)} %down_ref.1) | copy-start | bytes 393220
  77.6 8.0 %copy-start.7 = (bf16[128,128]{1,0:T(8,128)(2,1)S(1)}, bf16[128,128]{1,0:T(8,128)(2,1)}, u32[]{:S(2)}) copy-start(bf16[128,128]{1,0:T(8,128)(2,1)} %gate_ref.1) | copy-start | bytes 98308
  77.6 8.1 %copy-start.8 = (bf16[128,128]{1,0:T(8,128)(2,1)S(1)}, bf16[128,128]{1,0:T(8,128)(2,1)}, u32[]{:S(2)}) copy-start(bf16[128,128]{1,0:T(8,128)(2,1)} %proj_ref.1) | copy-start | bytes 98308
  77.6 29.5 %all-to-all-start.1 = ((bf16[128,16,128]{2,1,0:T(8,128)(2,1)}), bf16[128,16,128]{2,1,0:T(8,128)(2,1)S(1)}, u32[]{:S(2)}, u32[]{:S(2)}) async-start(bf16[128,16,128]{2,1,0:T(8,128)(2,1)} %bitcast.1), calls=%async_computation.1 | async-start | bytes 1048576 | tf_op jit(solution)/shard_map/to_columns/all_to_all | solution.py:152
  86.4 1.0 copy-start.2
  107.2 1.2 %copy-start.3 = (f32[8,128,256]{2,1,0:T(8,128)S(1)}, f32[8,128,256]{2,1,0:T(8,128)}, u32[]{:S(2)}) copy-start(f32[8,128,256]{2,1,0:T(8,128)} %copy-done.2) | copy-start | bytes 3145732

commit v3 on v2

v3 whole, which is shorter than its diff:
```python
import functools

import jax
import jax.numpy as jnp
from jax import lax
from jax.experimental import pallas as pl
from jax.experimental.pallas import tpu as pltpu
from jax.sharding import Mesh
from jax.sharding import PartitionSpec as P

AXES = ("xh", "xb", "zh", "y", "zl", "core")
SIZES = (2, 2, 2, 8, 4, 2)
PLANE = ("xh", "zh", "y", "zl")
QUAD = ("xb", "core")
ROWS = 128
COLS = 16
CH = 128
HALF = COLS // 2
SIDES = 2 * COLS + 8
SUMS = COLS + 8
EPS = 1e-05
LIMIT = 16 * 1024 * 1024


def sigmoid(v):
    return 0.5 * jnp.tanh(0.5 * v) + 0.5


def norm_rows(v):
    centred = v - jnp.mean(v, axis=0, keepdims=True)
    spread = jnp.mean(centred * centred, axis=0, keepdims=True)
    return (centred * lax.rsqrt(spread + EPS)).astype(jnp.bfloat16)


def dot(a, b):
    return jnp.dot(a, b, preferred_element_type=jnp.float32)


def half_columns(ref, h):
    return jnp.concatenate([ref[pl.ds(HALF * h + s, ROWS, stride=COLS), :].T for s in range(HALF)], axis=1)


def project_kernel(x_ref, w_ref, out_ref, stage):
    weights = w_ref[...].T
    for h in range(2):
        p = dot(weights, norm_rows(half_columns(x_ref, h)))
        for base, at in ((COLS, 0), (0, 2 * CH)):
            product = sigmoid(p[at : at + CH]) * p[at + CH : at + 2 * CH]
            for s in range(HALF):
                stage[pl.ds(base + HALF * h + s, CH, stride=SIDES), :] = product[:, s * ROWS : (s + 1) * ROWS]
    out_ref[...] = stage[...].reshape(CH, SIDES, ROWS)[:, : 2 * COLS].astype(jnp.bfloat16)


def gate_kernel(x_ref, gate_ref, proj_ref, in_ref, down_ref, xt_ref, gating_ref, proj_t_ref, in_t_ref, down_t_ref):
    weights = gate_ref[...].T
    for h in range(2):
        xt = half_columns(x_ref, h)
        xt_ref[h] = xt
        gating_ref[h] = sigmoid(dot(weights, norm_rows(xt)))
    proj_t_ref[...] = proj_ref[...].T
    in_t_ref[...] = in_ref[...].T
    down_t_ref[...] = down_ref[...].T


def triangle_kernel(left_ref, right_ref, keep_ref, send_ref):
    core = lax.axis_index("core")
    left = jnp.concatenate(
        [left_ref[32 * g : 32 * g + 32, COLS:, :].reshape(32 * COLS, ROWS) for g in range(4)], axis=1
    )
    for xh in range(2):
        right = jnp.concatenate(
            [right_ref[64 * xh + 32 * zh : 64 * xh + 32 * zh + 32].reshape(32 * COLS, ROWS) for zh in range(2)], axis=1
        )
        part = lax.dot_general(right, left, (((0,), (0,)), ((), ())), preferred_element_type=jnp.float32)
        part = part.astype(jnp.bfloat16).reshape(2, 4, 2, 16, 4 * ROWS)
        first, second = part[:, :, 0], part[:, :, 1]
        keep = jnp.where(core == 0, first, second)
        send = jnp.where(core == 0, second, first)
        for g in range(4):
            keep_ref[g, xh] = keep[..., g * ROWS : (g + 1) * ROWS]
            send_ref[g, xh] = send[..., g * ROWS : (g + 1) * ROWS]


def add_kernel(keep_ref, got_ref, keep_x_ref, got_x_ref, out_ref):
    xb = lax.axis_index("xb")
    for a, b, at in ((keep_ref, got_ref, xb), (keep_x_ref, got_x_ref, 1 - xb)):
        for xh in range(2):
            for zh in range(2):
                total = a[:, xh, zh].astype(jnp.float32) + b[:, xh, zh].astype(jnp.float32)
                out_ref[:, 4 * xh + 2 * at + zh] = total.astype(jnp.bfloat16)


def finish_kernel(xt_ref, gating_ref, t_ref, proj_ref, in_ref, down_ref, out_hbm, stage, held, sems):
    stage[:, :COLS] = t_ref[...].astype(jnp.float32)
    rows = stage.reshape(CH * SUMS, ROWS)
    hidden = down_ref.shape[1]
    copies = []
    for h in range(2):
        tri = jnp.concatenate([rows[pl.ds(HALF * h + s, CH, stride=SUMS), :] for s in range(HALF)], axis=1)
        middle = xt_ref[h] + gating_ref[h] * dot(proj_ref[...], norm_rows(tri))
        t = dot(in_ref[...], norm_rows(middle))
        up = t[:hidden]
        units = (up * sigmoid(up) * t[hidden:]).astype(jnp.bfloat16)
        result = middle + dot(down_ref[...], units)
        for s in range(HALF):
            held.at[h][pl.ds(s, ROWS, stride=HALF), :] = result[:, s * ROWS : (s + 1) * ROWS].T
        copy = pltpu.make_async_copy(
            held.at[h].reshape(ROWS, HALF, CH), out_hbm.at[:, pl.ds(HALF * h, HALF), :], sems.at[h]
        )
        copy.start()
        copies.append(copy)
    for copy in copies:
        copy.wait()


VMEM = pl.BlockSpec(memory_space=pltpu.VMEM)
HBM = pl.BlockSpec(memory_space=pltpu.HBM)
HELD = pltpu.VMEM((2, ROWS * HALF, CH), jnp.float32)


def call(kernel, ins, outs, scratch=(), flops=0, moved=0, out_specs=None):
    many = isinstance(outs, tuple)
    return pl.pallas_call(
        kernel,
        out_shape=outs,
        in_specs=ins,
        out_specs=out_specs if out_specs is not None else ((VMEM,) * len(outs) if many else VMEM),
        scratch_shapes=list(scratch),
        compiler_params=pltpu.CompilerParams(vmem_limit_bytes=LIMIT),
        cost_estimate=pl.CostEstimate(flops=flops, bytes_accessed=moved, transcendentals=0),
    )


def per_device(pair_rep, pair_proj, gate_proj, out_proj, trans_in, trans_out):
    bf16 = functools.partial(jax.ShapeDtypeStruct, dtype=jnp.bfloat16)
    f32 = functools.partial(jax.ShapeDtypeStruct, dtype=jnp.float32)
    flat = pair_rep.reshape(ROWS * COLS, CH)
    with jax.named_scope("project"):
        sides = call(
            project_kernel,
            [VMEM, VMEM],
            bf16((CH, 2 * COLS, ROWS)),
            [pltpu.VMEM((CH * SIDES, ROWS), jnp.float32)],
            270_000_000,
            2 << 20,
        )(flat, pair_proj)
    with jax.named_scope("to_channels"):
        sides = lax.all_to_all(sides, PLANE, 0, 0, tiled=True)
    with jax.named_scope("right_values"):
        right = sides[:, :COLS]
    with jax.named_scope("right_across_x"):
        right_x = lax.ppermute(right, QUAD, [(d, d ^ 2) for d in range(4)])
    part = bf16((4, 2, 2, 4, 16, ROWS))
    with jax.named_scope("triangle_own"):
        keep, send = call(triangle_kernel, [VMEM] * 2, (part, part), (), 270_000_000, 2 << 20)(sides, right)
    with jax.named_scope("sums_to_core"):
        got = lax.ppermute(send, QUAD, [(d, d ^ 1) for d in range(4)])
    flat, keep = lax.optimization_barrier((flat, keep))
    with jax.named_scope("gate"):
        wide = f32((2, CH, HALF * ROWS))
        gate = call(
            gate_kernel,
            [VMEM] * 5,
            (wide, wide, bf16(out_proj.shape[::-1]), bf16(trans_in.shape[::-1]), bf16(trans_out.shape[::-1])),
            (),
            70_000_000,
            4 << 20,
        )(flat, gate_proj, out_proj, trans_in, trans_out)
    right_x, gate = lax.optimization_barrier((right_x, gate))
    with jax.named_scope("triangle_across"):
        keep_x, send_x = call(triangle_kernel, [VMEM] * 2, (part, part), (), 270_000_000, 2 << 20)(sides, right_x)
    with jax.named_scope("sums_to_core_across"):
        got_x = lax.ppermute(send_x, QUAD, [(d, d ^ 1) for d in range(4)])
    with jax.named_scope("add"):
        tri = call(add_kernel, [VMEM] * 4, bf16((4, 8, 4, 16, ROWS)), (), 1_000_000, 2 << 20)(keep, got, keep_x, got_x)
    with jax.named_scope("to_columns"):
        tri = lax.all_to_all(tri.reshape(CH, COLS, ROWS), PLANE, 0, 0, tiled=True)
    with jax.named_scope("finish"):
        xt, gating, proj_t, in_t, down_t = gate
        return call(
            finish_kernel,
            [VMEM] * 6,
            f32((ROWS, COLS, CH)),
            [pltpu.VMEM((CH, SUMS, ROWS), jnp.float32), HELD, pltpu.SemaphoreType.DMA((2,))],
            1_000_000_000,
            4 << 20,
            HBM,
        )(xt, gating, tri, proj_t, in_t, down_t)


def solution(mesh):
    fine = Mesh(mesh.devices.reshape(SIZES), AXES)
    spec = P(("xh", "xb", "zh"), ("y", "zl", "core"), None)
    return jax.shard_map(
        per_device, mesh=fine, in_specs=(spec, P(), P(), P(), P(), P()), out_specs=spec, check_vma=False
    )
```

time: 116 us -> 109 us (0.940)
  blocking collectives: 52.5 us -> 81.6 us
  waiting for transfers between devices: 24.5 us -> 3.99 us
  starting transfers between devices: 22 us -> 14.2 us
  Pallas kernels: 11.5 us -> 6.41 us
  local copies, waits for them, and re-layouts: 4.37 us -> 2.19 us
    all_to_all x0 -> x1, blocking collectives: none -> 29.2 us  [per_device(): tri = lax.all_to_all(tri.reshape(CH, COLS, ROWS), PLANE, 0, 0, tiled=True)]
    all_to_all x1 -> x0, waiting for transfers between devices: 19.8 us -> none  [per_device(): tri = lax.all_to_all(tri.reshape(CH, COLS, ROWS), PLANE, 0, 0, tiled=True)]
    all_to_all x1 -> x0, starting transfers between devices: 8 us -> none  [per_device(): tri = lax.all_to_all(tri.reshape(CH, COLS, ROWS), PLANE, 0, 0, tiled=True)]
    pallas_call x6, Pallas kernels: 11.5 us -> 6.41 us  [the longest x1 3.37 us: per_device(): call(finish_kernel, [VMEM] * 6, f32((ROWS, COLS, CH)), [pltpu.VMEM((CH, S...]
    unnamed x18 -> x12, local copies, waits for them, and re-layouts: 4.34 us -> 2.15 us
  transfers between devices with their start and end apart: 4 -> 3, of which waited for: 3 -> 2; matrix products, arithmetic and copies ran while one was open for 0% -> 0% of each run, Pallas kernels for 1% -> 2%
where the time goes in v3:
time: 109 us
  blocking collectives  81.6 us (75%)
  starting transfers between devices  14.2 us (13%)
  Pallas kernels  6.41 us (6%)
  waiting for transfers between devices  3.99 us (4%)
  local copies, waits for them, and re-layouts  2.19 us (2%)
    all_to_all x1, blocking collectives, per_device(): sides = lax.all_to_all(sides, PLANE, 0, 0, tiled=True)  52.5 us
    all_to_all x1, blocking collectives, per_device(): tri = lax.all_to_all(tri.reshape(CH, COLS, ROWS), PLANE, 0, 0, tiled=True)  29.2 us
    ppermute x1, starting transfers between devices, per_device(): got_x = lax.ppermute(send_x, QUAD, [(d, d ^ 1) for d in range(4)])  6.22 us
    ppermute x1, starting transfers between devices, per_device(): got = lax.ppermute(send, QUAD, [(d, d ^ 1) for d in range(4)])  5.59 us
    pallas_call x1, Pallas kernels, per_device(): call(finish_kernel, [VMEM] * 6, f32((ROWS, COLS, CH)), [pltpu.VMEM((CH, S...  3.37 us
    ppermute x1, waiting for transfers between devices, per_device(): right_x = lax.ppermute(right, QUAD, [(d, d ^ 2) for d in range(4)])  2.86 us
    ppermute x1, starting transfers between devices, per_device(): right_x = lax.ppermute(right, QUAD, [(d, d ^ 2) for d in range(4)])  2.34 us
  transfers between devices with their start and end apart: 3, of which 2 were waited for; matrix products, arithmetic and copies ran while one was open for 0% of the time, Pallas kernels for 2%

profile of v3, /device:TPU:1, one launch (start us, length us, event | category | flops | bytes accessed | tf_op | source)
XLA Modules:
  0.0 108.5 jit_solution(12519697175357405662)
XLA Ops:
  0.0 0.0 copy-start
  0.0 1.2 %copy-done = f32[128,16,128]{2,1,0:T(8,128)S(1)} copy-done((f32[128,16,128]{2,1,0:T(8,128)S(1)}, f32[128,16,128]{2,1,0:T(8,128)}, u32[]{:S(2)}) %copy-start) | copy-done | bytes 1048600
  1.2 0.0 copy-start.2
  1.2 0.9 copy-done.2
  2.1 1.3 %project.1 = bf16[128,32,128]{2,1,0:T(8,128)(2,1)S(1)} custom-call(f32[2048,128]{1,0:T(8,128)S(1)} %bitcast.2, bf16[128,512]{1,0:T(8,128)(2,1)S(1)} %copy-done.2), custom_call_target="tpu_custom_call" | custom-call | flops 270000000 | bytes 2097152 | tf_op jit(solution)/shard_map/project/pallas_call | solution.py:139
  3.4 52.5 %all_to_all.10.left_ref = bf16[128,32,128]{2,1,0:T(8,128)(2,1)S(1)} all-to-all(bf16[128,32,128]{2,1,0:T(8,128)(2,1)S(1)} %project.1), channel_id=1, replica_groups=mesh['xh'=2,'xb'=2,'zh'=2,'y'=8,'zl'=4,'core'=2] {'xh','zh','y','zl'}, dimensions={0} | all-to-all | bytes 2097152 | tf_op jit(solution)/shard_map/to_channels/all_to_all | solution.py:148
  55.9 0.0 copy-start.1
  55.9 0.0 copy-start.3
  55.9 0.0 copy-start.4
  55.9 0.0 copy-start.5
  55.9 2.3 %collective-permute-start = (bf16[128,16,128]{2,1,0:T(8,128)(2,1)S(1)}, bf16[128,16,128]{2,1,0:T(8,128)(2,1)S(1)}, u32[]{:S(2)}, u32[]{:S(2)}) collective-permute-start(bf16[128,16,128]{2,1,0:T(8,128)(2,1)S(1)} %slice.4.right_ref), channel_id=1, source_target_pairs={{0,128},{1,129},{128,0},{129,1},{2,130},{3,131},{130,2},{131,3},{4... | collective-permute-start | bytes 1572872 | tf_op jit(solution)/shard_map/right_across_x/ppermute | solution.py:152
  58.3 0.5 triangle_own.1
  58.8 5.6 %collective-permute-start.1 = (bf16[4,2,2,4,16,128]{5,4,3,2,1,0:T(8,128)(2,1)S(1)}, bf16[4,2,2,4,16,128]{5,4,3,2,1,0:T(8,128)(2,1)S(1)}, u32[]{:S(2)}, u32[]{:S(2)}) collective-permute-start(bf16[4,2,2,4,16,128]{5,4,3,2,1,0:T(8,128)(2,1)S(1)} %get-tuple-element.32), channel_id=1, source_target_pairs={{0,1},{1,0},{128,129},{129,128},{2,3},{3,2},{130,131},{131,130},{4... | collective-permute-start | bytes 786440 | tf_op jit(solution)/shard_map/sums_to_core/ppermute | solution.py:157
  64.4 0.0 copy-done.1
  64.4 0.0 copy-done.3
  64.4 0.0 copy-done.4
  64.4 0.0 copy-done.5
  64.4 0.7 gate.1
  65.1 2.9 %collective-permute-done.right_ref = bf16[128,16,128]{2,1,0:T(8,128)(2,1)S(1)} collective-permute-done((bf16[128,16,128]{2,1,0:T(8,128)(2,1)S(1)}, bf16[128,16,128]{2,1,0:T(8,128)(2,1)S(1)}, u32[]{:S(2)}, u32[]{:S(2)}) %collective-permute-start) | collective-permute-done | bytes 524320 | tf_op jit(solution)/shard_map/right_across_x/ppermute | solution.py:152
  68.0 0.5 triangle_across.1
  68.5 6.2 %collective-permute-start.2 = (bf16[4,2,2,4,16,128]{5,4,3,2,1,0:T(8,128)(2,1)S(1)}, bf16[4,2,2,4,16,128]{5,4,3,2,1,0:T(8,128)(2,1)S(1)}, u32[]{:S(2)}, u32[]{:S(2)}) collective-permute-start(bf16[4,2,2,4,16,128]{5,4,3,2,1,0:T(8,128)(2,1)S(1)} %get-tuple-element.35), channel_id=1, source_target_pairs={{0,1},{1,0},{128,129},{129,128},{2,3},{3,2},{130,131},{131,130},{4... | collective-permute-start | bytes 786440 | tf_op jit(solution)/shard_map/sums_to_core_across/ppermute | solution.py:173
  74.7 0.0 collective-permute-done.1.got_ref
  74.7 1.1 %collective-permute-done.2.got_x_ref = bf16[4,2,2,4,16,128]{5,4,3,2,1,0:T(8,128)(2,1)S(1)} collective-permute-done((bf16[4,2,2,4,16,128]{5,4,3,2,1,0:T(8,128)(2,1)S(1)}, bf16[4,2,2,4,16,128]{5,4,3,2,1,0:T(8,128)(2,1)S(1)}, u32[]{:S(2)}, u32[]{:S(2)}) %collective-permute-start.2) | collective-permute-done | bytes 262176 | tf_op jit(solution)/shard_map/sums_to_core_across/ppermute | solution.py:173
  75.8 0.1 add.1
  76.0 29.2 %all_to_all.11.t_ref = bf16[128,16,128]{2,1,0:T(8,128)(2,1)S(1)} all-to-all(bf16[128,16,128]{2,1,0:T(8,128)(2,1)S(1)} %bitcast.4), channel_id=1, replica_groups=mesh['xh'=2,'xb'=2,'zh'=2,'y'=8,'zl'=4,'core'=2] {'xh','zh','y','zl'}, dimensions={0} | all-to-all | bytes 1048576 | tf_op jit(solution)/shard_map/to_columns/all_to_all | solution.py:177
  105.2 3.4 %finish.1 = f32[128,16,128]{2,1,0:T(8,128)} custom-call(f32[2,128,1024]{2,1,0:T(8,128)S(1)} %get-tuple-element.29.xt_ref, f32[2,128,1024]{2,1,0:T(8,128)S(1)} %get-tuple-element.30.gating_ref, bf16[128,16,128]{2,1,0:T(8,128)(2,1)S(1)} %all_to_all.11.t_ref, bf16[128,128]{1,0:T(8,128)(2,1)S(1)} %get-tuple-element.36.proj_ref, ...), custom_call_target="tpu_custom_call" | custom-call | flops 1000000000 | bytes 4194304 | tf_op jit(solution)/shard_map/finish/pallas_call | solution.py:180
  (1 shorter events, 0.0 us)
Async XLA Ops:
  0.0 1.2 %copy-start = (f32[128,16,128]{2,1,0:T(8,128)S(1)}, f32[128,16,128]{2,1,0:T(8,128)}, u32[]{:S(2)}) copy-start(f32[128,16,128]{2,1,0:T(8,128)} %param.6) | copy-start | bytes 3145732
  1.2 0.9 copy-start.2
  55.9 8.5 %copy-start.1 = (bf16[128,1024]{1,0:T(8,128)(2,1)S(1)}, bf16[128,1024]{1,0:T(8,128)(2,1)}, u32[]{:S(2)}) copy-start(bf16[128,1024]{1,0:T(8,128)(2,1)} %in_ref.1) | copy-start | bytes 786436
  55.9 8.5 %copy-start.3 = (bf16[512,128]{1,0:T(8,128)(2,1)S(1)}, bf16[512,128]{1,0:T(8,128)(2,1)}, u32[]{:S(2)}) copy-start(bf16[512,128]{1,0:T(8,128)(2,1)} %down_ref.1) | copy-start | bytes 393220
  55.9 8.5 %copy-start.4 = (bf16[128,128]{1,0:T(8,128)(2,1)S(1)}, bf16[128,128]{1,0:T(8,128)(2,1)}, u32[]{:S(2)}) copy-start(bf16[128,128]{1,0:T(8,128)(2,1)} %gate_ref.1) | copy-start | bytes 98308
  55.9 8.5 %copy-start.5 = (bf16[128,128]{1,0:T(8,128)(2,1)S(1)}, bf16[128,128]{1,0:T(8,128)(2,1)}, u32[]{:S(2)}) copy-start(bf16[128,128]{1,0:T(8,128)(2,1)} %proj_ref.1) | copy-start | bytes 98308
  55.9 12.0 %collective-permute-start = (bf16[128,16,128]{2,1,0:T(8,128)(2,1)S(1)}, bf16[128,16,128]{2,1,0:T(8,128)(2,1)S(1)}, u32[]{:S(2)}, u32[]{:S(2)}) collective-permute-start(bf16[128,16,128]{2,1,0:T(8,128)(2,1)S(1)} %slice.4.right_ref), channel_id=1, source_target_pairs={{0,128},{1,129},{128,0},{129,1},{2,130},{3,131},{130,2},{131,3},{4... | collective-permute-start | bytes 1572872 | tf_op jit(solution)/shard_map/right_across_x/ppermute | solution.py:152
  58.8 15.9 %collective-permute-start.1 = (bf16[4,2,2,4,16,128]{5,4,3,2,1,0:T(8,128)(2,1)S(1)}, bf16[4,2,2,4,16,128]{5,4,3,2,1,0:T(8,128)(2,1)S(1)}, u32[]{:S(2)}, u32[]{:S(2)}) collective-permute-start(bf16[4,2,2,4,16,128]{5,4,3,2,1,0:T(8,128)(2,1)S(1)} %get-tuple-element.32), channel_id=1, source_target_pairs={{0,1},{1,0},{128,129},{129,128},{2,3},{3,2},{130,131},{131,130},{4... | collective-permute-start | bytes 786440 | tf_op jit(solution)/shard_map/sums_to_core/ppermute | solution.py:157
  68.5 7.4 %collective-permute-start.2 = (bf16[4,2,2,4,16,128]{5,4,3,2,1,0:T(8,128)(2,1)S(1)}, bf16[4,2,2,4,16,128]{5,4,3,2,1,0:T(8,128)(2,1)S(1)}, u32[]{:S(2)}, u32[]{:S(2)}) collective-permute-start(bf16[4,2,2,4,16,128]{5,4,3,2,1,0:T(8,128)(2,1)S(1)} %get-tuple-element.35), channel_id=1, source_target_pairs={{0,1},{1,0},{128,129},{129,128},{2,3},{3,2},{130,131},{131,130},{4... | collective-permute-start | bytes 786440 | tf_op jit(solution)/shard_map/sums_to_core_across/ppermute | solution.py:173

commit v4 on v3

--- a/solution.py
+++ b/solution.py
@@ -10,8 +10,9 @@
 
 AXES = ("xh", "xb", "zh", "y", "zl", "core")
 SIZES = (2, 2, 2, 8, 4, 2)
-PLANE = ("xh", "zh", "y", "zl")
-QUAD = ("xb", "core")
+PLANE = ("y", "zh", "zl", "xb")
+GROUP = (8, 2, 4, 2)
+SHARE = ("xh", "xb", "core")
 ROWS = 128
 COLS = 16
 CH = 128
@@ -48,7 +49,10 @@
             product = sigmoid(p[at : at + CH]) * p[at + CH : at + 2 * CH]
             for s in range(HALF):
                 stage[pl.ds(base + HALF * h + s, CH, stride=SIDES), :] = product[:, s * ROWS : (s + 1) * ROWS]
-    out_ref[...] = stage[...].reshape(CH, SIDES, ROWS)[:, : 2 * COLS].astype(jnp.bfloat16)
+    xh = lax.axis_index("xh")
+    for b in range(2):
+        rows = stage[64 * SIDES * b : 64 * SIDES * (b + 1)].reshape(64, SIDES, ROWS)[:, : 2 * COLS]
+        out_ref[:, jnp.bitwise_xor(xh, b)] = rows.astype(jnp.bfloat16)
 
 
 def gate_kernel(x_ref, gate_ref, proj_ref, in_ref, down_ref, xt_ref, gating_ref, proj_t_ref, in_t_ref, down_t_ref):
@@ -64,34 +68,35 @@
 
 def triangle_kernel(left_ref, right_ref, keep_ref, send_ref):
     core = lax.axis_index("core")
+    left = left_ref[...].reshape(*GROUP, 2 * COLS, ROWS)
     left = jnp.concatenate(
-        [left_ref[32 * g : 32 * g + 32, COLS:, :].reshape(32 * COLS, ROWS) for g in range(4)], axis=1
+        [left[:, zh, :, x, COLS:].reshape(32 * COLS, ROWS) for zh in range(2) for x in range(2)], axis=1
     )
-    for xh in range(2):
-        right = jnp.concatenate(
-            [right_ref[64 * xh + 32 * zh : 64 * xh + 32 * zh + 32].reshape(32 * COLS, ROWS) for zh in range(2)], axis=1
-        )
-        part = lax.dot_general(right, left, (((0,), (0,)), ((), ())), preferred_element_type=jnp.float32)
+    right = right_ref[...].reshape(*GROUP, COLS, ROWS)
+    for xj in range(2):
+        rows = jnp.concatenate([right[:, zj, :, xj].reshape(32 * COLS, ROWS) for zj in range(2)], axis=1)
+        part = lax.dot_general(rows, left, (((0,), (0,)), ((), ())), preferred_element_type=jnp.float32)
         part = part.astype(jnp.bfloat16).reshape(2, 4, 2, 16, 4 * ROWS)
         first, second = part[:, :, 0], part[:, :, 1]
         keep = jnp.where(core == 0, first, second)
         send = jnp.where(core == 0, second, first)
-        for g in range(4):
-            keep_ref[g, xh] = keep[..., g * ROWS : (g + 1) * ROWS]
-            send_ref[g, xh] = send[..., g * ROWS : (g + 1) * ROWS]
+        for zh in range(2):
+            for x in range(2):
+                at = slice((2 * zh + x) * ROWS, (2 * zh + x + 1) * ROWS)
+                keep_ref[2 * xj : 2 * xj + 2, zh, :, x] = keep[..., at]
+                send_ref[2 * xj : 2 * xj + 2, zh, :, x] = send[..., at]
 
 
 def add_kernel(keep_ref, got_ref, keep_x_ref, got_x_ref, out_ref):
-    xb = lax.axis_index("xb")
-    for a, b, at in ((keep_ref, got_ref, xb), (keep_x_ref, got_x_ref, 1 - xb)):
-        for xh in range(2):
-            for zh in range(2):
-                total = a[:, xh, zh].astype(jnp.float32) + b[:, xh, zh].astype(jnp.float32)
-                out_ref[:, 4 * xh + 2 * at + zh] = total.astype(jnp.bfloat16)
+    xh = lax.axis_index("xh")
+    for a, b, at in ((keep_ref, got_ref, xh), (keep_x_ref, got_x_ref, 1 - xh)):
+        out_ref[at] = (a[...].astype(jnp.float32) + b[...].astype(jnp.float32)).astype(jnp.bfloat16)
 
 
 def finish_kernel(xt_ref, gating_ref, t_ref, proj_ref, in_ref, down_ref, out_hbm, stage, held, sems):
-    stage[:, :COLS] = t_ref[...].astype(jnp.float32)
+    xh = lax.axis_index("xh")
+    for b in range(2):
+        stage[64 * b : 64 * b + 64, :COLS] = t_ref[:, jnp.bitwise_xor(xh, b)].astype(jnp.float32)
     rows = stage.reshape(CH * SUMS, ROWS)
     hidden = down_ref.shape[1]
     copies = []
@@ -139,22 +144,22 @@
         sides = call(
             project_kernel,
             [VMEM, VMEM],
-            bf16((CH, 2 * COLS, ROWS)),
+            bf16((CH // 2, 2, 2 * COLS, ROWS)),
             [pltpu.VMEM((CH * SIDES, ROWS), jnp.float32)],
             270_000_000,
             2 << 20,
         )(flat, pair_proj)
     with jax.named_scope("to_channels"):
-        sides = lax.all_to_all(sides, PLANE, 0, 0, tiled=True)
+        sides = lax.all_to_all(sides.reshape(CH, 2 * COLS, ROWS), PLANE, 0, 0, tiled=True)
     with jax.named_scope("right_values"):
         right = sides[:, :COLS]
     with jax.named_scope("right_across_x"):
-        right_x = lax.ppermute(right, QUAD, [(d, d ^ 2) for d in range(4)])
-    part = bf16((4, 2, 2, 4, 16, ROWS))
+        right_x = lax.ppermute(right, SHARE, [(d, d ^ 6) for d in range(8)])
+    part = bf16((4, 2, 4, 2, COLS, ROWS))
     with jax.named_scope("triangle_own"):
         keep, send = call(triangle_kernel, [VMEM] * 2, (part, part), (), 270_000_000, 2 << 20)(sides, right)
     with jax.named_scope("sums_to_core"):
-        got = lax.ppermute(send, QUAD, [(d, d ^ 1) for d in range(4)])
+        got = lax.ppermute(send, SHARE, [(d, d ^ 1) for d in range(8)])
     flat, keep = lax.optimization_barrier((flat, keep))
     with jax.named_scope("gate"):
         wide = f32((2, CH, HALF * ROWS))
@@ -170,9 +175,9 @@
     with jax.named_scope("triangle_across"):
         keep_x, send_x = call(triangle_kernel, [VMEM] * 2, (part, part), (), 270_000_000, 2 << 20)(sides, right_x)
     with jax.named_scope("sums_to_core_across"):
-        got_x = lax.ppermute(send_x, QUAD, [(d, d ^ 1) for d in range(4)])
+        got_x = lax.ppermute(send_x, SHARE, [(d, d ^ 1) for d in range(8)])
     with jax.named_scope("add"):
-        tri = call(add_kernel, [VMEM] * 4, bf16((4, 8, 4, 16, ROWS)), (), 1_000_000, 2 << 20)(keep, got, keep_x, got_x)
+        tri = call(add_kernel, [VMEM] * 4, bf16((2, 4, 2, 4, 2, COLS, ROWS)), (), 1_000_000, 2 << 20)(keep, got, keep_x, got_x)
     with jax.named_scope("to_columns"):
         tri = lax.all_to_all(tri.reshape(CH, COLS, ROWS), PLANE, 0, 0, tiled=True)
     with jax.named_scope("finish"):
@@ -185,7 +190,7 @@
             1_000_000_000,
             4 << 20,
             HBM,
-        )(xt, gating, tri, proj_t, in_t, down_t)
+        )(xt, gating, tri.reshape(CH // 2, 2, COLS, ROWS), proj_t, in_t, down_t)
 
 
 def solution(mesh):

time: 109 us -> 104 us (0.954); the launches traced: 109 us -> 102 us
  blocking collectives: 81.6 us -> 73.6 us
  starting transfers between devices: 14.2 us -> 16 us
    all_to_all x1, blocking collectives: 52.5 us -> 47.1 us  [per_device(): lax.all_to_all(sides.reshape(CH, 2 * COLS, ROWS), PLANE, 0, 0, tiled=True)]
    all_to_all x1, blocking collectives: 29.2 us -> 26.6 us  [per_device(): tri = lax.all_to_all(tri.reshape(CH, COLS, ROWS), PLANE, 0, 0, tiled=True)]
    ppermute x3, starting transfers between devices: 14.2 us -> 16 us  [the longest x1 6.08 us: per_device(): got_x = lax.ppermute(send_x, SHARE, [(d, d ^ 1) for d in range(8)])]
where the time goes in v4:
time: 104 us; the launch traced here: 102 us
  blocking collectives  73.6 us (71%)
  starting transfers between devices  16 us (15%)
  Pallas kernels  6.48 us (6%)
  waiting for transfers between devices  3.35 us (3%)
  local copies, waits for them, and re-layouts  2.19 us (2%)
    all_to_all x1, blocking collectives, per_device(): lax.all_to_all(sides.reshape(CH, 2 * COLS, ROWS), PLANE, 0, 0, tiled=True)  47.1 us
    all_to_all x1, blocking collectives, per_device(): tri = lax.all_to_all(tri.reshape(CH, COLS, ROWS), PLANE, 0, 0, tiled=True)  26.6 us
    ppermute x1, starting transfers between devices, per_device(): got_x = lax.ppermute(send_x, SHARE, [(d, d ^ 1) for d in range(8)])  6.08 us
    ppermute x1, starting transfers between devices, per_device(): got = lax.ppermute(send, SHARE, [(d, d ^ 1) for d in range(8)])  5.65 us
    ppermute x1, starting transfers between devices, per_device(): right_x = lax.ppermute(right, SHARE, [(d, d ^ 6) for d in range(8)])  4.28 us
    pallas_call x1, Pallas kernels, per_device(): call(finish_kernel, [VMEM] * 6, f32((ROWS, COLS, CH)), [pltpu.VMEM((CH, S...  3.37 us
    ppermute x1, waiting for transfers between devices, per_device(): right_x = lax.ppermute(right, SHARE, [(d, d ^ 6) for d in range(8)])  2.22 us
    unnamed x12, local copies, waits for them, and re-layouts  2.15 us
  transfers between devices with their start and end apart: 3, of which 2 were waited for; matrix products, arithmetic and copies ran while one was open for 0% of the time, Pallas kernels for 2%

profile of v4, /device:TPU:1, one launch (start us, length us, event | category | flops | bytes accessed | tf_op | source)
XLA Modules:
  0.0 101.8 jit_solution(17773925054821688329)
XLA Ops:
  0.0 0.0 copy-start
  0.0 1.2 %copy-done = f32[128,16,128]{2,1,0:T(8,128)S(1)} copy-done((f32[128,16,128]{2,1,0:T(8,128)S(1)}, f32[128,16,128]{2,1,0:T(8,128)}, u32[]{:S(2)}) %copy-start) | copy-done | bytes 1048600
  1.2 0.0 copy-start.2
  1.2 0.9 copy-done.2
  2.1 1.3 %project.1 = bf16[64,2,32,128]{3,2,1,0:T(8,128)(2,1)S(1)} custom-call(f32[2048,128]{1,0:T(8,128)S(1)} %bitcast.4, bf16[128,512]{1,0:T(8,128)(2,1)S(1)} %copy-done.2), custom_call_target="tpu_custom_call" | custom-call | flops 270000000 | bytes 2097152 | tf_op jit(solution)/shard_map/project/pallas_call | solution.py:144
  3.5 47.1 %all_to_all.10.left_ref = bf16[128,32,128]{2,1,0:T(8,128)(2,1)S(1)} all-to-all(bf16[128,32,128]{2,1,0:T(8,128)(2,1)S(1)} %bitcast.6), channel_id=1, replica_groups=mesh['xh'=2,'xb'=2,'zh'=2,'y'=8,'zl'=4,'core'=2] {'y','zh','zl','xb'}, dimensions={0} | all-to-all | bytes 2097152 | tf_op jit(solution)/shard_map/to_channels/all_to_all | solution.py:153
  50.6 0.0 copy-start.1
  50.6 0.0 copy-start.3
  50.6 0.0 copy-start.4
  50.6 0.0 copy-start.5
  50.6 4.3 %collective-permute-start = (bf16[128,16,128]{2,1,0:T(8,128)(2,1)S(1)}, bf16[128,16,128]{2,1,0:T(8,128)(2,1)S(1)}, u32[]{:S(2)}, u32[]{:S(2)}) collective-permute-start(bf16[128,16,128]{2,1,0:T(8,128)(2,1)S(1)} %slice.4.right_ref), channel_id=1, source_target_pairs={{0,384},{1,385},{128,256},{129,257},{256,128},{257,129},{384,0},{3... | collective-permute-start | bytes 1572872 | tf_op jit(solution)/shard_map/right_across_x/ppermute | solution.py:157
  54.9 0.5 triangle_own.1
  55.4 5.7 %collective-permute-start.1 = (bf16[4,2,4,2,16,128]{5,4,3,2,1,0:T(8,128)(2,1)S(1)}, bf16[4,2,4,2,16,128]{5,4,3,2,1,0:T(8,128)(2,1)S(1)}, u32[]{:S(2)}, u32[]{:S(2)}) collective-permute-start(bf16[4,2,4,2,16,128]{5,4,3,2,1,0:T(8,128)(2,1)S(1)} %get-tuple-element.32), channel_id=1, source_target_pairs={{0,1},{1,0},{128,129},{129,128},{256,257},{257,256},{384,385},{385... | collective-permute-start | bytes 786440 | tf_op jit(solution)/shard_map/sums_to_core/ppermute | solution.py:162
  61.1 0.0 copy-done.1
  61.1 0.0 copy-done.3
  61.1 0.0 copy-done.4
  61.1 0.0 copy-done.5
  61.1 0.7 gate.1
  61.8 2.2 %collective-permute-done.right_ref = bf16[128,16,128]{2,1,0:T(8,128)(2,1)S(1)} collective-permute-done((bf16[128,16,128]{2,1,0:T(8,128)(2,1)S(1)}, bf16[128,16,128]{2,1,0:T(8,128)(2,1)S(1)}, u32[]{:S(2)}, u32[]{:S(2)}) %collective-permute-start) | collective-permute-done | bytes 524320 | tf_op jit(solution)/shard_map/right_across_x/ppermute | solution.py:157
  64.0 0.5 triangle_across.1
  64.5 6.1 %collective-permute-start.2 = (bf16[4,2,4,2,16,128]{5,4,3,2,1,0:T(8,128)(2,1)S(1)}, bf16[4,2,4,2,16,128]{5,4,3,2,1,0:T(8,128)(2,1)S(1)}, u32[]{:S(2)}, u32[]{:S(2)}) collective-permute-start(bf16[4,2,4,2,16,128]{5,4,3,2,1,0:T(8,128)(2,1)S(1)} %get-tuple-element.35), channel_id=1, source_target_pairs={{0,1},{1,0},{128,129},{129,128},{256,257},{257,256},{384,385},{385... | collective-permute-start | bytes 786440 | tf_op jit(solution)/shard_map/sums_to_core_across/ppermute | solution.py:178
  70.6 0.0 collective-permute-done.1.got_ref
  70.6 1.1 %collective-permute-done.2.got_x_ref = bf16[4,2,4,2,16,128]{5,4,3,2,1,0:T(8,128)(2,1)S(1)} collective-permute-done((bf16[4,2,4,2,16,128]{5,4,3,2,1,0:T(8,128)(2,1)S(1)}, bf16[4,2,4,2,16,128]{5,4,3,2,1,0:T(8,128)(2,1)S(1)}, u32[]{:S(2)}, u32[]{:S(2)}) %collective-permute-start.2) | collective-permute-done | bytes 262176 | tf_op jit(solution)/shard_map/sums_to_core_across/ppermute | solution.py:178
  71.7 0.1 add.1
  71.9 26.6 %all_to_all.11 = bf16[128,16,128]{2,1,0:T(8,128)(2,1)S(1)} all-to-all(bf16[128,16,128]{2,1,0:T(8,128)(2,1)S(1)} %bitcast.7), channel_id=1, replica_groups=mesh['xh'=2,'xb'=2,'zh'=2,'y'=8,'zl'=4,'core'=2] {'y','zh','zl','xb'}, dimensions={0} | all-to-all | bytes 1048576 | tf_op jit(solution)/shard_map/to_columns/all_to_all | solution.py:182
  98.4 3.4 %finish.1 = f32[128,16,128]{2,1,0:T(8,128)} custom-call(f32[2,128,1024]{2,1,0:T(8,128)S(1)} %get-tuple-element.29.xt_ref, f32[2,128,1024]{2,1,0:T(8,128)S(1)} %get-tuple-element.30.gating_ref, bf16[64,2,16,128]{3,2,1,0:T(8,128)(2,1)S(1)} %bitcast.8, bf16[128,128]{1,0:T(8,128)(2,1)S(1)} %get-tuple-element.36.proj_ref, ...), custom_call_target="tpu_custom_call" | custom-call | flops 1000000000 | bytes 4194304 | tf_op jit(solution)/shard_map/finish/pallas_call | solution.py:185
  (1 shorter events, 0.0 us)
Async XLA Ops:
  0.0 1.2 %copy-start = (f32[128,16,128]{2,1,0:T(8,128)S(1)}, f32[128,16,128]{2,1,0:T(8,128)}, u32[]{:S(2)}) copy-start(f32[128,16,128]{2,1,0:T(8,128)} %param.6) | copy-start | bytes 3145732
  1.2 0.9 copy-start.2
  50.6 10.5 %copy-start.1 = (bf16[128,1024]{1,0:T(8,128)(2,1)S(1)}, bf16[128,1024]{1,0:T(8,128)(2,1)}, u32[]{:S(2)}) copy-start(bf16[128,1024]{1,0:T(8,128)(2,1)} %in_ref.1) | copy-start | bytes 786436
  50.6 10.5 %copy-start.3 = (bf16[512,128]{1,0:T(8,128)(2,1)S(1)}, bf16[512,128]{1,0:T(8,128)(2,1)}, u32[]{:S(2)}) copy-start(bf16[512,128]{1,0:T(8,128)(2,1)} %down_ref.1) | copy-start | bytes 393220
  50.6 10.5 %copy-start.4 = (bf16[128,128]{1,0:T(8,128)(2,1)S(1)}, bf16[128,128]{1,0:T(8,128)(2,1)}, u32[]{:S(2)}) copy-start(bf16[128,128]{1,0:T(8,128)(2,1)} %gate_ref.1) | copy-start | bytes 98308
  50.6 10.5 %copy-start.5 = (bf16[128,128]{1,0:T(8,128)(2,1)S(1)}, bf16[128,128]{1,0:T(8,128)(2,1)}, u32[]{:S(2)}) copy-start(bf16[128,128]{1,0:T(8,128)(2,1)} %proj_ref.1) | copy-start | bytes 98308
  50.6 13.4 %collective-permute-start = (bf16[128,16,128]{2,1,0:T(8,128)(2,1)S(1)}, bf16[128,16,128]{2,1,0:T(8,128)(2,1)S(1)}, u32[]{:S(2)}, u32[]{:S(2)}) collective-permute-start(bf16[128,16,128]{2,1,0:T(8,128)(2,1)S(1)} %slice.4.right_ref), channel_id=1, source_target_pairs={{0,384},{1,385},{128,256},{129,257},{256,128},{257,129},{384,0},{3... | collective-permute-start | bytes 1572872 | tf_op jit(solution)/shard_map/right_across_x/ppermute | solution.py:157
  55.4 15.2 %collective-permute-start.1 = (bf16[4,2,4,2,16,128]{5,4,3,2,1,0:T(8,128)(2,1)S(1)}, bf16[4,2,4,2,16,128]{5,4,3,2,1,0:T(8,128)(2,1)S(1)}, u32[]{:S(2)}, u32[]{:S(2)}) collective-permute-start(bf16[4,2,4,2,16,128]{5,4,3,2,1,0:T(8,128)(2,1)S(1)} %get-tuple-element.32), channel_id=1, source_target_pairs={{0,1},{1,0},{128,129},{129,128},{256,257},{257,256},{384,385},{385... | collective-permute-start | bytes 786440 | tf_op jit(solution)/shard_map/sums_to_core/ppermute | solution.py:162
  64.5 7.2 %collective-permute-start.2 = (bf16[4,2,4,2,16,128]{5,4,3,2,1,0:T(8,128)(2,1)S(1)}, bf16[4,2,4,2,16,128]{5,4,3,2,1,0:T(8,128)(2,1)S(1)}, u32[]{:S(2)}, u32[]{:S(2)}) collective-permute-start(bf16[4,2,4,2,16,128]{5,4,3,2,1,0:T(8,128)(2,1)S(1)} %get-tuple-element.35), channel_id=1, source_target_pairs={{0,1},{1,0},{128,129},{129,128},{256,257},{257,256},{384,385},{385... | collective-permute-start | bytes 786440 | tf_op jit(solution)/shard_map/sums_to_core_across/ppermute | solution.py:178

commit v5 on v4

--- a/solution.py
+++ b/solution.py
@@ -1,4 +1,5 @@
 import functools
+import itertools
 
 import jax
 import jax.numpy as jnp
@@ -8,15 +9,14 @@
 from jax.sharding import Mesh
 from jax.sharding import PartitionSpec as P
 
-AXES = ("xh", "xb", "zh", "y", "zl", "core")
-SIZES = (2, 2, 2, 8, 4, 2)
-PLANE = ("y", "zh", "zl", "xb")
-GROUP = (8, 2, 4, 2)
+AXES = ("xh", "xb", "zh", "y2", "y1", "y0", "zl1", "zl0", "core")
+PLANE = ("xb", "y0", "zl0", "y1", "zl1", "y2", "zh")
 SHARE = ("xh", "xb", "core")
 ROWS = 128
 COLS = 16
 CH = 128
 HALF = COLS // 2
+QUARTER = HALF // 2
 SIDES = 2 * COLS + 8
 SUMS = COLS + 8
 EPS = 1e-05
@@ -41,10 +41,15 @@
     return jnp.concatenate([ref[pl.ds(HALF * h + s, ROWS, stride=COLS), :].T for s in range(HALF)], axis=1)
 
 
-def project_kernel(x_ref, w_ref, out_ref, stage):
+def norm_kernel(x_ref, normed_ref):
+    for h in range(2):
+        normed_ref[h] = norm_rows(half_columns(x_ref, h))
+
+
+def project_kernel(normed_ref, w_ref, out_ref, stage):
     weights = w_ref[...].T
     for h in range(2):
-        p = dot(weights, norm_rows(half_columns(x_ref, h)))
+        p = dot(weights, normed_ref[h])
         for base, at in ((COLS, 0), (0, 2 * CH)):
             product = sigmoid(p[at : at + CH]) * p[at + CH : at + 2 * CH]
             for s in range(HALF):
@@ -52,7 +57,7 @@
     xh = lax.axis_index("xh")
     for b in range(2):
         rows = stage[64 * SIDES * b : 64 * SIDES * (b + 1)].reshape(64, SIDES, ROWS)[:, : 2 * COLS]
-        out_ref[:, jnp.bitwise_xor(xh, b)] = rows.astype(jnp.bfloat16)
+        out_ref[jnp.bitwise_xor(xh, b)] = rows.astype(jnp.bfloat16)
 
 
 def gate_kernel(x_ref, gate_ref, proj_ref, in_ref, down_ref, xt_ref, gating_ref, proj_t_ref, in_t_ref, down_t_ref):
@@ -68,35 +73,35 @@
 
 def triangle_kernel(left_ref, right_ref, keep_ref, send_ref):
     core = lax.axis_index("core")
-    left = left_ref[...].reshape(*GROUP, 2 * COLS, ROWS)
+    left = left_ref[...].reshape(2, 32, 2, 2 * COLS, ROWS)
     left = jnp.concatenate(
-        [left[:, zh, :, x, COLS:].reshape(32 * COLS, ROWS) for zh in range(2) for x in range(2)], axis=1
+        [left[x, :, zh, COLS:].reshape(32 * COLS, ROWS) for zh in range(2) for x in range(2)], axis=1
     )
-    right = right_ref[...].reshape(*GROUP, COLS, ROWS)
+    right = right_ref[...].reshape(2, 32, 2, COLS, ROWS)
     for xj in range(2):
-        rows = jnp.concatenate([right[:, zj, :, xj].reshape(32 * COLS, ROWS) for zj in range(2)], axis=1)
+        rows = jnp.concatenate([right[xj, :, zj].reshape(32 * COLS, ROWS) for zj in range(2)], axis=1)
         part = lax.dot_general(rows, left, (((0,), (0,)), ((), ())), preferred_element_type=jnp.float32)
         part = part.astype(jnp.bfloat16).reshape(2, 4, 2, 16, 4 * ROWS)
         first, second = part[:, :, 0], part[:, :, 1]
         keep = jnp.where(core == 0, first, second)
         send = jnp.where(core == 0, second, first)
-        for zh in range(2):
-            for x in range(2):
-                at = slice((2 * zh + x) * ROWS, (2 * zh + x + 1) * ROWS)
-                keep_ref[2 * xj : 2 * xj + 2, zh, :, x] = keep[..., at]
-                send_ref[2 * xj : 2 * xj + 2, zh, :, x] = send[..., at]
+        for x, zj, z0, z1, zh in itertools.product(range(2), repeat=5):
+            at = slice((2 * zh + x) * ROWS, (2 * zh + x + 1) * ROWS)
+            to = 16 * x + 8 * zj + 4 * z0 + 2 * xj + z1
+            keep_ref[to, zh] = keep[zj, 2 * z1 + z0, :, at]
+            send_ref[to, zh] = send[zj, 2 * z1 + z0, :, at]
 
 
 def add_kernel(keep_ref, got_ref, keep_x_ref, got_x_ref, out_ref):
     xh = lax.axis_index("xh")
     for a, b, at in ((keep_ref, got_ref, xh), (keep_x_ref, got_x_ref, 1 - xh)):
-        out_ref[at] = (a[...].astype(jnp.float32) + b[...].astype(jnp.float32)).astype(jnp.bfloat16)
+        out_ref[:, at] = (a[...].astype(jnp.float32) + b[...].astype(jnp.float32)).astype(jnp.bfloat16)
 
 
 def finish_kernel(xt_ref, gating_ref, t_ref, proj_ref, in_ref, down_ref, out_hbm, stage, held, sems):
     xh = lax.axis_index("xh")
     for b in range(2):
-        stage[64 * b : 64 * b + 64, :COLS] = t_ref[:, jnp.bitwise_xor(xh, b)].astype(jnp.float32)
+        stage[64 * b : 64 * b + 64, :COLS] = t_ref[jnp.bitwise_xor(xh, b)].astype(jnp.float32)
     rows = stage.reshape(CH * SUMS, ROWS)
     hidden = down_ref.shape[1]
     copies = []
@@ -107,13 +112,17 @@
         up = t[:hidden]
         units = (up * sigmoid(up) * t[hidden:]).astype(jnp.bfloat16)
         result = middle + dot(down_ref[...], units)
-        for s in range(HALF):
-            held.at[h][pl.ds(s, ROWS, stride=HALF), :] = result[:, s * ROWS : (s + 1) * ROWS].T
-        copy = pltpu.make_async_copy(
-            held.at[h].reshape(ROWS, HALF, CH), out_hbm.at[:, pl.ds(HALF * h, HALF), :], sems.at[h]
-        )
-        copy.start()
-        copies.append(copy)
+        for q in range(2):
+            for s in range(QUARTER):
+                c = QUARTER * q + s
+                held.at[h][pl.ds(c, ROWS, stride=HALF), :] = result[:, c * ROWS : (c + 1) * ROWS].T
+            copy = pltpu.make_async_copy(
+                held.at[h].reshape(ROWS, HALF, CH).at[:, pl.ds(QUARTER * q, QUARTER), :],
+                out_hbm.at[:, pl.ds(HALF * h + QUARTER * q, QUARTER), :],
+                sems.at[2 * h + q],
+            )
+            copy.start()
+            copies.append(copy)
     for copy in copies:
         copy.wait()
 
@@ -140,22 +149,24 @@
     bf16 = functools.partial(jax.ShapeDtypeStruct, dtype=jnp.bfloat16)
     f32 = functools.partial(jax.ShapeDtypeStruct, dtype=jnp.float32)
     flat = pair_rep.reshape(ROWS * COLS, CH)
+    with jax.named_scope("norm"):
+        normed = call(norm_kernel, [VMEM], bf16((2, CH, HALF * ROWS)), (), 2_000_000, 2 << 20)(flat)
     with jax.named_scope("project"):
         sides = call(
             project_kernel,
             [VMEM, VMEM],
-            bf16((CH // 2, 2, 2 * COLS, ROWS)),
+            bf16((2, CH // 2, 2 * COLS, ROWS)),
             [pltpu.VMEM((CH * SIDES, ROWS), jnp.float32)],
             270_000_000,
             2 << 20,
-        )(flat, pair_proj)
+        )(normed, pair_proj)
     with jax.named_scope("to_channels"):
         sides = lax.all_to_all(sides.reshape(CH, 2 * COLS, ROWS), PLANE, 0, 0, tiled=True)
     with jax.named_scope("right_values"):
         right = sides[:, :COLS]
     with jax.named_scope("right_across_x"):
         right_x = lax.ppermute(right, SHARE, [(d, d ^ 6) for d in range(8)])
-    part = bf16((4, 2, 4, 2, COLS, ROWS))
+    part = bf16((32, 2, COLS, ROWS))
     with jax.named_scope("triangle_own"):
         keep, send = call(triangle_kernel, [VMEM] * 2, (part, part), (), 270_000_000, 2 << 20)(sides, right)
     with jax.named_scope("sums_to_core"):
@@ -177,7 +188,7 @@
     with jax.named_scope("sums_to_core_across"):
         got_x = lax.ppermute(send_x, SHARE, [(d, d ^ 1) for d in range(8)])
     with jax.named_scope("add"):
-        tri = call(add_kernel, [VMEM] * 4, bf16((2, 4, 2, 4, 2, COLS, ROWS)), (), 1_000_000, 2 << 20)(keep, got, keep_x, got_x)
+        tri = call(add_kernel, [VMEM] * 4, bf16((32, 2, 2, COLS, ROWS)), (), 1_000_000, 2 << 20)(keep, got, keep_x, got_x)
     with jax.named_scope("to_columns"):
         tri = lax.all_to_all(tri.reshape(CH, COLS, ROWS), PLANE, 0, 0, tiled=True)
     with jax.named_scope("finish"):
@@ -186,16 +197,16 @@
             finish_kernel,
             [VMEM] * 6,
             f32((ROWS, COLS, CH)),
-            [pltpu.VMEM((CH, SUMS, ROWS), jnp.float32), HELD, pltpu.SemaphoreType.DMA((2,))],
+            [pltpu.VMEM((CH, SUMS, ROWS), jnp.float32), HELD, pltpu.SemaphoreType.DMA((4,))],
             1_000_000_000,
             4 << 20,
             HBM,
-        )(xt, gating, tri.reshape(CH // 2, 2, COLS, ROWS), proj_t, in_t, down_t)
+        )(xt, gating, tri.reshape(2, CH // 2, COLS, ROWS), proj_t, in_t, down_t)
 
 
 def solution(mesh):
-    fine = Mesh(mesh.devices.reshape(SIZES), AXES)
-    spec = P(("xh", "xb", "zh"), ("y", "zl", "core"), None)
+    fine = Mesh(mesh.devices.reshape((2,) * len(AXES)), AXES)
+    spec = P(AXES[:3], AXES[3:], None)
     return jax.shard_map(
         per_device, mesh=fine, in_specs=(spec, P(), P(), P(), P(), P()), out_specs=spec, check_vma=False
     )

time: 104 us -> 103 us (level); the launches traced: 102 us -> 102 us
    ppermute x1, starting transfers between devices: 4.28 us -> 2.94 us  [per_device(): right_x = lax.ppermute(right, SHARE, [(d, d ^ 6) for d in range(8)])]
    unnamed x12 -> x14, local copies, waits for them, and re-layouts: 2.15 us -> 1.63 us
where the time goes in v5:
time: 103 us; the launch traced here: 102 us
  blocking collectives  74.5 us (72%)
  starting transfers between devices  15.1 us (15%)
  Pallas kernels  6.52 us (6%)
  waiting for transfers between devices  4.3 us (4%)
  local copies, waits for them, and re-layouts  1.66 us (2%)
    all_to_all x1, blocking collectives, per_device(): lax.all_to_all(sides.reshape(CH, 2 * COLS, ROWS), PLANE, 0, 0, tiled=True)  47.9 us
    all_to_all x1, blocking collectives, per_device(): tri = lax.all_to_all(tri.reshape(CH, COLS, ROWS), PLANE, 0, 0, tiled=True)  26.6 us
    ppermute x1, starting transfers between devices, per_device(): got_x = lax.ppermute(send_x, SHARE, [(d, d ^ 1) for d in range(8)])  6.29 us
    ppermute x1, starting transfers between devices, per_device(): got = lax.ppermute(send, SHARE, [(d, d ^ 1) for d in range(8)])  5.82 us
    pallas_call x1, Pallas kernels, per_device(): call(finish_kernel, [VMEM] * 6, f32((ROWS, COLS, CH)), [pltpu.VMEM((CH, S...  3.31 us
    ppermute x1, waiting for transfers between devices, per_device(): right_x = lax.ppermute(right, SHARE, [(d, d ^ 6) for d in range(8)])  3.17 us
    ppermute x1, starting transfers between devices, per_device(): right_x = lax.ppermute(right, SHARE, [(d, d ^ 6) for d in range(8)])  2.94 us
  transfers between devices with their start and end apart: 3, of which 2 were waited for; matrix products, arithmetic and copies ran while one was open for 0% of the time, Pallas kernels for 2%

profile of v5, /device:TPU:1, one launch (start us, length us, event | category | flops | bytes accessed | tf_op | source)
XLA Modules:
  0.0 102.2 jit_solution(11841516274748168054)
XLA Ops:
  0.0 0.0 copy-start
  0.0 1.2 %copy-done = f32[128,16,128]{2,1,0:T(8,128)S(1)} copy-done((f32[128,16,128]{2,1,0:T(8,128)S(1)}, f32[128,16,128]{2,1,0:T(8,128)}, u32[]{:S(2)}) %copy-start) | copy-done | bytes 1048600
  1.2 0.0 copy-start.4
  1.2 0.5 norm.1.normed_ref
  1.8 0.4 copy-done.4
  2.1 0.9 project.1
  3.1 47.9 %all_to_all.10.left_ref = bf16[128,32,128]{2,1,0:T(8,128)(2,1)S(1)} all-to-all(bf16[128,32,128]{2,1,0:T(8,128)(2,1)S(1)} %bitcast.6), channel_id=1, replica_groups=mesh['xh'=2,'xb'=2,'zh'=2,'y2'=2,'y1'=2,'y0'=2,'zl1'=2,'zl0'=2,'core'=2]..., dimensions={0} | all-to-all | bytes 2097152 | tf_op jit(solution)/shard_map/to_channels/all_to_all | solution.py:164
  51.0 0.0 copy-start.1
  51.0 0.0 copy-start.2
  51.0 0.0 copy-start.3
  51.1 0.0 copy-start.5
  51.1 0.0 copy-start.6
  51.1 2.9 %collective-permute-start = (bf16[128,16,128]{2,1,0:T(8,128)(2,1)S(1)}, bf16[128,16,128]{2,1,0:T(8,128)(2,1)S(1)}, u32[]{:S(2)}, u32[]{:S(2)}) collective-permute-start(bf16[128,16,128]{2,1,0:T(8,128)(2,1)S(1)} %slice.4.right_ref), channel_id=1, source_target_pairs={{0,384},{1,385},{128,256},{129,257},{256,128},{257,129},{384,0},{3... | collective-permute-start | bytes 1572872 | tf_op jit(solution)/shard_map/right_across_x/ppermute | solution.py:168
  54.0 0.5 triangle_own.1
  54.5 5.8 %collective-permute-start.1 = (bf16[32,2,16,128]{3,2,1,0:T(8,128)(2,1)S(1)}, bf16[32,2,16,128]{3,2,1,0:T(8,128)(2,1)S(1)}, u32[]{:S(2)}, u32[]{:S(2)}) collective-permute-start(bf16[32,2,16,128]{3,2,1,0:T(8,128)(2,1)S(1)} %get-tuple-element.32), channel_id=1, source_target_pairs={{0,1},{1,0},{128,129},{129,128},{256,257},{257,256},{384,385},{385... | collective-permute-start | bytes 786440 | tf_op jit(solution)/shard_map/sums_to_core/ppermute | solution.py:173
  60.3 0.0 copy-done.1
  60.3 0.0 copy-done.2
  60.4 0.0 copy-done.3
  60.4 0.0 copy-done.5
  60.4 0.0 copy-done.6
  60.4 0.7 gate.1
  61.1 3.2 %collective-permute-done.right_ref = bf16[128,16,128]{2,1,0:T(8,128)(2,1)S(1)} collective-permute-done((bf16[128,16,128]{2,1,0:T(8,128)(2,1)S(1)}, bf16[128,16,128]{2,1,0:T(8,128)(2,1)S(1)}, u32[]{:S(2)}, u32[]{:S(2)}) %collective-permute-start) | collective-permute-done | bytes 524320 | tf_op jit(solution)/shard_map/right_across_x/ppermute | solution.py:168
  64.3 0.5 triangle_across.1
  64.8 6.3 %collective-permute-start.2 = (bf16[32,2,16,128]{3,2,1,0:T(8,128)(2,1)S(1)}, bf16[32,2,16,128]{3,2,1,0:T(8,128)(2,1)S(1)}, u32[]{:S(2)}, u32[]{:S(2)}) collective-permute-start(bf16[32,2,16,128]{3,2,1,0:T(8,128)(2,1)S(1)} %get-tuple-element.35), channel_id=1, source_target_pairs={{0,1},{1,0},{128,129},{129,128},{256,257},{257,256},{384,385},{385... | collective-permute-start | bytes 786440 | tf_op jit(solution)/shard_map/sums_to_core_across/ppermute | solution.py:189
  71.0 0.0 collective-permute-done.1.got_ref
  71.1 1.1 %collective-permute-done.2.got_x_ref = bf16[32,2,16,128]{3,2,1,0:T(8,128)(2,1)S(1)} collective-permute-done((bf16[32,2,16,128]{3,2,1,0:T(8,128)(2,1)S(1)}, bf16[32,2,16,128]{3,2,1,0:T(8,128)(2,1)S(1)}, u32[]{:S(2)}, u32[]{:S(2)}) %collective-permute-start.2) | collective-permute-done | bytes 262176 | tf_op jit(solution)/shard_map/sums_to_core_across/ppermute | solution.py:189
  72.2 0.1 add.1
  72.3 26.6 %all_to_all.11 = bf16[128,16,128]{2,1,0:T(8,128)(2,1)S(1)} all-to-all(bf16[128,16,128]{2,1,0:T(8,128)(2,1)S(1)} %bitcast.7), channel_id=1, replica_groups=mesh['xh'=2,'xb'=2,'zh'=2,'y2'=2,'y1'=2,'y0'=2,'zl1'=2,'zl0'=2,'core'=2]..., dimensions={0} | all-to-all | bytes 1048576 | tf_op jit(solution)/shard_map/to_columns/all_to_all | solution.py:193
  98.9 3.3 %finish.1 = f32[128,16,128]{2,1,0:T(8,128)} custom-call(f32[2,128,1024]{2,1,0:T(8,128)S(1)} %get-tuple-element.29.xt_ref, f32[2,128,1024]{2,1,0:T(8,128)S(1)} %get-tuple-element.30.gating_ref, bf16[2,64,16,128]{3,2,1,0:T(8,128)(2,1)S(1)} %bitcast.8, bf16[128,128]{1,0:T(8,128)(2,1)S(1)} %get-tuple-element.36.proj_ref, ...), custom_call_target="tpu_custom_call" | custom-call | flops 1000000000 | bytes 4194304 | tf_op jit(solution)/shard_map/finish/pallas_call | solution.py:196
  (1 shorter events, 0.0 us)
Async XLA Ops:
  0.0 1.2 %copy-start = (f32[128,16,128]{2,1,0:T(8,128)S(1)}, f32[128,16,128]{2,1,0:T(8,128)}, u32[]{:S(2)}) copy-start(f32[128,16,128]{2,1,0:T(8,128)} %param.6) | copy-start | bytes 3145732
  1.2 0.9 copy-start.4
  51.0 9.3 %copy-start.1 = (f32[128,16,128]{2,1,0:T(8,128)S(1)}, f32[128,16,128]{2,1,0:T(8,128)}, u32[]{:S(2)}) copy-start(f32[128,16,128]{2,1,0:T(8,128)} %param.6) | copy-start | bytes 3145732
  51.0 9.3 %copy-start.2 = (bf16[128,1024]{1,0:T(8,128)(2,1)S(1)}, bf16[128,1024]{1,0:T(8,128)(2,1)}, u32[]{:S(2)}) copy-start(bf16[128,1024]{1,0:T(8,128)(2,1)} %in_ref.1) | copy-start | bytes 786436
  51.0 9.3 %copy-start.3 = (bf16[512,128]{1,0:T(8,128)(2,1)S(1)}, bf16[512,128]{1,0:T(8,128)(2,1)}, u32[]{:S(2)}) copy-start(bf16[512,128]{1,0:T(8,128)(2,1)} %down_ref.1) | copy-start | bytes 393220
  51.1 9.3 %copy-start.5 = (bf16[128,128]{1,0:T(8,128)(2,1)S(1)}, bf16[128,128]{1,0:T(8,128)(2,1)}, u32[]{:S(2)}) copy-start(bf16[128,128]{1,0:T(8,128)(2,1)} %gate_ref.1) | copy-start | bytes 98308
  51.1 9.3 %copy-start.6 = (bf16[128,128]{1,0:T(8,128)(2,1)S(1)}, bf16[128,128]{1,0:T(8,128)(2,1)}, u32[]{:S(2)}) copy-start(bf16[128,128]{1,0:T(8,128)(2,1)} %proj_ref.1) | copy-start | bytes 98308
  51.1 13.2 %collective-permute-start = (bf16[128,16,128]{2,1,0:T(8,128)(2,1)S(1)}, bf16[128,16,128]{2,1,0:T(8,128)(2,1)S(1)}, u32[]{:S(2)}, u32[]{:S(2)}) collective-permute-start(bf16[128,16,128]{2,1,0:T(8,128)(2,1)S(1)} %slice.4.right_ref), channel_id=1, source_target_pairs={{0,384},{1,385},{128,256},{129,257},{256,128},{257,129},{384,0},{3... | collective-permute-start | bytes 1572872 | tf_op jit(solution)/shard_map/right_across_x/ppermute | solution.py:168
  54.5 16.5 %collective-permute-start.1 = (bf16[32,2,16,128]{3,2,1,0:T(8,128)(2,1)S(1)}, bf16[32,2,16,128]{3,2,1,0:T(8,128)(2,1)S(1)}, u32[]{:S(2)}, u32[]{:S(2)}) collective-permute-start(bf16[32,2,16,128]{3,2,1,0:T(8,128)(2,1)S(1)} %get-tuple-element.32), channel_id=1, source_target_pairs={{0,1},{1,0},{128,129},{129,128},{256,257},{257,256},{384,385},{385... | collective-permute-start | bytes 786440 | tf_op jit(solution)/shard_map/sums_to_core/ppermute | solution.py:173
  64.8 7.4 %collective-permute-start.2 = (bf16[32,2,16,128]{3,2,1,0:T(8,128)(2,1)S(1)}, bf16[32,2,16,128]{3,2,1,0:T(8,128)(2,1)S(1)}, u32[]{:S(2)}, u32[]{:S(2)}) collective-permute-start(bf16[32,2,16,128]{3,2,1,0:T(8,128)(2,1)S(1)} %get-tuple-element.35), channel_id=1, source_target_pairs={{0,1},{1,0},{128,129},{129,128},{256,257},{257,256},{384,385},{385... | collective-permute-start | bytes 786440 | tf_op jit(solution)/shard_map/sums_to_core_across/ppermute | solution.py:189

commit v6 on v5

v6 whole, which is shorter than its diff:
```python
import functools
import itertools

import jax
import jax.numpy as jnp
from jax import lax
from jax.experimental import pallas as pl
from jax.experimental.pallas import tpu as pltpu
from jax.sharding import Mesh
from jax.sharding import PartitionSpec as P

AXES = ("xh", "xb", "zh", "y2", "y1", "y0", "zl1", "zl0", "core")
PLANE = ("xb", "y0", "zl0", "y1", "zl1", "y2", "zh")
SHARE = ("xh", "xb", "core")
ROWS = 128
COLS = 16
CH = 128
HALF = COLS // 2
QUARTER = HALF // 2
SIDES = 2 * COLS + 8
SUMS = COLS + 8
EPS = 1e-05
FLOPS_X = 16_000_000_000
LIMIT = 16 * 1024 * 1024


def sigmoid(v):
    return 0.5 * jnp.tanh(0.5 * v) + 0.5


def norm_rows(v):
    centred = v - jnp.mean(v, axis=0, keepdims=True)
    spread = jnp.mean(centred * centred, axis=0, keepdims=True)
    return (centred * lax.rsqrt(spread + EPS)).astype(jnp.bfloat16)


def dot(a, b):
    return jnp.dot(a, b, preferred_element_type=jnp.float32)


def by_core(x):
    return x.reshape(4, 2, 16, CH).transpose(1, 0, 2, 3).reshape(2, 64, CH)


def half_columns(ref, h):
    return jnp.concatenate(
        [by_core(ref[pl.ds(HALF * h + s, ROWS, stride=COLS), :]).reshape(ROWS, CH).T for s in range(HALF)], axis=1
    )


def half_pairs(ref, h):
    tiles = []
    for pair in range(QUARTER):
        even, odd = (by_core(ref[pl.ds(HALF * h + 2 * pair + s, ROWS, stride=COLS), :]) for s in range(2))
        tiles += [jnp.concatenate([even[c], odd[c]], axis=0).T for c in range(2)]
    return jnp.concatenate(tiles, axis=1)


def norm_kernel(x_ref, normed_ref):
    for h in range(2):
        normed_ref[h] = norm_rows(half_pairs(x_ref, h))


def project_kernel(normed_ref, w_ref, out_ref, stage):
    core = lax.axis_index("core")
    weights = w_ref[...].T
    for h in range(2):
        p = dot(weights, normed_ref[h])
        left = sigmoid(p[:CH]) * p[CH : 2 * CH]
        right = sigmoid(p[2 * CH : 3 * CH]) * p[3 * CH :]
        for pair in range(QUARTER):
            row = QUARTER * h + pair
            for c in range(2):
                at = slice((2 * pair + c) * ROWS, (2 * pair + c + 1) * ROWS)
                stage[pl.ds(HALF * jnp.bitwise_xor(core, c) + row, CH, stride=SIDES), :] = right[:, at]
                stage[pl.ds(COLS + HALF * c + row, CH, stride=SIDES), :] = left[:, at]
    xh = lax.axis_index("xh")
    for b in range(2):
        rows = stage[64 * SIDES * b : 64 * SIDES * (b + 1)].reshape(64, SIDES, ROWS)[:, : 2 * COLS]
        out_ref[jnp.bitwise_xor(xh, b)] = rows.astype(jnp.bfloat16)


def gate_kernel(x_ref, gate_ref, proj_ref, in_ref, down_ref, xt_ref, gating_ref, proj_t_ref, in_t_ref, down_t_ref):
    weights = gate_ref[...].T
    for h in range(2):
        xt = half_columns(x_ref, h)
        xt_ref[h] = xt
        gating_ref[h] = sigmoid(dot(weights, norm_rows(xt)))
    proj_t_ref[...] = proj_ref[...].T
    in_t_ref[...] = in_ref[...].T
    down_t_ref[...] = down_ref[...].T


def halves(sides):
    low = lax.broadcasted_iota(jnp.int32, (32 * HALF, ROWS), 1) < 64
    parts = ([], [])
    for zh in range(2):
        for x in range(2):
            first = sides[x, :, zh, COLS : COLS + HALF].reshape(32 * HALF, ROWS)
            second = sides[x, :, zh, COLS + HALF :].reshape(32 * HALF, ROWS)
            parts[0].append(jnp.where(low, first, pltpu.roll(second, 64, 1)))
            parts[1].append(jnp.where(low, pltpu.roll(first, 64, 1), second))
    return [jnp.concatenate(part, axis=1).astype(jnp.bfloat16) for part in parts]


def turned(right):
    blocks = [right[x, :, zh].reshape(32 * HALF, ROWS).T for x in range(2) for zh in range(2)]
    return [
        jnp.concatenate([block[64 * s : 64 * s + 64] for block in blocks], axis=0).astype(jnp.bfloat16) for s in range(2)
    ]


def product(right, left):
    return dot(right[0], left[0]) + dot(right[1], left[1])


def wide(ref, rows):
    return ref[...].astype(jnp.float32).reshape(2, 32, 2, rows, ROWS)


def triangle_x_kernel(sides_ref, x_ref, left_ref, across_ref):
    left = halves(wide(sides_ref, 2 * COLS))
    for s in range(2):
        left_ref[s] = left[s]
    across_ref[...] = product(turned(wide(x_ref, HALF)), left)


def triangle_kernel(sides_ref, other_ref, xc_ref, left_ref, across_ref, out_ref):
    xh = lax.axis_index("xh")
    sides, other = wide(sides_ref, 2 * COLS), wide(other_ref, 2 * COLS)
    left, left_other = [left_ref[s] for s in range(2)], halves(other)
    own = product(turned(sides[:, :, :, :HALF]), left) + product(turned(other[:, :, :, HALF:COLS]), left_other)
    across = across_ref[...] + product(turned(wide(xc_ref, HALF)), left_other)
    for total, at in ((own, xh), (across, 1 - xh)):
        total = total.astype(jnp.bfloat16).reshape(2, 2, 4, 16, 4 * ROWS)
        for x, zj, z0, xj, z1, zh in itertools.product(range(2), repeat=6):
            lanes = slice((2 * zh + x) * ROWS, (2 * zh + x + 1) * ROWS)
            out_ref[16 * x + 8 * zj + 4 * z0 + 2 * xj + z1, at, zh] = total[xj, zj, 2 * z1 + z0, :, lanes]


def finish_kernel(xt_ref, gating_ref, t_ref, proj_ref, in_ref, down_ref, out_hbm, stage, held, sems):
    xh = lax.axis_index("xh")
    for b in range(2):
        stage[64 * b : 64 * b + 64, :COLS] = t_ref[jnp.bitwise_xor(xh, b)].astype(jnp.float32)
    sums = stage.reshape(CH * SUMS, ROWS)
    hidden = down_ref.shape[1]
    copies = []
    for h in range(2):
        tri = jnp.concatenate([sums[pl.ds(HALF * h + s, CH, stride=SUMS), :] for s in range(HALF)], axis=1)
        middle = xt_ref[h] + gating_ref[h] * dot(proj_ref[...], norm_rows(tri))
        t = dot(in_ref[...], norm_rows(middle))
        up = t[:hidden]
        units = (up * sigmoid(up) * t[hidden:]).astype(jnp.bfloat16)
        result = middle + dot(down_ref[...], units)
        for q in range(2):
            for s in range(QUARTER):
                c = QUARTER * q + s
                rows = result[:, c * ROWS : (c + 1) * ROWS].T.reshape(2, 4, 16, CH).transpose(1, 0, 2, 3)
                held.at[h][pl.ds(c, ROWS, stride=HALF), :] = rows.reshape(ROWS, CH)
            copy = pltpu.make_async_copy(
                held.at[h].reshape(ROWS, HALF, CH).at[:, pl.ds(QUARTER * q, QUARTER), :],
                out_hbm.at[:, pl.ds(HALF * h + QUARTER * q, QUARTER), :],
                sems.at[2 * h + q],
            )
            copy.start()
            copies.append(copy)
    for copy in copies:
        copy.wait()


VMEM = pl.BlockSpec(memory_space=pltpu.VMEM)
HBM = pl.BlockSpec(memory_space=pltpu.HBM)
HELD = pltpu.VMEM((2, ROWS * HALF, CH), jnp.float32)


def call(kernel, ins, outs, scratch=(), flops=0, moved=0, out_specs=None):
    many = isinstance(outs, tuple)
    return pl.pallas_call(
        kernel,
        out_shape=outs,
        in_specs=ins,
        out_specs=out_specs if out_specs is not None else ((VMEM,) * len(outs) if many else VMEM),
        scratch_shapes=list(scratch),
        compiler_params=pltpu.CompilerParams(vmem_limit_bytes=LIMIT),
        cost_estimate=pl.CostEstimate(flops=flops, bytes_accessed=moved, transcendentals=0),
    )


def per_device(pair_rep, pair_proj, gate_proj, out_proj, trans_in, trans_out):
    bf16 = functools.partial(jax.ShapeDtypeStruct, dtype=jnp.bfloat16)
    f32 = functools.partial(jax.ShapeDtypeStruct, dtype=jnp.float32)
    flat = pair_rep.reshape(ROWS * COLS, CH)
    with jax.named_scope("norm"):
        normed = call(norm_kernel, [VMEM], bf16((2, CH, HALF * ROWS)), (), 2_000_000, 2 << 20)(flat)
    with jax.named_scope("project"):
        sides = call(
            project_kernel,
            [VMEM, VMEM],
            bf16((2, CH // 2, 2 * COLS, ROWS)),
            [pltpu.VMEM((CH * SIDES, ROWS), jnp.float32)],
            270_000_000,
            2 << 20,
        )(normed, pair_proj)
    with jax.named_scope("to_channels"):
        sides = lax.all_to_all(sides.reshape(CH, 2 * COLS, ROWS), PLANE, 0, 0, tiled=True)
    flat, sides = lax.optimization_barrier((flat, sides))
    with jax.named_scope("right_across_x"):
        right_x = lax.ppermute(sides[:, :HALF].reshape(64, COLS, ROWS), SHARE, [(d, d ^ 6) for d in range(8)])
    with jax.named_scope("right_across_x_and_core"):
        right_xc = lax.ppermute(sides[:, HALF:COLS].reshape(64, COLS, ROWS), SHARE, [(d, d ^ 7) for d in range(8)])
    with jax.named_scope("sides_of_other_core"):
        other = lax.ppermute(sides, SHARE, [(d, d ^ 1) for d in range(8)])
    with jax.named_scope("gate"):
        turn = f32((2, CH, HALF * ROWS))
        gate = call(
            gate_kernel,
            [VMEM] * 5,
            (turn, turn, bf16(out_proj.shape[::-1]), bf16(trans_in.shape[::-1]), bf16(trans_out.shape[::-1])),
            (),
            70_000_000,
            4 << 20,
        )(flat, gate_proj, out_proj, trans_in, trans_out)
    right_x, right_xc, gate = lax.optimization_barrier((right_x, right_xc, gate))
    with jax.named_scope("triangle_x"):
        left, across = call(
            triangle_x_kernel, [VMEM] * 2, (bf16((2, 32 * HALF, 4 * ROWS)), f32((256, 4 * ROWS))), (), FLOPS_X, 3 << 20
        )(sides, right_x)
    left, across, other = lax.optimization_barrier((left, across, other))
    with jax.named_scope("triangle"):
        tri = call(triangle_kernel, [VMEM] * 5, bf16((32, 2, 2, COLS, ROWS)), (), 400_000_000, 4 << 20)(
            sides, other, right_xc, left, across
        )
    with jax.named_scope("to_columns"):
        tri = lax.all_to_all(tri.reshape(CH, COLS, ROWS), PLANE, 0, 0, tiled=True)
    with jax.named_scope("finish"):
        xt, gating, proj_t, in_t, down_t = gate
        return call(
            finish_kernel,
            [VMEM] * 6,
            f32((ROWS, COLS, CH)),
            [pltpu.VMEM((CH, SUMS, ROWS), jnp.float32), HELD, pltpu.SemaphoreType.DMA((4,))],
            1_000_000_000,
            4 << 20,
            HBM,
        )(xt, gating, tri.reshape(2, CH // 2, COLS, ROWS), proj_t, in_t, down_t)


def solution(mesh):
    fine = Mesh(mesh.devices.reshape((2,) * len(AXES)), AXES)
    spec = P(AXES[:3], AXES[3:], None)
    return jax.shard_map(
        per_device, mesh=fine, in_specs=(spec, P(), P(), P(), P(), P()), out_specs=spec, check_vma=False
    )
```

time: 103 us -> 101 us (0.981)
  starting transfers between devices: 15.1 us -> 12.2 us
    ppermute x3, starting transfers between devices: 15.1 us -> 12.2 us  [the longest x1 7.3 us: per_device(): lax.ppermute(sides[:, HALF:COLS].reshape(64, COLS, ROWS), SHARE, [(d, d ^...]
    pallas_call x4 -> x3, Pallas kernels: 1.77 us -> 2.11 us  [the longest x1 0.84 us: per_device(): call(triangle_kernel, [VMEM] * 5, bf16((32, 2, 2, COLS, ROWS)), (), 40000...]
  transfers between devices with their start and end apart: 3 -> 3, of which waited for: 2 -> 1; matrix products, arithmetic and copies ran while one was open for 0% -> 0% of each run, Pallas kernels for 2% -> 1%
where the time goes in v6:
time: 101 us; the launch traced here: 100 us
  blocking collectives  73.8 us (73%)
  starting transfers between devices  12.2 us (12%)
  Pallas kernels  7.32 us (7%)
  waiting for transfers between devices  5.28 us (5%)
  local copies, waits for them, and re-layouts  1.59 us (2%)
    all_to_all x1, blocking collectives, per_device(): lax.all_to_all(sides.reshape(CH, 2 * COLS, ROWS), PLANE, 0, 0, tiled=True)  48 us
    all_to_all x1, blocking collectives, per_device(): tri = lax.all_to_all(tri.reshape(CH, COLS, ROWS), PLANE, 0, 0, tiled=True)  25.7 us
    ppermute x1, starting transfers between devices, per_device(): lax.ppermute(sides[:, HALF:COLS].reshape(64, COLS, ROWS), SHARE, [(d, d ^...  7.3 us
    ppermute x1, waiting for transfers between devices, per_device(): lax.ppermute(sides[:, HALF:COLS].reshape(64, COLS, ROWS), SHARE, [(d, d ^...  5.27 us
    pallas_call x1, Pallas kernels, per_device(): call(finish_kernel, [VMEM] * 6, f32((ROWS, COLS, CH)), [pltpu.VMEM((CH, S...  3.31 us
    ppermute x1, starting transfers between devices, per_device(): lax.ppermute(sides[:, :HALF].reshape(64, COLS, ROWS), SHARE, [(d, d ^ 6)...  2.95 us
  transfers between devices with their start and end apart: 3, of which 1 were waited for; matrix products, arithmetic and copies ran while one was open for 0% of the time, Pallas kernels for 1%

profile of v6, /device:TPU:1, one launch (start us, length us, event | category | flops | bytes accessed | tf_op | source)
XLA Modules:
  0.0 100.3 jit_solution(8724312272071891648)
XLA Ops:
  0.0 0.0 copy-start
  0.0 1.2 %copy-done = f32[128,16,128]{2,1,0:T(8,128)S(1)} copy-done((f32[128,16,128]{2,1,0:T(8,128)S(1)}, f32[128,16,128]{2,1,0:T(8,128)}, u32[]{:S(2)}) %copy-start) | copy-done | bytes 1048600
  1.2 0.0 copy-start.4
  1.2 0.6 norm.1.normed_ref
  1.8 0.3 copy-done.4
  2.1 1.3 %project.1 = bf16[2,64,32,128]{3,2,1,0:T(8,128)(2,1)S(1)} custom-call(bf16[2,128,1024]{2,1,0:T(8,128)(2,1)S(1)} %norm.1.normed_ref, bf16[128,512]{1,0:T(8,128)(2,1)S(1)} %copy-done.4), custom_call_target="tpu_custom_call" | custom-call | flops 270000000 | bytes 2097152 | tf_op jit(solution)/shard_map/project/pallas_call | solution.py:196
  3.5 0.0 copy-start.2
  3.5 0.0 copy-start.3
  3.5 0.0 copy-start.5
  3.5 0.0 copy-start.6
  3.5 48.0 %all_to_all.10.sides_ref = bf16[128,32,128]{2,1,0:T(8,128)(2,1)S(1)} all-to-all(bf16[128,32,128]{2,1,0:T(8,128)(2,1)S(1)} %bitcast.8), channel_id=1, replica_groups=mesh['xh'=2,'xb'=2,'zh'=2,'y2'=2,'y1'=2,'y0'=2,'zl1'=2,'zl0'=2,'core'=2]..., dimensions={0} | all-to-all | bytes 2097152 | tf_op jit(solution)/shard_map/to_channels/all_to_all | solution.py:205
  51.6 0.0 copy-start.1
  51.6 2.9 %collective-permute-start = (bf16[64,16,128]{2,1,0:T(8,128)(2,1)S(1)}, bf16[64,16,128]{2,1,0:T(8,128)(2,1)S(1)}, u32[]{:S(2)}, u32[]{:S(2)}) collective-permute-start(bf16[64,16,128]{2,1,0:T(8,128)(2,1)S(1)} %bitcast.12), channel_id=1, source_target_pairs={{0,384},{1,385},{128,256},{129,257},{256,128},{257,129},{384,0},{3... | collective-permute-start | bytes 786440 | tf_op jit(solution)/shard_map/right_across_x/ppermute | solution.py:208
  54.6 7.3 %collective-permute-start.1 = (bf16[64,16,128]{2,1,0:T(8,128)(2,1)S(1)}, bf16[64,16,128]{2,1,0:T(8,128)(2,1)S(1)}, u32[]{:S(2)}, u32[]{:S(2)}) collective-permute-start(bf16[64,16,128]{2,1,0:T(8,128)(2,1)S(1)} %bitcast.11), channel_id=1, source_target_pairs={{0,385},{1,384},{128,257},{129,256},{256,129},{257,128},{384,1},{3... | collective-permute-start | bytes 786440 | tf_op jit(solution)/shard_map/right_across_x_and_core/ppermute | solution.py:210
  61.9 1.9 %collective-permute-start.2 = (bf16[128,32,128]{2,1,0:T(8,128)(2,1)S(1)}, bf16[128,32,128]{2,1,0:T(8,128)(2,1)S(1)}, u32[]{:S(2)}, u32[]{:S(2)}) collective-permute-start(bf16[128,32,128]{2,1,0:T(8,128)(2,1)S(1)} %all_to_all.10.sides_ref), channel_id=1, source_target_pairs={{0,1},{1,0},{128,129},{129,128},{256,257},{257,256},{384,385},{385... | collective-permute-start | bytes 3145736 | tf_op jit(solution)/shard_map/sides_of_other_core/ppermute | solution.py:212
  63.8 0.0 copy-done.2
  63.8 0.0 copy-done.3
  63.8 0.0 copy-done.5
  63.8 0.0 copy-done.6
  63.8 0.0 copy-done.1
  63.8 0.7 gate.1
  64.6 0.0 collective-permute-done.x_ref
  64.6 5.3 %collective-permute-done.1.xc_ref = bf16[64,16,128]{2,1,0:T(8,128)(2,1)S(1)} collective-permute-done((bf16[64,16,128]{2,1,0:T(8,128)(2,1)S(1)}, bf16[64,16,128]{2,1,0:T(8,128)(2,1)S(1)}, u32[]{:S(2)}, u32[]{:S(2)}) %collective-permute-start.1) | collective-permute-done | bytes 262176 | tf_op jit(solution)/shard_map/right_across_x_and_core/ppermute | solution.py:210
  69.8 0.6 triangle_x.1
  70.4 0.0 collective-permute-done.2.other_ref
  70.4 0.8 triangle.1
  71.3 25.7 %all_to_all.11 = bf16[128,16,128]{2,1,0:T(8,128)(2,1)S(1)} all-to-all(bf16[128,16,128]{2,1,0:T(8,128)(2,1)S(1)} %bitcast.9), channel_id=1, replica_groups=mesh['xh'=2,'xb'=2,'zh'=2,'y2'=2,'y1'=2,'y0'=2,'zl1'=2,'zl0'=2,'core'=2]..., dimensions={0} | all-to-all | bytes 1048576 | tf_op jit(solution)/shard_map/to_columns/all_to_all | solution.py:234
  97.0 3.3 %finish.1 = f32[128,16,128]{2,1,0:T(8,128)} custom-call(f32[2,128,1024]{2,1,0:T(8,128)S(1)} %get-tuple-element.31.xt_ref, f32[2,128,1024]{2,1,0:T(8,128)S(1)} %get-tuple-element.32.gating_ref, bf16[2,64,16,128]{3,2,1,0:T(8,128)(2,1)S(1)} %bitcast.10, bf16[128,128]{1,0:T(8,128)(2,1)S(1)} %get-tuple-element.40.proj_ref, ...), custom_call_target="tpu_custom_call" | custom-call | flops 1000000000 | bytes 4194304 | tf_op jit(solution)/shard_map/finish/pallas_call | solution.py:237
  (1 shorter events, 0.0 us)
Async XLA Ops:
  0.0 1.2 %copy-start = (f32[128,16,128]{2,1,0:T(8,128)S(1)}, f32[128,16,128]{2,1,0:T(8,128)}, u32[]{:S(2)}) copy-start(f32[128,16,128]{2,1,0:T(8,128)} %param.6) | copy-start | bytes 3145732
  1.2 0.9 copy-start.4
  3.5 60.3 %copy-start.2 = (bf16[128,1024]{1,0:T(8,128)(2,1)S(1)}, bf16[128,1024]{1,0:T(8,128)(2,1)}, u32[]{:S(2)}) copy-start(bf16[128,1024]{1,0:T(8,128)(2,1)} %in_ref.1) | copy-start | bytes 786436
  3.5 60.3 %copy-start.3 = (bf16[512,128]{1,0:T(8,128)(2,1)S(1)}, bf16[512,128]{1,0:T(8,128)(2,1)}, u32[]{:S(2)}) copy-start(bf16[512,128]{1,0:T(8,128)(2,1)} %down_ref.1) | copy-start | bytes 393220
  3.5 60.3 %copy-start.5 = (bf16[128,128]{1,0:T(8,128)(2,1)S(1)}, bf16[128,128]{1,0:T(8,128)(2,1)}, u32[]{:S(2)}) copy-start(bf16[128,128]{1,0:T(8,128)(2,1)} %gate_ref.1) | copy-start | bytes 98308
  3.5 60.3 %copy-start.6 = (bf16[128,128]{1,0:T(8,128)(2,1)S(1)}, bf16[128,128]{1,0:T(8,128)(2,1)}, u32[]{:S(2)}) copy-start(bf16[128,128]{1,0:T(8,128)(2,1)} %proj_ref.1) | copy-start | bytes 98308
  51.6 12.3 %copy-start.1 = (f32[128,16,128]{2,1,0:T(8,128)S(1)}, f32[128,16,128]{2,1,0:T(8,128)}, u32[]{:S(2)}) copy-start(f32[128,16,128]{2,1,0:T(8,128)} %param.6) | copy-start | bytes 3145732
  51.6 13.0 %collective-permute-start = (bf16[64,16,128]{2,1,0:T(8,128)(2,1)S(1)}, bf16[64,16,128]{2,1,0:T(8,128)(2,1)S(1)}, u32[]{:S(2)}, u32[]{:S(2)}) collective-permute-start(bf16[64,16,128]{2,1,0:T(8,128)(2,1)S(1)} %bitcast.12), channel_id=1, source_target_pairs={{0,384},{1,385},{128,256},{129,257},{256,128},{257,129},{384,0},{3... | collective-permute-start | bytes 786440 | tf_op jit(solution)/shard_map/right_across_x/ppermute | solution.py:208
  54.6 15.3 %collective-permute-start.1 = (bf16[64,16,128]{2,1,0:T(8,128)(2,1)S(1)}, bf16[64,16,128]{2,1,0:T(8,128)(2,1)S(1)}, u32[]{:S(2)}, u32[]{:S(2)}) collective-permute-start(bf16[64,16,128]{2,1,0:T(8,128)(2,1)S(1)} %bitcast.11), channel_id=1, source_target_pairs={{0,385},{1,384},{128,257},{129,256},{256,129},{257,128},{384,1},{3... | collective-permute-start | bytes 786440 | tf_op jit(solution)/shard_map/right_across_x_and_core/ppermute | solution.py:210
  61.9 8.5 %collective-permute-start.2 = (bf16[128,32,128]{2,1,0:T(8,128)(2,1)S(1)}, bf16[128,32,128]{2,1,0:T(8,128)(2,1)S(1)}, u32[]{:S(2)}, u32[]{:S(2)}) collective-permute-start(bf16[128,32,128]{2,1,0:T(8,128)(2,1)S(1)} %all_to_all.10.sides_ref), channel_id=1, source_target_pairs={{0,1},{1,0},{128,129},{129,128},{256,257},{257,256},{384,385},{385... | collective-permute-start | bytes 3145736 | tf_op jit(solution)/shard_map/sides_of_other_core/ppermute | solution.py:212

commit v7 on v6

--- a/solution.py
+++ b/solution.py
@@ -72,11 +72,15 @@
             row = QUARTER * h + pair
             for c in range(2):
                 at = slice((2 * pair + c) * ROWS, (2 * pair + c + 1) * ROWS)
-                stage[pl.ds(HALF * jnp.bitwise_xor(core, c) + row, CH, stride=SIDES), :] = right[:, at]
+                stage[pl.ds(HALF * c + row, CH, stride=SIDES), :] = right[:, at]
                 stage[pl.ds(COLS + HALF * c + row, CH, stride=SIDES), :] = left[:, at]
     xh = lax.axis_index("xh")
     for b in range(2):
-        rows = stage[64 * SIDES * b : 64 * SIDES * (b + 1)].reshape(64, SIDES, ROWS)[:, : 2 * COLS]
+        rows = stage[64 * SIDES * b : 64 * SIDES * (b + 1)].reshape(64, SIDES, ROWS)
+        first, second = rows[:, :HALF], rows[:, HALF:COLS]
+        own = jnp.where(core == 0, first, second)
+        other = jnp.where(core == 0, second, first)
+        rows = jnp.concatenate([own, other, rows[:, COLS : 2 * COLS]], axis=1)
         out_ref[jnp.bitwise_xor(xh, b)] = rows.astype(jnp.bfloat16)
 
 
@@ -118,19 +122,24 @@
     return ref[...].astype(jnp.float32).reshape(2, 32, 2, rows, ROWS)
 
 
-def triangle_x_kernel(sides_ref, x_ref, left_ref, across_ref):
-    left = halves(wide(sides_ref, 2 * COLS))
+def triangle_own_kernel(sides_ref, left_ref, own_ref):
+    sides = wide(sides_ref, 2 * COLS)
+    left = halves(sides)
     for s in range(2):
         left_ref[s] = left[s]
-    across_ref[...] = product(turned(wide(x_ref, HALF)), left)
-
-
-def triangle_kernel(sides_ref, other_ref, xc_ref, left_ref, across_ref, out_ref):
+    own_ref[...] = product(turned(sides[:, :, :, :HALF]), left)
+
+
+def triangle_x_kernel(x_ref, left_ref, across_ref):
+    across_ref[...] = product(turned(wide(x_ref, HALF)), [left_ref[s] for s in range(2)])
+
+
+def triangle_kernel(other_ref, xc_ref, own_ref, across_ref, out_ref):
     xh = lax.axis_index("xh")
-    sides, other = wide(sides_ref, 2 * COLS), wide(other_ref, 2 * COLS)
-    left, left_other = [left_ref[s] for s in range(2)], halves(other)
-    own = product(turned(sides[:, :, :, :HALF]), left) + product(turned(other[:, :, :, HALF:COLS]), left_other)
-    across = across_ref[...] + product(turned(wide(xc_ref, HALF)), left_other)
+    other = wide(other_ref, 2 * COLS)
+    left = halves(other)
+    own = own_ref[...] + product(turned(other[:, :, :, HALF:COLS]), left)
+    across = across_ref[...] + product(turned(wide(xc_ref, HALF)), left)
     for total, at in ((own, xh), (across, 1 - xh)):
         total = total.astype(jnp.bfloat16).reshape(2, 2, 4, 16, 4 * ROWS)
         for x, zj, z0, xj, z1, zh in itertools.product(range(2), repeat=6):
@@ -220,15 +229,18 @@
             70_000_000,
             4 << 20,
         )(flat, gate_proj, out_proj, trans_in, trans_out)
-    right_x, right_xc, gate = lax.optimization_barrier((right_x, right_xc, gate))
+    with jax.named_scope("triangle_own"):
+        sums = f32((256, 4 * ROWS))
+        left, own = call(
+            triangle_own_kernel, [VMEM], (bf16((2, 32 * HALF, 4 * ROWS)), sums), (), 140_000_000, 3 << 20
+        )(sides)
+    right_x, right_xc, left, own, gate = lax.optimization_barrier((right_x, right_xc, left, own, gate))
     with jax.named_scope("triangle_x"):
-        left, across = call(
-            triangle_x_kernel, [VMEM] * 2, (bf16((2, 32 * HALF, 4 * ROWS)), f32((256, 4 * ROWS))), (), FLOPS_X, 3 << 20
-        )(sides, right_x)
-    left, across, other = lax.optimization_barrier((left, across, other))
+        across = call(triangle_x_kernel, [VMEM] * 2, sums, (), FLOPS_X, 2 << 20)(right_x, left)
+    across, other = lax.optimization_barrier((across, other))
     with jax.named_scope("triangle"):
-        tri = call(triangle_kernel, [VMEM] * 5, bf16((32, 2, 2, COLS, ROWS)), (), 400_000_000, 4 << 20)(
-            sides, other, right_xc, left, across
+        tri = call(triangle_kernel, [VMEM] * 4, bf16((32, 2, 2, COLS, ROWS)), (), 280_000_000, 4 << 20)(
+            other, right_xc, own, across
         )
     with jax.named_scope("to_columns"):
         tri = lax.all_to_all(tri.reshape(CH, COLS, ROWS), PLANE, 0, 0, tiled=True)

time: 101 us -> 100 us (0.990)
  transfers between devices with their start and end apart: 3 -> 3, of which waited for: 1 -> 1; matrix products, arithmetic and copies ran while one was open for 0% -> 0% of each run, Pallas kernels for 1% -> 2%
where the time goes in v7:
time: 100 us; the launch traced here: 99.9 us
  blocking collectives  74.1 us (74%)
  starting transfers between devices  12.2 us (12%)
  Pallas kernels  7.18 us (7%)
  waiting for transfers between devices  4.72 us (5%)
  local copies, waits for them, and re-layouts  1.59 us (2%)
    all_to_all x1, blocking collectives, per_device(): lax.all_to_all(sides.reshape(CH, 2 * COLS, ROWS), PLANE, 0, 0, tiled=True)  48.1 us
    all_to_all x1, blocking collectives, per_device(): tri = lax.all_to_all(tri.reshape(CH, COLS, ROWS), PLANE, 0, 0, tiled=True)  26 us
    ppermute x1, starting transfers between devices, per_device(): lax.ppermute(sides[:, HALF:COLS].reshape(64, COLS, ROWS), SHARE, [(d, d ^...  7.31 us
    ppermute x1, waiting for transfers between devices, per_device(): lax.ppermute(sides[:, HALF:COLS].reshape(64, COLS, ROWS), SHARE, [(d, d ^...  4.71 us
    pallas_call x1, Pallas kernels, per_device(): call(finish_kernel, [VMEM] * 6, f32((ROWS, COLS, CH)), [pltpu.VMEM((CH, S...  3.31 us
    ppermute x1, starting transfers between devices, per_device(): lax.ppermute(sides[:, :HALF].reshape(64, COLS, ROWS), SHARE, [(d, d ^ 6)...  2.94 us
  transfers between devices with their start and end apart: 3, of which 1 were waited for; matrix products, arithmetic and copies ran while one was open for 0% of the time, Pallas kernels for 2%

profile of v7, /device:TPU:1, one launch (start us, length us, event | category | flops | bytes accessed | tf_op | source)
XLA Modules:
  0.0 99.9 jit_solution(11721795516526125115)
XLA Ops:
  0.0 0.0 copy-start
  0.0 1.2 %copy-done = f32[128,16,128]{2,1,0:T(8,128)S(1)} copy-done((f32[128,16,128]{2,1,0:T(8,128)S(1)}, f32[128,16,128]{2,1,0:T(8,128)}, u32[]{:S(2)}) %copy-start) | copy-done | bytes 1048600
  1.2 0.0 copy-start.4
  1.2 0.6 norm.1.normed_ref
  1.8 0.3 copy-done.4
  2.1 0.9 project.1
  3.1 0.0 copy-start.2
  3.1 0.0 copy-start.3
  3.1 0.0 copy-start.5
  3.1 0.0 copy-start.6
  3.1 48.1 %all_to_all.10.sides_ref = bf16[128,32,128]{2,1,0:T(8,128)(2,1)S(1)} all-to-all(bf16[128,32,128]{2,1,0:T(8,128)(2,1)S(1)} %bitcast.8), channel_id=1, replica_groups=mesh['xh'=2,'xb'=2,'zh'=2,'y2'=2,'y1'=2,'y0'=2,'zl1'=2,'zl0'=2,'core'=2]..., dimensions={0} | all-to-all | bytes 2097152 | tf_op jit(solution)/shard_map/to_channels/all_to_all | solution.py:214
  51.2 0.0 copy-start.1
  51.2 2.9 %collective-permute-start = (bf16[64,16,128]{2,1,0:T(8,128)(2,1)S(1)}, bf16[64,16,128]{2,1,0:T(8,128)(2,1)S(1)}, u32[]{:S(2)}, u32[]{:S(2)}) collective-permute-start(bf16[64,16,128]{2,1,0:T(8,128)(2,1)S(1)} %bitcast.12), channel_id=1, source_target_pairs={{0,384},{1,385},{128,256},{129,257},{256,128},{257,129},{384,0},{3... | collective-permute-start | bytes 786440 | tf_op jit(solution)/shard_map/right_across_x/ppermute | solution.py:217
  54.2 7.3 %collective-permute-start.1 = (bf16[64,16,128]{2,1,0:T(8,128)(2,1)S(1)}, bf16[64,16,128]{2,1,0:T(8,128)(2,1)S(1)}, u32[]{:S(2)}, u32[]{:S(2)}) collective-permute-start(bf16[64,16,128]{2,1,0:T(8,128)(2,1)S(1)} %bitcast.11), channel_id=1, source_target_pairs={{0,385},{1,384},{128,257},{129,256},{256,129},{257,128},{384,1},{3... | collective-permute-start | bytes 786440 | tf_op jit(solution)/shard_map/right_across_x_and_core/ppermute | solution.py:219
  61.5 1.9 %collective-permute-start.2 = (bf16[128,32,128]{2,1,0:T(8,128)(2,1)S(1)}, bf16[128,32,128]{2,1,0:T(8,128)(2,1)S(1)}, u32[]{:S(2)}, u32[]{:S(2)}) collective-permute-start(bf16[128,32,128]{2,1,0:T(8,128)(2,1)S(1)} %all_to_all.10.sides_ref), channel_id=1, source_target_pairs={{0,1},{1,0},{128,129},{129,128},{256,257},{257,256},{384,385},{385... | collective-permute-start | bytes 3145736 | tf_op jit(solution)/shard_map/sides_of_other_core/ppermute | solution.py:221
  63.4 0.0 copy-done.2
  63.4 0.0 copy-done.3
  63.4 0.0 copy-done.5
  63.5 0.0 copy-done.6
  63.5 0.0 copy-done.1
  63.5 0.7 gate.1
  64.2 0.6 triangle_own.1
  64.7 0.0 collective-permute-done.x_ref
  64.8 4.7 %collective-permute-done.1.xc_ref = bf16[64,16,128]{2,1,0:T(8,128)(2,1)S(1)} collective-permute-done((bf16[64,16,128]{2,1,0:T(8,128)(2,1)S(1)}, bf16[64,16,128]{2,1,0:T(8,128)(2,1)S(1)}, u32[]{:S(2)}, u32[]{:S(2)}) %collective-permute-start.1) | collective-permute-done | bytes 262176 | tf_op jit(solution)/shard_map/right_across_x_and_core/ppermute | solution.py:219
  69.5 0.4 triangle_x.1.across_ref
  69.8 0.0 collective-permute-done.2.other_ref
  69.8 0.7 triangle.1
  70.6 26.0 %all_to_all.11 = bf16[128,16,128]{2,1,0:T(8,128)(2,1)S(1)} all-to-all(bf16[128,16,128]{2,1,0:T(8,128)(2,1)S(1)} %bitcast.9), channel_id=1, replica_groups=mesh['xh'=2,'xb'=2,'zh'=2,'y2'=2,'y1'=2,'y0'=2,'zl1'=2,'zl0'=2,'core'=2]..., dimensions={0} | all-to-all | bytes 1048576 | tf_op jit(solution)/shard_map/to_columns/all_to_all | solution.py:246
  96.6 3.3 %finish.1 = f32[128,16,128]{2,1,0:T(8,128)} custom-call(f32[2,128,1024]{2,1,0:T(8,128)S(1)} %get-tuple-element.34.xt_ref, f32[2,128,1024]{2,1,0:T(8,128)S(1)} %get-tuple-element.35.gating_ref, bf16[2,64,16,128]{3,2,1,0:T(8,128)(2,1)S(1)} %bitcast.10, bf16[128,128]{1,0:T(8,128)(2,1)S(1)} %get-tuple-element.42.proj_ref, ...), custom_call_target="tpu_custom_call" | custom-call | flops 1000000000 | bytes 4194304 | tf_op jit(solution)/shard_map/finish/pallas_call | solution.py:249
  (1 shorter events, 0.0 us)
Async XLA Ops:
  0.0 1.2 %copy-start = (f32[128,16,128]{2,1,0:T(8,128)S(1)}, f32[128,16,128]{2,1,0:T(8,128)}, u32[]{:S(2)}) copy-start(f32[128,16,128]{2,1,0:T(8,128)} %param.6) | copy-start | bytes 3145732
  1.2 0.9 copy-start.4
  3.1 60.3 %copy-start.2 = (bf16[128,1024]{1,0:T(8,128)(2,1)S(1)}, bf16[128,1024]{1,0:T(8,128)(2,1)}, u32[]{:S(2)}) copy-start(bf16[128,1024]{1,0:T(8,128)(2,1)} %in_ref.1) | copy-start | bytes 786436
  3.1 60.3 %copy-start.3 = (bf16[512,128]{1,0:T(8,128)(2,1)S(1)}, bf16[512,128]{1,0:T(8,128)(2,1)}, u32[]{:S(2)}) copy-start(bf16[512,128]{1,0:T(8,128)(2,1)} %down_ref.1) | copy-start | bytes 393220
  3.1 60.3 %copy-start.5 = (bf16[128,128]{1,0:T(8,128)(2,1)S(1)}, bf16[128,128]{1,0:T(8,128)(2,1)}, u32[]{:S(2)}) copy-start(bf16[128,128]{1,0:T(8,128)(2,1)} %gate_ref.1) | copy-start | bytes 98308
  3.1 60.3 %copy-start.6 = (bf16[128,128]{1,0:T(8,128)(2,1)S(1)}, bf16[128,128]{1,0:T(8,128)(2,1)}, u32[]{:S(2)}) copy-start(bf16[128,128]{1,0:T(8,128)(2,1)} %proj_ref.1) | copy-start | bytes 98308
  51.2 12.3 %copy-start.1 = (f32[128,16,128]{2,1,0:T(8,128)S(1)}, f32[128,16,128]{2,1,0:T(8,128)}, u32[]{:S(2)}) copy-start(f32[128,16,128]{2,1,0:T(8,128)} %param.6) | copy-start | bytes 3145732
  51.2 13.5 %collective-permute-start = (bf16[64,16,128]{2,1,0:T(8,128)(2,1)S(1)}, bf16[64,16,128]{2,1,0:T(8,128)(2,1)S(1)}, u32[]{:S(2)}, u32[]{:S(2)}) collective-permute-start(bf16[64,16,128]{2,1,0:T(8,128)(2,1)S(1)} %bitcast.12), channel_id=1, source_target_pairs={{0,384},{1,385},{128,256},{129,257},{256,128},{257,129},{384,0},{3... | collective-permute-start | bytes 786440 | tf_op jit(solution)/shard_map/right_across_x/ppermute | solution.py:217
  54.2 15.3 %collective-permute-start.1 = (bf16[64,16,128]{2,1,0:T(8,128)(2,1)S(1)}, bf16[64,16,128]{2,1,0:T(8,128)(2,1)S(1)}, u32[]{:S(2)}, u32[]{:S(2)}) collective-permute-start(bf16[64,16,128]{2,1,0:T(8,128)(2,1)S(1)} %bitcast.11), channel_id=1, source_target_pairs={{0,385},{1,384},{128,257},{129,256},{256,129},{257,128},{384,1},{3... | collective-permute-start | bytes 786440 | tf_op jit(solution)/shard_map/right_across_x_and_core/ppermute | solution.py:219
  61.5 8.3 %collective-permute-start.2 = (bf16[128,32,128]{2,1,0:T(8,128)(2,1)S(1)}, bf16[128,32,128]{2,1,0:T(8,128)(2,1)S(1)}, u32[]{:S(2)}, u32[]{:S(2)}) collective-permute-start(bf16[128,32,128]{2,1,0:T(8,128)(2,1)S(1)} %all_to_all.10.sides_ref), channel_id=1, source_target_pairs={{0,1},{1,0},{128,129},{129,128},{256,257},{257,256},{384,385},{385... | collective-permute-start | bytes 3145736 | tf_op jit(solution)/shard_map/sides_of_other_core/ppermute | solution.py:221

commit v8 on v7

--- a/solution.py
+++ b/solution.py
@@ -108,9 +108,9 @@
 
 
 def turned(right):
-    blocks = [right[x, :, zh].reshape(32 * HALF, ROWS).T for x in range(2) for zh in range(2)]
+    blocks = [right[x, :, zh].reshape(32 * HALF, ROWS).astype(jnp.bfloat16).T for x in range(2) for zh in range(2)]
     return [
-        jnp.concatenate([block[64 * s : 64 * s + 64] for block in blocks], axis=0).astype(jnp.bfloat16) for s in range(2)
+        jnp.concatenate([block[64 * s : 64 * s + 64] for block in blocks], axis=0) for s in range(2)
     ]
 
 
@@ -122,23 +122,26 @@
     return ref[...].astype(jnp.float32).reshape(2, 32, 2, rows, ROWS)
 
 
-def triangle_own_kernel(sides_ref, left_ref, own_ref):
+LEFT = 4 * ROWS
+
+
+def triangle_own_kernel(sides_ref, pack_ref, own_ref):
     sides = wide(sides_ref, 2 * COLS)
-    left = halves(sides)
+    left, right = halves(sides), turned(sides[:, :, :, HALF:COLS])
     for s in range(2):
-        left_ref[s] = left[s]
+        pack_ref[s, :, :LEFT] = left[s]
+        pack_ref[s, :, LEFT:] = right[s]
     own_ref[...] = product(turned(sides[:, :, :, :HALF]), left)
 
 
-def triangle_x_kernel(x_ref, left_ref, across_ref):
-    across_ref[...] = product(turned(wide(x_ref, HALF)), [left_ref[s] for s in range(2)])
+def triangle_x_kernel(x_ref, pack_ref, across_ref):
+    across_ref[...] = product(turned(wide(x_ref, HALF)), [pack_ref[s, :, :LEFT] for s in range(2)])
 
 
 def triangle_kernel(other_ref, xc_ref, own_ref, across_ref, out_ref):
     xh = lax.axis_index("xh")
-    other = wide(other_ref, 2 * COLS)
-    left = halves(other)
-    own = own_ref[...] + product(turned(other[:, :, :, HALF:COLS]), left)
+    left = [other_ref[s, :, :LEFT] for s in range(2)]
+    own = own_ref[...] + product([other_ref[s, :, LEFT:] for s in range(2)], left)
     across = across_ref[...] + product(turned(wide(xc_ref, HALF)), left)
     for total, at in ((own, xh), (across, 1 - xh)):
         total = total.astype(jnp.bfloat16).reshape(2, 2, 4, 16, 4 * ROWS)
@@ -217,8 +220,6 @@
         right_x = lax.ppermute(sides[:, :HALF].reshape(64, COLS, ROWS), SHARE, [(d, d ^ 6) for d in range(8)])
     with jax.named_scope("right_across_x_and_core"):
         right_xc = lax.ppermute(sides[:, HALF:COLS].reshape(64, COLS, ROWS), SHARE, [(d, d ^ 7) for d in range(8)])
-    with jax.named_scope("sides_of_other_core"):
-        other = lax.ppermute(sides, SHARE, [(d, d ^ 1) for d in range(8)])
     with jax.named_scope("gate"):
         turn = f32((2, CH, HALF * ROWS))
         gate = call(
@@ -230,13 +231,15 @@
             4 << 20,
         )(flat, gate_proj, out_proj, trans_in, trans_out)
     with jax.named_scope("triangle_own"):
-        sums = f32((256, 4 * ROWS))
-        left, own = call(
-            triangle_own_kernel, [VMEM], (bf16((2, 32 * HALF, 4 * ROWS)), sums), (), 140_000_000, 3 << 20
+        sums = f32((256, LEFT))
+        pack, own = call(
+            triangle_own_kernel, [VMEM], (bf16((2, 256, LEFT + 256)), sums), (), 140_000_000, 3 << 20
         )(sides)
-    right_x, right_xc, left, own, gate = lax.optimization_barrier((right_x, right_xc, left, own, gate))
+    with jax.named_scope("pack_of_other_core"):
+        other = lax.ppermute(pack, SHARE, [(d, d ^ 1) for d in range(8)])
+    right_x, right_xc, pack, own, gate = lax.optimization_barrier((right_x, right_xc, pack, own, gate))
     with jax.named_scope("triangle_x"):
-        across = call(triangle_x_kernel, [VMEM] * 2, sums, (), FLOPS_X, 2 << 20)(right_x, left)
+        across = call(triangle_x_kernel, [VMEM] * 2, sums, (), FLOPS_X, 2 << 20)(right_x, pack)
     across, other = lax.optimization_barrier((across, other))
     with jax.named_scope("triangle"):
         tri = call(triangle_kernel, [VMEM] * 4, bf16((32, 2, 2, COLS, ROWS)), (), 280_000_000, 4 << 20)(

time: 100 us -> 99.5 us (level)
  no operation moved by 1% of the time
where the time goes in v8:
time: 99.5 us; the launch traced here: 99.1 us
  blocking collectives  73.7 us (74%)
  starting transfers between devices  12.3 us (12%)
  Pallas kernels  6.9 us (7%)
  waiting for transfers between devices  4.44 us (4%)
  local copies, waits for them, and re-layouts  1.59 us (2%)
    all_to_all x1, blocking collectives, per_device(): lax.all_to_all(sides.reshape(CH, 2 * COLS, ROWS), PLANE, 0, 0, tiled=True)  47.9 us
    all_to_all x1, blocking collectives, per_device(): tri = lax.all_to_all(tri.reshape(CH, COLS, ROWS), PLANE, 0, 0, tiled=True)  25.8 us
    ppermute x1, starting transfers between devices, per_device(): lax.ppermute(sides[:, HALF:COLS].reshape(64, COLS, ROWS), SHARE, [(d, d ^...  7.44 us
    ppermute x1, waiting for transfers between devices, per_device(): lax.ppermute(sides[:, HALF:COLS].reshape(64, COLS, ROWS), SHARE, [(d, d ^...  4.43 us
    pallas_call x1, Pallas kernels, per_device(): call(finish_kernel, [VMEM] * 6, f32((ROWS, COLS, CH)), [pltpu.VMEM((CH, S...  3.3 us
    ppermute x1, starting transfers between devices, per_device(): lax.ppermute(sides[:, :HALF].reshape(64, COLS, ROWS), SHARE, [(d, d ^ 6)...  2.94 us
  transfers between devices with their start and end apart: 3, of which 1 were waited for; matrix products, arithmetic and copies ran while one was open for 0% of the time, Pallas kernels for 2%

profile of v8, /device:TPU:1, one launch (start us, length us, event | category | flops | bytes accessed | tf_op | source)
XLA Modules:
  0.0 99.1 jit_solution(9779266462569285626)
XLA Ops:
  0.0 0.0 copy-start
  0.0 1.2 %copy-done = f32[128,16,128]{2,1,0:T(8,128)S(1)} copy-done((f32[128,16,128]{2,1,0:T(8,128)S(1)}, f32[128,16,128]{2,1,0:T(8,128)}, u32[]{:S(2)}) %copy-start) | copy-done | bytes 1048600
  1.2 0.0 copy-start.4
  1.2 0.6 norm.1.normed_ref
  1.8 0.3 copy-done.4
  2.1 0.9 project.1
  3.1 47.9 %all_to_all.10.sides_ref = bf16[128,32,128]{2,1,0:T(8,128)(2,1)S(1)} all-to-all(bf16[128,32,128]{2,1,0:T(8,128)(2,1)S(1)} %bitcast.8), channel_id=1, replica_groups=mesh['xh'=2,'xb'=2,'zh'=2,'y2'=2,'y1'=2,'y0'=2,'zl1'=2,'zl0'=2,'core'=2]..., dimensions={0} | all-to-all | bytes 2097152 | tf_op jit(solution)/shard_map/to_channels/all_to_all | solution.py:217
  51.0 0.0 copy-start.1
  51.0 2.9 %collective-permute-start = (bf16[64,16,128]{2,1,0:T(8,128)(2,1)S(1)}, bf16[64,16,128]{2,1,0:T(8,128)(2,1)S(1)}, u32[]{:S(2)}, u32[]{:S(2)}) collective-permute-start(bf16[64,16,128]{2,1,0:T(8,128)(2,1)S(1)} %bitcast.12), channel_id=1, source_target_pairs={{0,384},{1,385},{128,256},{129,257},{256,128},{257,129},{384,0},{3... | collective-permute-start | bytes 786440 | tf_op jit(solution)/shard_map/right_across_x/ppermute | solution.py:220
  54.0 0.0 copy-start.2
  54.0 0.0 copy-start.3
  54.0 0.0 copy-start.5
  54.0 0.0 copy-start.6
  54.0 7.4 %collective-permute-start.1 = (bf16[64,16,128]{2,1,0:T(8,128)(2,1)S(1)}, bf16[64,16,128]{2,1,0:T(8,128)(2,1)S(1)}, u32[]{:S(2)}, u32[]{:S(2)}) collective-permute-start(bf16[64,16,128]{2,1,0:T(8,128)(2,1)S(1)} %bitcast.11), channel_id=1, source_target_pairs={{0,385},{1,384},{128,257},{129,256},{256,129},{257,128},{384,1},{3... | collective-permute-start | bytes 786440 | tf_op jit(solution)/shard_map/right_across_x_and_core/ppermute | solution.py:222
  61.5 0.6 triangle_own.1
  62.1 1.9 %collective-permute-start.2 = (bf16[2,256,768]{2,1,0:T(8,128)(2,1)S(1)}, bf16[2,256,768]{2,1,0:T(8,128)(2,1)S(1)}, u32[]{:S(2)}, u32[]{:S(2)}) collective-permute-start(bf16[2,256,768]{2,1,0:T(8,128)(2,1)S(1)} %get-tuple-element.37.pack_ref), channel_id=1, source_target_pairs={{0,1},{1,0},{128,129},{129,128},{256,257},{257,256},{384,385},{385... | collective-permute-start | bytes 2359304 | tf_op jit(solution)/shard_map/pack_of_other_core/ppermute | solution.py:239
  64.0 0.0 copy-done.1
  64.0 0.0 copy-done.2
  64.0 0.0 copy-done.3
  64.0 0.0 copy-done.5
  64.0 0.0 copy-done.6
  64.0 0.7 gate.1
  64.8 0.0 collective-permute-done.x_ref
  64.8 4.4 %collective-permute-done.1.xc_ref = bf16[64,16,128]{2,1,0:T(8,128)(2,1)S(1)} collective-permute-done((bf16[64,16,128]{2,1,0:T(8,128)(2,1)S(1)}, bf16[64,16,128]{2,1,0:T(8,128)(2,1)S(1)}, u32[]{:S(2)}, u32[]{:S(2)}) %collective-permute-start.1) | collective-permute-done | bytes 262176 | tf_op jit(solution)/shard_map/right_across_x_and_core/ppermute | solution.py:222
  69.2 0.3 triangle_x.1.across_ref
  69.5 0.0 collective-permute-done.2.other_ref
  69.5 0.5 triangle.1
  70.0 25.8 %all_to_all.11 = bf16[128,16,128]{2,1,0:T(8,128)(2,1)S(1)} all-to-all(bf16[128,16,128]{2,1,0:T(8,128)(2,1)S(1)} %bitcast.9), channel_id=1, replica_groups=mesh['xh'=2,'xb'=2,'zh'=2,'y2'=2,'y1'=2,'y0'=2,'zl1'=2,'zl0'=2,'core'=2]..., dimensions={0} | all-to-all | bytes 1048576 | tf_op jit(solution)/shard_map/to_columns/all_to_all | solution.py:249
  95.8 3.3 %finish.1 = f32[128,16,128]{2,1,0:T(8,128)} custom-call(f32[2,128,1024]{2,1,0:T(8,128)S(1)} %get-tuple-element.34.xt_ref, f32[2,128,1024]{2,1,0:T(8,128)S(1)} %get-tuple-element.35.gating_ref, bf16[2,64,16,128]{3,2,1,0:T(8,128)(2,1)S(1)} %bitcast.10, bf16[128,128]{1,0:T(8,128)(2,1)S(1)} %get-tuple-element.42.proj_ref, ...), custom_call_target="tpu_custom_call" | custom-call | flops 1000000000 | bytes 4194304 | tf_op jit(solution)/shard_map/finish/pallas_call | solution.py:252
  (1 shorter events, 0.0 us)
Async XLA Ops:
  0.0 1.2 %copy-start = (f32[128,16,128]{2,1,0:T(8,128)S(1)}, f32[128,16,128]{2,1,0:T(8,128)}, u32[]{:S(2)}) copy-start(f32[128,16,128]{2,1,0:T(8,128)} %param.6) | copy-start | bytes 3145732
  1.2 0.9 copy-start.4
  51.0 13.0 %copy-start.1 = (f32[128,16,128]{2,1,0:T(8,128)S(1)}, f32[128,16,128]{2,1,0:T(8,128)}, u32[]{:S(2)}) copy-start(f32[128,16,128]{2,1,0:T(8,128)} %param.6) | copy-start | bytes 3145732
  51.0 13.7 %collective-permute-start = (bf16[64,16,128]{2,1,0:T(8,128)(2,1)S(1)}, bf16[64,16,128]{2,1,0:T(8,128)(2,1)S(1)}, u32[]{:S(2)}, u32[]{:S(2)}) collective-permute-start(bf16[64,16,128]{2,1,0:T(8,128)(2,1)S(1)} %bitcast.12), channel_id=1, source_target_pairs={{0,384},{1,385},{128,256},{129,257},{256,128},{257,129},{384,0},{3... | collective-permute-start | bytes 786440 | tf_op jit(solution)/shard_map/right_across_x/ppermute | solution.py:220
  54.0 10.0 %copy-start.2 = (bf16[128,1024]{1,0:T(8,128)(2,1)S(1)}, bf16[128,1024]{1,0:T(8,128)(2,1)}, u32[]{:S(2)}) copy-start(bf16[128,1024]{1,0:T(8,128)(2,1)} %in_ref.1) | copy-start | bytes 786436
  54.0 10.0 %copy-start.3 = (bf16[512,128]{1,0:T(8,128)(2,1)S(1)}, bf16[512,128]{1,0:T(8,128)(2,1)}, u32[]{:S(2)}) copy-start(bf16[512,128]{1,0:T(8,128)(2,1)} %down_ref.1) | copy-start | bytes 393220
  54.0 10.0 %copy-start.5 = (bf16[128,128]{1,0:T(8,128)(2,1)S(1)}, bf16[128,128]{1,0:T(8,128)(2,1)}, u32[]{:S(2)}) copy-start(bf16[128,128]{1,0:T(8,128)(2,1)} %gate_ref.1) | copy-start | bytes 98308
  54.0 10.0 %copy-start.6 = (bf16[128,128]{1,0:T(8,128)(2,1)S(1)}, bf16[128,128]{1,0:T(8,128)(2,1)}, u32[]{:S(2)}) copy-start(bf16[128,128]{1,0:T(8,128)(2,1)} %proj_ref.1) | copy-start | bytes 98308
  54.0 15.2 %collective-permute-start.1 = (bf16[64,16,128]{2,1,0:T(8,128)(2,1)S(1)}, bf16[64,16,128]{2,1,0:T(8,128)(2,1)S(1)}, u32[]{:S(2)}, u32[]{:S(2)}) collective-permute-start(bf16[64,16,128]{2,1,0:T(8,128)(2,1)S(1)} %bitcast.11), channel_id=1, source_target_pairs={{0,385},{1,384},{128,257},{129,256},{256,129},{257,128},{384,1},{3... | collective-permute-start | bytes 786440 | tf_op jit(solution)/shard_map/right_across_x_and_core/ppermute | solution.py:222
  62.1 7.5 %collective-permute-start.2 = (bf16[2,256,768]{2,1,0:T(8,128)(2,1)S(1)}, bf16[2,256,768]{2,1,0:T(8,128)(2,1)S(1)}, u32[]{:S(2)}, u32[]{:S(2)}) collective-permute-start(bf16[2,256,768]{2,1,0:T(8,128)(2,1)S(1)} %get-tuple-element.37.pack_ref), channel_id=1, source_target_pairs={{0,1},{1,0},{128,129},{129,128},{256,257},{257,256},{384,385},{385... | collective-permute-start | bytes 2359304 | tf_op jit(solution)/shard_map/pack_of_other_core/ppermute | solution.py:239

commit v9 on v8

--- a/solution.py
+++ b/solution.py
@@ -22,6 +22,7 @@
 EPS = 1e-05
 FLOPS_X = 16_000_000_000
 LIMIT = 16 * 1024 * 1024
+PROJECT_LIMIT = 60 * 1024 * 1024
 
 
 def sigmoid(v):
@@ -48,40 +49,55 @@
     )
 
 
-def half_pairs(ref, h):
+def pairs(ref):
     tiles = []
     for pair in range(QUARTER):
-        even, odd = (by_core(ref[pl.ds(HALF * h + 2 * pair + s, ROWS, stride=COLS), :]) for s in range(2))
+        even, odd = (by_core(ref[pl.ds(2 * pair + s, ROWS, stride=HALF), :]) for s in range(2))
         tiles += [jnp.concatenate([even[c], odd[c]], axis=0).T for c in range(2)]
     return jnp.concatenate(tiles, axis=1)
 
 
-def norm_kernel(x_ref, normed_ref):
+def project_kernel(x_hbm, w_hbm, out_hbm, held, w_ref, stage, ready, sems):
+    copies = [
+        pltpu.make_async_copy(x_hbm.at[:, pl.ds(HALF * h, HALF), :], held.at[h].reshape(ROWS, HALF, CH), sems.at[h])
+        for h in range(2)
+    ]
+    copies.append(pltpu.make_async_copy(w_hbm, w_ref, sems.at[2]))
+    for copy in copies:
+        copy.start()
+    core, xh = lax.axis_index("core"), lax.axis_index("xh")
+    normed = []
     for h in range(2):
-        normed_ref[h] = norm_rows(half_pairs(x_ref, h))
-
-
-def project_kernel(normed_ref, w_ref, out_ref, stage):
-    core = lax.axis_index("core")
+        copies[h].wait()
+        normed.append(norm_rows(pairs(held.at[h])))
+    copies[2].wait()
     weights = w_ref[...].T
-    for h in range(2):
-        p = dot(weights, normed_ref[h])
-        left = sigmoid(p[:CH]) * p[CH : 2 * CH]
-        right = sigmoid(p[2 * CH : 3 * CH]) * p[3 * CH :]
-        for pair in range(QUARTER):
-            row = QUARTER * h + pair
-            for c in range(2):
-                at = slice((2 * pair + c) * ROWS, (2 * pair + c + 1) * ROWS)
-                stage[pl.ds(HALF * c + row, CH, stride=SIDES), :] = right[:, at]
-                stage[pl.ds(COLS + HALF * c + row, CH, stride=SIDES), :] = left[:, at]
-    xh = lax.axis_index("xh")
-    for b in range(2):
-        rows = stage[64 * SIDES * b : 64 * SIDES * (b + 1)].reshape(64, SIDES, ROWS)
-        first, second = rows[:, :HALF], rows[:, HALF:COLS]
-        own = jnp.where(core == 0, first, second)
-        other = jnp.where(core == 0, second, first)
-        rows = jnp.concatenate([own, other, rows[:, COLS : 2 * COLS]], axis=1)
-        out_ref[jnp.bitwise_xor(xh, b)] = rows.astype(jnp.bfloat16)
+    sent = []
+    for base, at in ((COLS, 0), (0, 2 * CH)):
+        for h in range(2):
+            p = dot(weights[at : at + 2 * CH], normed[h])
+            values = sigmoid(p[:CH]) * p[CH:]
+            for pair in range(QUARTER):
+                for c in range(2):
+                    lanes = slice((2 * pair + c) * ROWS, (2 * pair + c + 1) * ROWS)
+                    stage[pl.ds(base + HALF * c + QUARTER * h + pair, CH, stride=SIDES), :] = values[:, lanes]
+        for b in range(2):
+            rows = stage[64 * SIDES * b : 64 * SIDES * (b + 1)].reshape(64, SIDES, ROWS)[:, base : base + COLS]
+            if base == 0:
+                first, second = rows[:, :HALF], rows[:, HALF:]
+                own = jnp.where(core == 0, first, second)
+                other = jnp.where(core == 0, second, first)
+                rows = jnp.concatenate([own, other], axis=1)
+            ready[b, :, base : base + COLS] = rows.astype(jnp.bfloat16)
+            copy = pltpu.make_async_copy(
+                ready.at[b, :, pl.ds(base, COLS), :],
+                out_hbm.at[jnp.bitwise_xor(xh, b), :, pl.ds(base, COLS), :],
+                sems.at[3 + len(sent)],
+            )
+            copy.start()
+            sent.append(copy)
+    for copy in sent:
+        copy.wait()
 
 
 def gate_kernel(x_ref, gate_ref, proj_ref, in_ref, down_ref, xt_ref, gating_ref, proj_t_ref, in_t_ref, down_t_ref):
@@ -185,7 +201,7 @@
 HELD = pltpu.VMEM((2, ROWS * HALF, CH), jnp.float32)
 
 
-def call(kernel, ins, outs, scratch=(), flops=0, moved=0, out_specs=None):
+def call(kernel, ins, outs, scratch=(), flops=0, moved=0, out_specs=None, limit=LIMIT):
     many = isinstance(outs, tuple)
     return pl.pallas_call(
         kernel,
@@ -193,7 +209,7 @@
         in_specs=ins,
         out_specs=out_specs if out_specs is not None else ((VMEM,) * len(outs) if many else VMEM),
         scratch_shapes=list(scratch),
-        compiler_params=pltpu.CompilerParams(vmem_limit_bytes=LIMIT),
+        compiler_params=pltpu.CompilerParams(vmem_limit_bytes=limit),
         cost_estimate=pl.CostEstimate(flops=flops, bytes_accessed=moved, transcendentals=0),
     )
 
@@ -202,17 +218,23 @@
     bf16 = functools.partial(jax.ShapeDtypeStruct, dtype=jnp.bfloat16)
     f32 = functools.partial(jax.ShapeDtypeStruct, dtype=jnp.float32)
     flat = pair_rep.reshape(ROWS * COLS, CH)
-    with jax.named_scope("norm"):
-        normed = call(norm_kernel, [VMEM], bf16((2, CH, HALF * ROWS)), (), 2_000_000, 2 << 20)(flat)
     with jax.named_scope("project"):
         sides = call(
             project_kernel,
-            [VMEM, VMEM],
+            [HBM, HBM],
             bf16((2, CH // 2, 2 * COLS, ROWS)),
-            [pltpu.VMEM((CH * SIDES, ROWS), jnp.float32)],
+            [
+                HELD,
+                pltpu.VMEM(pair_proj.shape, jnp.bfloat16),
+                pltpu.VMEM((CH * SIDES, ROWS), jnp.float32),
+                pltpu.VMEM((2, CH // 2, 2 * COLS, ROWS), jnp.bfloat16),
+                pltpu.SemaphoreType.DMA((7,)),
+            ],
             270_000_000,
             2 << 20,
-        )(normed, pair_proj)
+            HBM,
+            PROJECT_LIMIT,
+        )(pair_rep, pair_proj)
     with jax.named_scope("to_channels"):
         sides = lax.all_to_all(sides.reshape(CH, 2 * COLS, ROWS), PLANE, 0, 0, tiled=True)
     flat, sides = lax.optimization_barrier((flat, sides))

time: 99.5 us -> 100 us (level)
  Pallas kernels: 6.9 us -> 8.75 us
  local copies, waits for them, and re-layouts: 1.59 us -> 0.06 us
    pallas_call x2 -> x1, Pallas kernels: 1.53 us -> 3.38 us  [per_device(): call(project_kernel, [HBM, HBM], bf16((2, CH // 2, 2 * COLS, ROWS)), [HEL...]
    unnamed x14 -> x10, local copies, waits for them, and re-layouts: 1.56 us -> 0.03 us
where the time goes in v9:
time: 100 us
  blocking collectives  74.3 us (74%)
  starting transfers between devices  12.3 us (12%)
  Pallas kernels  8.75 us (9%)
  waiting for transfers between devices  4.44 us (4%)
    all_to_all x1, blocking collectives, per_device(): lax.all_to_all(sides.reshape(CH, 2 * COLS, ROWS), PLANE, 0, 0, tiled=True)  48.1 us
    all_to_all x1, blocking collectives, per_device(): tri = lax.all_to_all(tri.reshape(CH, COLS, ROWS), PLANE, 0, 0, tiled=True)  26.2 us
    ppermute x1, starting transfers between devices, per_device(): lax.ppermute(sides[:, HALF:COLS].reshape(64, COLS, ROWS), SHARE, [(d, d ^...  7.45 us
    ppermute x1, waiting for transfers between devices, per_device(): lax.ppermute(sides[:, HALF:COLS].reshape(64, COLS, ROWS), SHARE, [(d, d ^...  4.44 us
    pallas_call x1, Pallas kernels, per_device(): call(project_kernel, [HBM, HBM], bf16((2, CH // 2, 2 * COLS, ROWS)), [HEL...  3.38 us
    pallas_call x1, Pallas kernels, per_device(): call(finish_kernel, [VMEM] * 6, f32((ROWS, COLS, CH)), [pltpu.VMEM((CH, S...  3.31 us
    ppermute x1, starting transfers between devices, per_device(): lax.ppermute(sides[:, :HALF].reshape(64, COLS, ROWS), SHARE, [(d, d ^ 6)...  2.92 us
  transfers between devices with their start and end apart: 3, of which 1 were waited for; matrix products, arithmetic and copies ran while one was open for 0% of the time, Pallas kernels for 2%

profile of v9, /device:TPU:1, one launch (start us, length us, event | category | flops | bytes accessed | tf_op | source)
XLA Modules:
  0.0 100.0 jit_solution(1856574625387527699)
XLA Ops:
  0.0 3.4 %project.1 = bf16[2,64,32,128]{3,2,1,0:T(8,128)(2,1)} custom-call(f32[128,16,128]{2,1,0:T(8,128)} %x_hbm.1, bf16[128,512]{1,0:T(8,128)(2,1)} %w_hbm.1), custom_call_target="tpu_custom_call" | custom-call | flops 270000000 | bytes 2097152 | tf_op jit(solution)/shard_map/project/pallas_call | solution.py:222
  3.4 48.1 %all_to_all.10.sides_ref = bf16[128,32,128]{2,1,0:T(8,128)(2,1)S(1)} all-to-all(bf16[128,32,128]{2,1,0:T(8,128)(2,1)} %bitcast.9), channel_id=1, replica_groups=mesh['xh'=2,'xb'=2,'zh'=2,'y2'=2,'y1'=2,'y0'=2,'zl1'=2,'zl0'=2,'core'=2]..., dimensions={0} | all-to-all | bytes 2097152 | tf_op jit(solution)/shard_map/to_channels/all_to_all | solution.py:239
  51.5 0.0 copy-start
  51.6 2.9 %collective-permute-start = (bf16[64,16,128]{2,1,0:T(8,128)(2,1)S(1)}, bf16[64,16,128]{2,1,0:T(8,128)(2,1)S(1)}, u32[]{:S(2)}, u32[]{:S(2)}) collective-permute-start(bf16[64,16,128]{2,1,0:T(8,128)(2,1)S(1)} %bitcast.11), channel_id=1, source_target_pairs={{0,384},{1,385},{128,256},{129,257},{256,128},{257,129},{384,0},{3... | collective-permute-start | bytes 786440 | tf_op jit(solution)/shard_map/right_across_x/ppermute | solution.py:242
  54.5 0.0 copy-start.1
  54.5 0.0 copy-start.2
  54.5 0.0 copy-start.3
  54.5 0.0 copy-start.4
  54.6 7.5 %collective-permute-start.1 = (bf16[64,16,128]{2,1,0:T(8,128)(2,1)S(1)}, bf16[64,16,128]{2,1,0:T(8,128)(2,1)S(1)}, u32[]{:S(2)}, u32[]{:S(2)}) collective-permute-start(bf16[64,16,128]{2,1,0:T(8,128)(2,1)S(1)} %bitcast.10), channel_id=1, source_target_pairs={{0,385},{1,384},{128,257},{129,256},{256,129},{257,128},{384,1},{3... | collective-permute-start | bytes 786440 | tf_op jit(solution)/shard_map/right_across_x_and_core/ppermute | solution.py:244
  62.0 0.6 triangle_own.1
  62.6 1.9 %collective-permute-start.2 = (bf16[2,256,768]{2,1,0:T(8,128)(2,1)S(1)}, bf16[2,256,768]{2,1,0:T(8,128)(2,1)S(1)}, u32[]{:S(2)}, u32[]{:S(2)}) collective-permute-start(bf16[2,256,768]{2,1,0:T(8,128)(2,1)S(1)} %get-tuple-element.37.pack_ref), channel_id=1, source_target_pairs={{0,1},{1,0},{128,129},{129,128},{256,257},{257,256},{384,385},{385... | collective-permute-start | bytes 2359304 | tf_op jit(solution)/shard_map/pack_of_other_core/ppermute | solution.py:261
  64.5 0.0 copy-done
  64.5 0.0 copy-done.1
  64.5 0.0 copy-done.2
  64.6 0.0 copy-done.3
  64.6 0.0 copy-done.4
  64.6 0.7 gate.1
  65.3 0.0 collective-permute-done.x_ref
  65.3 4.4 %collective-permute-done.1.xc_ref = bf16[64,16,128]{2,1,0:T(8,128)(2,1)S(1)} collective-permute-done((bf16[64,16,128]{2,1,0:T(8,128)(2,1)S(1)}, bf16[64,16,128]{2,1,0:T(8,128)(2,1)S(1)}, u32[]{:S(2)}, u32[]{:S(2)}) %collective-permute-start.1) | collective-permute-done | bytes 262176 | tf_op jit(solution)/shard_map/right_across_x_and_core/ppermute | solution.py:244
  69.7 0.3 triangle_x.1.across_ref
  70.1 0.0 collective-permute-done.2.other_ref
  70.1 0.5 triangle.1
  70.5 26.2 %all_to_all.11 = bf16[128,16,128]{2,1,0:T(8,128)(2,1)S(1)} all-to-all(bf16[128,16,128]{2,1,0:T(8,128)(2,1)S(1)} %bitcast.7), channel_id=1, replica_groups=mesh['xh'=2,'xb'=2,'zh'=2,'y2'=2,'y1'=2,'y0'=2,'zl1'=2,'zl0'=2,'core'=2]..., dimensions={0} | all-to-all | bytes 1048576 | tf_op jit(solution)/shard_map/to_columns/all_to_all | solution.py:271
  96.7 3.3 %finish.1 = f32[128,16,128]{2,1,0:T(8,128)} custom-call(f32[2,128,1024]{2,1,0:T(8,128)S(1)} %get-tuple-element.34.xt_ref, f32[2,128,1024]{2,1,0:T(8,128)S(1)} %get-tuple-element.35.gating_ref, bf16[2,64,16,128]{3,2,1,0:T(8,128)(2,1)S(1)} %bitcast.8, bf16[128,128]{1,0:T(8,128)(2,1)S(1)} %get-tuple-element.42.proj_ref, ...), custom_call_target="tpu_custom_call" | custom-call | flops 1000000000 | bytes 4194304 | tf_op jit(solution)/shard_map/finish/pallas_call | solution.py:274
  (1 shorter events, 0.0 us)
Async XLA Ops:
  51.5 13.0 %copy-start = (f32[128,16,128]{2,1,0:T(8,128)S(1)}, f32[128,16,128]{2,1,0:T(8,128)}, u32[]{:S(2)}) copy-start(f32[128,16,128]{2,1,0:T(8,128)} %x_hbm.1) | copy-start | bytes 3145732
  51.6 13.7 %collective-permute-start = (bf16[64,16,128]{2,1,0:T(8,128)(2,1)S(1)}, bf16[64,16,128]{2,1,0:T(8,128)(2,1)S(1)}, u32[]{:S(2)}, u32[]{:S(2)}) collective-permute-start(bf16[64,16,128]{2,1,0:T(8,128)(2,1)S(1)} %bitcast.11), channel_id=1, source_target_pairs={{0,384},{1,385},{128,256},{129,257},{256,128},{257,129},{384,0},{3... | collective-permute-start | bytes 786440 | tf_op jit(solution)/shard_map/right_across_x/ppermute | solution.py:242
  54.5 10.0 %copy-start.1 = (bf16[128,1024]{1,0:T(8,128)(2,1)S(1)}, bf16[128,1024]{1,0:T(8,128)(2,1)}, u32[]{:S(2)}) copy-start(bf16[128,1024]{1,0:T(8,128)(2,1)} %in_ref.1) | copy-start | bytes 786436
  54.5 10.0 %copy-start.2 = (bf16[512,128]{1,0:T(8,128)(2,1)S(1)}, bf16[512,128]{1,0:T(8,128)(2,1)}, u32[]{:S(2)}) copy-start(bf16[512,128]{1,0:T(8,128)(2,1)} %down_ref.1) | copy-start | bytes 393220
  54.5 10.0 %copy-start.3 = (bf16[128,128]{1,0:T(8,128)(2,1)S(1)}, bf16[128,128]{1,0:T(8,128)(2,1)}, u32[]{:S(2)}) copy-start(bf16[128,128]{1,0:T(8,128)(2,1)} %gate_ref.1) | copy-start | bytes 98308
  54.5 10.0 %copy-start.4 = (bf16[128,128]{1,0:T(8,128)(2,1)S(1)}, bf16[128,128]{1,0:T(8,128)(2,1)}, u32[]{:S(2)}) copy-start(bf16[128,128]{1,0:T(8,128)(2,1)} %proj_ref.1) | copy-start | bytes 98308
  54.6 15.2 %collective-permute-start.1 = (bf16[64,16,128]{2,1,0:T(8,128)(2,1)S(1)}, bf16[64,16,128]{2,1,0:T(8,128)(2,1)S(1)}, u32[]{:S(2)}, u32[]{:S(2)}) collective-permute-start(bf16[64,16,128]{2,1,0:T(8,128)(2,1)S(1)} %bitcast.10), channel_id=1, source_target_pairs={{0,385},{1,384},{128,257},{129,256},{256,129},{257,128},{384,1},{3... | collective-permute-start | bytes 786440 | tf_op jit(solution)/shard_map/right_across_x_and_core/ppermute | solution.py:244
  62.6 7.5 %collective-permute-start.2 = (bf16[2,256,768]{2,1,0:T(8,128)(2,1)S(1)}, bf16[2,256,768]{2,1,0:T(8,128)(2,1)S(1)}, u32[]{:S(2)}, u32[]{:S(2)}) collective-permute-start(bf16[2,256,768]{2,1,0:T(8,128)(2,1)S(1)} %get-tuple-element.37.pack_ref), channel_id=1, source_target_pairs={{0,1},{1,0},{128,129},{129,128},{256,257},{257,256},{384,385},{385... | collective-permute-start | bytes 2359304 | tf_op jit(solution)/shard_map/pack_of_other_core/ppermute | solution.py:261

commit v10 on v8

--- a/solution.py
+++ b/solution.py
@@ -164,18 +164,14 @@
         up = t[:hidden]
         units = (up * sigmoid(up) * t[hidden:]).astype(jnp.bfloat16)
         result = middle + dot(down_ref[...], units)
-        for q in range(2):
-            for s in range(QUARTER):
-                c = QUARTER * q + s
-                rows = result[:, c * ROWS : (c + 1) * ROWS].T.reshape(2, 4, 16, CH).transpose(1, 0, 2, 3)
-                held.at[h][pl.ds(c, ROWS, stride=HALF), :] = rows.reshape(ROWS, CH)
-            copy = pltpu.make_async_copy(
-                held.at[h].reshape(ROWS, HALF, CH).at[:, pl.ds(QUARTER * q, QUARTER), :],
-                out_hbm.at[:, pl.ds(HALF * h + QUARTER * q, QUARTER), :],
-                sems.at[2 * h + q],
-            )
-            copy.start()
-            copies.append(copy)
+        for c in range(HALF):
+            rows = result[:, c * ROWS : (c + 1) * ROWS].T.reshape(2, 4, 16, CH).transpose(1, 0, 2, 3)
+            held.at[h][pl.ds(c, ROWS, stride=HALF), :] = rows.reshape(ROWS, CH)
+        copy = pltpu.make_async_copy(
+            held.at[h].reshape(ROWS, HALF, CH), out_hbm.at[:, pl.ds(HALF * h, HALF), :], sems.at[h]
+        )
+        copy.start()
+        copies.append(copy)
     for copy in copies:
         copy.wait()
 
@@ -253,7 +249,7 @@
             finish_kernel,
             [VMEM] * 6,
             f32((ROWS, COLS, CH)),
-            [pltpu.VMEM((CH, SUMS, ROWS), jnp.float32), HELD, pltpu.SemaphoreType.DMA((4,))],
+            [pltpu.VMEM((CH, SUMS, ROWS), jnp.float32), HELD, pltpu.SemaphoreType.DMA((2,))],
             1_000_000_000,
             4 << 20,
             HBM,

time: 99.5 us -> 99.6 us (level)
  no operation moved by 1% of the time
where the time goes in v10:
time: 99.6 us; the launch traced here: 99.2 us
  blocking collectives  73.7 us (74%)
  starting transfers between devices  12.3 us (12%)
  Pallas kernels  6.96 us (7%)
  waiting for transfers between devices  4.44 us (4%)
  local copies, waits for them, and re-layouts  1.59 us (2%)
    all_to_all x1, blocking collectives, per_device(): lax.all_to_all(sides.reshape(CH, 2 * COLS, ROWS), PLANE, 0, 0, tiled=True)  47.9 us
    all_to_all x1, blocking collectives, per_device(): tri = lax.all_to_all(tri.reshape(CH, COLS, ROWS), PLANE, 0, 0, tiled=True)  25.8 us
    ppermute x1, starting transfers between devices, per_device(): lax.ppermute(sides[:, HALF:COLS].reshape(64, COLS, ROWS), SHARE, [(d, d ^...  7.44 us
    ppermute x1, waiting for transfers between devices, per_device(): lax.ppermute(sides[:, HALF:COLS].reshape(64, COLS, ROWS), SHARE, [(d, d ^...  4.43 us
    pallas_call x1, Pallas kernels, per_device(): call(finish_kernel, [VMEM] * 6, f32((ROWS, COLS, CH)), [pltpu.VMEM((CH, S...  3.37 us
    ppermute x1, starting transfers between devices, per_device(): lax.ppermute(sides[:, :HALF].reshape(64, COLS, ROWS), SHARE, [(d, d ^ 6)...  2.94 us
  transfers between devices with their start and end apart: 3, of which 1 were waited for; matrix products, arithmetic and copies ran while one was open for 0% of the time, Pallas kernels for 2%

profile of v10, /device:TPU:1, one launch (start us, length us, event | category | flops | bytes accessed | tf_op | source)
XLA Modules:
  0.0 99.2 jit_solution(6770885293347897821)
XLA Ops:
  0.0 0.0 copy-start
  0.0 1.2 %copy-done = f32[128,16,128]{2,1,0:T(8,128)S(1)} copy-done((f32[128,16,128]{2,1,0:T(8,128)S(1)}, f32[128,16,128]{2,1,0:T(8,128)}, u32[]{:S(2)}) %copy-start) | copy-done | bytes 1048600
  1.2 0.0 copy-start.4
  1.2 0.6 norm.1.normed_ref
  1.8 0.3 copy-done.4
  2.1 0.9 project.1
  3.1 47.9 %all_to_all.10.sides_ref = bf16[128,32,128]{2,1,0:T(8,128)(2,1)S(1)} all-to-all(bf16[128,32,128]{2,1,0:T(8,128)(2,1)S(1)} %bitcast.8), channel_id=1, replica_groups=mesh['xh'=2,'xb'=2,'zh'=2,'y2'=2,'y1'=2,'y0'=2,'zl1'=2,'zl0'=2,'core'=2]..., dimensions={0} | all-to-all | bytes 2097152 | tf_op jit(solution)/shard_map/to_channels/all_to_all | solution.py:213
  51.0 0.0 copy-start.1
  51.0 2.9 %collective-permute-start = (bf16[64,16,128]{2,1,0:T(8,128)(2,1)S(1)}, bf16[64,16,128]{2,1,0:T(8,128)(2,1)S(1)}, u32[]{:S(2)}, u32[]{:S(2)}) collective-permute-start(bf16[64,16,128]{2,1,0:T(8,128)(2,1)S(1)} %bitcast.12), channel_id=1, source_target_pairs={{0,384},{1,385},{128,256},{129,257},{256,128},{257,129},{384,0},{3... | collective-permute-start | bytes 786440 | tf_op jit(solution)/shard_map/right_across_x/ppermute | solution.py:216
  54.0 0.0 copy-start.2
  54.0 0.0 copy-start.3
  54.0 0.0 copy-start.5
  54.0 0.0 copy-start.6
  54.0 7.4 %collective-permute-start.1 = (bf16[64,16,128]{2,1,0:T(8,128)(2,1)S(1)}, bf16[64,16,128]{2,1,0:T(8,128)(2,1)S(1)}, u32[]{:S(2)}, u32[]{:S(2)}) collective-permute-start(bf16[64,16,128]{2,1,0:T(8,128)(2,1)S(1)} %bitcast.11), channel_id=1, source_target_pairs={{0,385},{1,384},{128,257},{129,256},{256,129},{257,128},{384,1},{3... | collective-permute-start | bytes 786440 | tf_op jit(solution)/shard_map/right_across_x_and_core/ppermute | solution.py:218
  61.5 0.6 triangle_own.1
  62.1 1.9 %collective-permute-start.2 = (bf16[2,256,768]{2,1,0:T(8,128)(2,1)S(1)}, bf16[2,256,768]{2,1,0:T(8,128)(2,1)S(1)}, u32[]{:S(2)}, u32[]{:S(2)}) collective-permute-start(bf16[2,256,768]{2,1,0:T(8,128)(2,1)S(1)} %get-tuple-element.37.pack_ref), channel_id=1, source_target_pairs={{0,1},{1,0},{128,129},{129,128},{256,257},{257,256},{384,385},{385... | collective-permute-start | bytes 2359304 | tf_op jit(solution)/shard_map/pack_of_other_core/ppermute | solution.py:235
  64.0 0.0 copy-done.1
  64.0 0.0 copy-done.2
  64.0 0.0 copy-done.3
  64.0 0.0 copy-done.5
  64.0 0.0 copy-done.6
  64.0 0.7 gate.1
  64.8 0.0 collective-permute-done.x_ref
  64.8 4.4 %collective-permute-done.1.xc_ref = bf16[64,16,128]{2,1,0:T(8,128)(2,1)S(1)} collective-permute-done((bf16[64,16,128]{2,1,0:T(8,128)(2,1)S(1)}, bf16[64,16,128]{2,1,0:T(8,128)(2,1)S(1)}, u32[]{:S(2)}, u32[]{:S(2)}) %collective-permute-start.1) | collective-permute-done | bytes 262176 | tf_op jit(solution)/shard_map/right_across_x_and_core/ppermute | solution.py:218
  69.2 0.3 triangle_x.1.across_ref
  69.5 0.0 collective-permute-done.2.other_ref
  69.5 0.5 triangle.1
  70.0 25.8 %all_to_all.11 = bf16[128,16,128]{2,1,0:T(8,128)(2,1)S(1)} all-to-all(bf16[128,16,128]{2,1,0:T(8,128)(2,1)S(1)} %bitcast.9), channel_id=1, replica_groups=mesh['xh'=2,'xb'=2,'zh'=2,'y2'=2,'y1'=2,'y0'=2,'zl1'=2,'zl0'=2,'core'=2]..., dimensions={0} | all-to-all | bytes 1048576 | tf_op jit(solution)/shard_map/to_columns/all_to_all | solution.py:245
  95.8 3.4 %finish.1 = f32[128,16,128]{2,1,0:T(8,128)} custom-call(f32[2,128,1024]{2,1,0:T(8,128)S(1)} %get-tuple-element.34.xt_ref, f32[2,128,1024]{2,1,0:T(8,128)S(1)} %get-tuple-element.35.gating_ref, bf16[2,64,16,128]{3,2,1,0:T(8,128)(2,1)S(1)} %bitcast.10, bf16[128,128]{1,0:T(8,128)(2,1)S(1)} %get-tuple-element.42.proj_ref, ...), custom_call_target="tpu_custom_call" | custom-call | flops 1000000000 | bytes 4194304 | tf_op jit(solution)/shard_map/finish/pallas_call | solution.py:248
  (1 shorter events, 0.0 us)
Async XLA Ops:
  0.0 1.2 %copy-start = (f32[128,16,128]{2,1,0:T(8,128)S(1)}, f32[128,16,128]{2,1,0:T(8,128)}, u32[]{:S(2)}) copy-start(f32[128,16,128]{2,1,0:T(8,128)} %param.6) | copy-start | bytes 3145732
  1.2 0.9 copy-start.4
  51.0 13.0 %copy-start.1 = (f32[128,16,128]{2,1,0:T(8,128)S(1)}, f32[128,16,128]{2,1,0:T(8,128)}, u32[]{:S(2)}) copy-start(f32[128,16,128]{2,1,0:T(8,128)} %param.6) | copy-start | bytes 3145732
  51.0 13.7 %collective-permute-start = (bf16[64,16,128]{2,1,0:T(8,128)(2,1)S(1)}, bf16[64,16,128]{2,1,0:T(8,128)(2,1)S(1)}, u32[]{:S(2)}, u32[]{:S(2)}) collective-permute-start(bf16[64,16,128]{2,1,0:T(8,128)(2,1)S(1)} %bitcast.12), channel_id=1, source_target_pairs={{0,384},{1,385},{128,256},{129,257},{256,128},{257,129},{384,0},{3... | collective-permute-start | bytes 786440 | tf_op jit(solution)/shard_map/right_across_x/ppermute | solution.py:216
  54.0 10.0 %copy-start.2 = (bf16[128,1024]{1,0:T(8,128)(2,1)S(1)}, bf16[128,1024]{1,0:T(8,128)(2,1)}, u32[]{:S(2)}) copy-start(bf16[128,1024]{1,0:T(8,128)(2,1)} %in_ref.1) | copy-start | bytes 786436
  54.0 10.0 %copy-start.3 = (bf16[512,128]{1,0:T(8,128)(2,1)S(1)}, bf16[512,128]{1,0:T(8,128)(2,1)}, u32[]{:S(2)}) copy-start(bf16[512,128]{1,0:T(8,128)(2,1)} %down_ref.1) | copy-start | bytes 393220
  54.0 10.0 %copy-start.5 = (bf16[128,128]{1,0:T(8,128)(2,1)S(1)}, bf16[128,128]{1,0:T(8,128)(2,1)}, u32[]{:S(2)}) copy-start(bf16[128,128]{1,0:T(8,128)(2,1)} %gate_ref.1) | copy-start | bytes 98308
  54.0 10.0 %copy-start.6 = (bf16[128,128]{1,0:T(8,128)(2,1)S(1)}, bf16[128,128]{1,0:T(8,128)(2,1)}, u32[]{:S(2)}) copy-start(bf16[128,128]{1,0:T(8,128)(2,1)} %proj_ref.1) | copy-start | bytes 98308
  54.0 15.2 %collective-permute-start.1 = (bf16[64,16,128]{2,1,0:T(8,128)(2,1)S(1)}, bf16[64,16,128]{2,1,0:T(8,128)(2,1)S(1)}, u32[]{:S(2)}, u32[]{:S(2)}) collective-permute-start(bf16[64,16,128]{2,1,0:T(8,128)(2,1)S(1)} %bitcast.11), channel_id=1, source_target_pairs={{0,385},{1,384},{128,257},{129,256},{256,129},{257,128},{384,1},{3... | collective-permute-start | bytes 786440 | tf_op jit(solution)/shard_map/right_across_x_and_core/ppermute | solution.py:218
  62.1 7.5 %collective-permute-start.2 = (bf16[2,256,768]{2,1,0:T(8,128)(2,1)S(1)}, bf16[2,256,768]{2,1,0:T(8,128)(2,1)S(1)}, u32[]{:S(2)}, u32[]{:S(2)}) collective-permute-start(bf16[2,256,768]{2,1,0:T(8,128)(2,1)S(1)} %get-tuple-element.37.pack_ref), channel_id=1, source_target_pairs={{0,1},{1,0},{128,129},{129,128},{256,257},{257,256},{384,385},{385... | collective-permute-start | bytes 2359304 | tf_op jit(solution)/shard_map/pack_of_other_core/ppermute | solution.py:235
